TPU v7x, 32 devices: a whole 2x2x4 slice. The times are simulated.
32 devices in a mesh: dp: 4 (over x, core), ctx: 8 (over z, y).
Axes of the slice: x: 2, y: 2, z: 4, core: 2. Of those that a mesh axis runs over, the one named last changes fastest.
Arguments:
- grad_out: bfloat16 [4096, 4096], P(('dp', 'ctx')), may hold values from -6 to 6
- gate: bfloat16 [4096, 4096], P(('dp', 'ctx')), may hold values from -6 to 6
- conv_in: bfloat16 [4096, 4096], P(('dp', 'ctx')), may hold values from -6 to 6
- filt: bfloat16 [4096, 64], P('dp'), may hold values from -0.75 to 0.75
- doc_end: int32 [4096], P(('dp', 'ctx')), may hold values from 1 to 4096, as said below
Outputs:
- grad_in: bfloat16 [4096, 4096], P(('dp', 'ctx'))
- grad_filt: float32 [4096, 64], P('dp')
Inputs may be any that keep to these rules, and one draw needn't show every extreme that they name: doc_end is the same for all rows of one document and larger than the row's own index; no document crosses a multiple of 1024.
All inputs are finite; a program needn't handle non-finite values.
Results may differ from a plain program's by a relative error of at most 0.0049.
Values may be sent and summed in bfloat16 or wider, within the bound.
No kernel may reach another device: no remote copies, remote signals or barrier semaphores. Data moves between devices by JAX's collectives and lax.ppermute only.
A program may use at most 64 MiB of HBM per device.

v0:
```python
import jax
import jax.numpy as jnp
from jax import lax
from jax.sharding import PartitionSpec as P


def from_behind(value, axis, steps):
    count = lax.axis_size(axis)
    first, last = (max(0, -steps), min(count, count - steps))
    return lax.ppermute(value, axis, [(source, source + steps) for source in range(first, last)])


def body(grad_out, gate, conv_in, filt, doc_end):
    row_count, channels = grad_out.shape
    tap_count = filt.shape[1]
    group_size = 8
    whole_filter = lax.all_gather(filt, "dp", axis=0, tiled=True)
    filter_rows = whole_filter.T
    grad_y = (grad_out.astype(jnp.float32) * gate.astype(jnp.float32)).astype(jnp.bfloat16)
    following = from_behind(grad_y, "ctx", -1)
    extended = jnp.concatenate([grad_y, following], axis=0)
    first_row = (lax.axis_index("dp") * lax.axis_size("ctx") + lax.axis_index("ctx")) * row_count
    remaining = doc_end - (first_row + jnp.arange(row_count, dtype=jnp.int32))
    within = jnp.arange(group_size, dtype=jnp.int32)

    def one_group(which, state):
        accum, tap_rows = state
        base = (which * group_size).astype(jnp.int32)
        offsets = base + within
        windows = jax.vmap(lambda offset: lax.dynamic_slice_in_dim(extended, offset, row_count, 0))(
            offsets
        )
        inside = (offsets[:, None] < remaining[None, :])[:, :, None]
        windows = jnp.where(inside, windows, jnp.zeros((), jnp.bfloat16))
        weights = lax.dynamic_slice_in_dim(filter_rows, base, group_size, 0)
        accum = accum + jnp.einsum(
            "trc,tc->rc", windows, weights, preferred_element_type=jnp.float32
        )
        tap_block = jnp.einsum("trc,rc->tc", windows, conv_in, preferred_element_type=jnp.float32)
        tap_rows = lax.dynamic_update_slice_in_dim(tap_rows, tap_block, base, 0)
        return (accum, tap_rows)

    start = (
        jnp.zeros((row_count, channels), jnp.float32),
        jnp.zeros((tap_count, channels), jnp.float32),
    )
    accum, tap_rows = lax.fori_loop(0, tap_count // group_size, one_group, start)
    grad_in = accum.astype(jnp.bfloat16)
    filt_terms = tap_rows.T
    owned = lax.psum_scatter(filt_terms, "dp", scatter_dimension=0, tiled=True)
    grad_filt = lax.psum(owned, "ctx")
    return (grad_in, grad_filt)


def solution(mesh):
    placed = (
        P(("dp", "ctx"), None),
        P(("dp", "ctx"), None),
        P(("dp", "ctx"), None),
        P("dp", None),
        P(("dp", "ctx")),
    )
    return jax.shard_map(
        body,
        mesh=mesh,
        in_specs=placed,
        out_specs=(P(("dp", "ctx"), None), P("dp", None)),
        check_vma=False,
    )
```

profile of v0, /device:TPU:0, one launch (start us, length us, event | category | flops | bytes accessed | tf_op | source)
XLA Modules:
  0.0 451.6 jit_solution(11002482210145527600)
XLA Ops:
  10.4 10.2 %all_gather.3 = bf16[4096,64]{0,1:T(8,128)(2,1)} all-gather(bf16[1024,64]{0,1:T(8,128)(2,1)} %param.10), channel_id=1, replica_groups=mesh['dp'=4,'ctx'=8] {'dp'}, dimensions={0}, use_global_device_ids=true | all-gather | bytes 655360 | tf_op jit(solution)/shard_map/all_gather | solution.py:17
  21.3 15.9 %collective-permute-done = bf16[128,4096]{1,0:T(8,128)(2,1)} collective-permute-done((bf16[128,4096]{1,0:T(8,128)(2,1)S(1)}, bf16[128,4096]{1,0:T(8,128)(2,1)}, u32[]{:S(2)}, u32[]{:S(2)}) %collective-permute-start) | collective-permute-done | bytes 1048608 | tf_op jit(solution)/shard_map/ppermute | solution.py:10
  40.0 302.4 %while.23 = (s32[]{:T(128)}, f32[128,4096]{1,0:T(8,128)}, f32[64,4096]{1,0:T(8,128)}, bf16[64,4096]{1,0:T(8,128)(2,1)}, s32[128]{0:T(128)S(1)}, /*index=5*/bf16[...) while((s32[]{:T(128)}, f32[128,4096]{1,0:T(8,128)}, ...), condition=%wide.region_1.2_spmd.clone.clone, body=%wide.region_0.1_spmd.clone.sunk.clone | while | flops 34604080 | bytes 66786340 | solution.py:47
  40.9 19.0 %while.22 = (s32[]{:T(128)}, bf16[256,4096]{1,0:T(8,128)(2,1)S(1)}, s32[8,2]{0,1:T(2,128)S(1)}, bf16[8,128,4096]{2,1,0:T(8,128)(2,1)}, s32[]{:T(128)}) while((s32[]{:T(128)}, bf16[256,4096]{1,0:T(8,128)(2,1)S(1)}, s32[8,2]{0,1:T(2,128)S(1)}, bf16[8,128,4096]{2,1,0:T(8,128)(2,1)}, s32[]{:T(128)}) %tuple.56), condition=%wide.while_cond, body=%wide.while_body.sunk | while | flops 2 | bytes 2098265 | solution.py:30
  59.9 8.2 %multiply_reduce_fusion.6 = f32[4096,128]{0,1:T(8,128)} fusion(f32[4096,8]{0,1:T(8,128)S(1)} %bitcast_convert_fusion.6, bf16[8,128,4096]{2,1,0:T(8,128)(2,1)} %get-tuple-element.289, pred[8,128]{1,0:T(8,128)(4,1)S(1)} %broadcast_compare_fusion.3), kind=kLoop, calls=%fused_computation.4.clone.1.clone | loop fusion | flops 16252928 | bytes 10617856 | tf_op jit(solution)/shard_map/while/body/eval_jaxpr/trc,tc->rc/dot_general | solution.py:36
  78.1 19.0 %while.22 = (s32[]{:T(128)}, bf16[256,4096]{1,0:T(8,128)(2,1)S(1)}, s32[8,2]{0,1:T(2,128)S(1)}, bf16[8,128,4096]{2,1,0:T(8,128)(2,1)}, s32[]{:T(128)}) while((s32[]{:T(128)}, bf16[256,4096]{1,0:T(8,128)(2,1)S(1)}, s32[8,2]{0,1:T(2,128)S(1)}, bf16[8,128,4096]{2,1,0:T(8,128)(2,1)}, s32[]{:T(128)}) %tuple.56), condition=%wide.while_cond, body=%wide.while_body.sunk | while | flops 2 | bytes 2098265 | solution.py:30
  97.2 8.2 %multiply_reduce_fusion.6 = f32[4096,128]{0,1:T(8,128)} fusion(f32[4096,8]{0,1:T(8,128)S(1)} %bitcast_convert_fusion.6, bf16[8,128,4096]{2,1,0:T(8,128)(2,1)} %get-tuple-element.289, pred[8,128]{1,0:T(8,128)(4,1)S(1)} %broadcast_compare_fusion.3), kind=kLoop, calls=%fused_computation.4.clone.1.clone | loop fusion | flops 16252928 | bytes 10617856 | tf_op jit(solution)/shard_map/while/body/eval_jaxpr/trc,tc->rc/dot_general | solution.py:36
  116.0 19.0 %while.22 = (s32[]{:T(128)}, bf16[256,4096]{1,0:T(8,128)(2,1)S(1)}, s32[8,2]{0,1:T(2,128)S(1)}, bf16[8,128,4096]{2,1,0:T(8,128)(2,1)}, s32[]{:T(128)}) while((s32[]{:T(128)}, bf16[256,4096]{1,0:T(8,128)(2,1)S(1)}, s32[8,2]{0,1:T(2,128)S(1)}, bf16[8,128,4096]{2,1,0:T(8,128)(2,1)}, s32[]{:T(128)}) %tuple.56), condition=%wide.while_cond, body=%wide.while_body.sunk | while | flops 2 | bytes 2098265 | solution.py:30
  135.1 8.2 %multiply_reduce_fusion.6 = f32[4096,128]{0,1:T(8,128)} fusion(f32[4096,8]{0,1:T(8,128)S(1)} %bitcast_convert_fusion.6, bf16[8,128,4096]{2,1,0:T(8,128)(2,1)} %get-tuple-element.289, pred[8,128]{1,0:T(8,128)(4,1)S(1)} %broadcast_compare_fusion.3), kind=kLoop, calls=%fused_computation.4.clone.1.clone | loop fusion | flops 16252928 | bytes 10617856 | tf_op jit(solution)/shard_map/while/body/eval_jaxpr/trc,tc->rc/dot_general | solution.py:36
  153.9 19.0 %while.22 = (s32[]{:T(128)}, bf16[256,4096]{1,0:T(8,128)(2,1)S(1)}, s32[8,2]{0,1:T(2,128)S(1)}, bf16[8,128,4096]{2,1,0:T(8,128)(2,1)}, s32[]{:T(128)}) while((s32[]{:T(128)}, bf16[256,4096]{1,0:T(8,128)(2,1)S(1)}, s32[8,2]{0,1:T(2,128)S(1)}, bf16[8,128,4096]{2,1,0:T(8,128)(2,1)}, s32[]{:T(128)}) %tuple.56), condition=%wide.while_cond, body=%wide.while_body.sunk | while | flops 2 | bytes 2098265 | solution.py:30
  172.9 8.2 %multiply_reduce_fusion.6 = f32[4096,128]{0,1:T(8,128)} fusion(f32[4096,8]{0,1:T(8,128)S(1)} %bitcast_convert_fusion.6, bf16[8,128,4096]{2,1,0:T(8,128)(2,1)} %get-tuple-element.289, pred[8,128]{1,0:T(8,128)(4,1)S(1)} %broadcast_compare_fusion.3), kind=kLoop, calls=%fused_computation.4.clone.1.clone | loop fusion | flops 16252928 | bytes 10617856 | tf_op jit(solution)/shard_map/while/body/eval_jaxpr/trc,tc->rc/dot_general | solution.py:36
  191.7 19.0 %while.22 = (s32[]{:T(128)}, bf16[256,4096]{1,0:T(8,128)(2,1)S(1)}, s32[8,2]{0,1:T(2,128)S(1)}, bf16[8,128,4096]{2,1,0:T(8,128)(2,1)}, s32[]{:T(128)}) while((s32[]{:T(128)}, bf16[256,4096]{1,0:T(8,128)(2,1)S(1)}, s32[8,2]{0,1:T(2,128)S(1)}, bf16[8,128,4096]{2,1,0:T(8,128)(2,1)}, s32[]{:T(128)}) %tuple.56), condition=%wide.while_cond, body=%wide.while_body.sunk | while | flops 2 | bytes 2098265 | solution.py:30
  210.8 8.2 %multiply_reduce_fusion.6 = f32[4096,128]{0,1:T(8,128)} fusion(f32[4096,8]{0,1:T(8,128)S(1)} %bitcast_convert_fusion.6, bf16[8,128,4096]{2,1,0:T(8,128)(2,1)} %get-tuple-element.289, pred[8,128]{1,0:T(8,128)(4,1)S(1)} %broadcast_compare_fusion.3), kind=kLoop, calls=%fused_computation.4.clone.1.clone | loop fusion | flops 16252928 | bytes 10617856 | tf_op jit(solution)/shard_map/while/body/eval_jaxpr/trc,tc->rc/dot_general | solution.py:36
  229.6 19.0 %while.22 = (s32[]{:T(128)}, bf16[256,4096]{1,0:T(8,128)(2,1)S(1)}, s32[8,2]{0,1:T(2,128)S(1)}, bf16[8,128,4096]{2,1,0:T(8,128)(2,1)}, s32[]{:T(128)}) while((s32[]{:T(128)}, bf16[256,4096]{1,0:T(8,128)(2,1)S(1)}, s32[8,2]{0,1:T(2,128)S(1)}, bf16[8,128,4096]{2,1,0:T(8,128)(2,1)}, s32[]{:T(128)}) %tuple.56), condition=%wide.while_cond, body=%wide.while_body.sunk | while | flops 2 | bytes 2098265 | solution.py:30
  248.7 8.2 %multiply_reduce_fusion.6 = f32[4096,128]{0,1:T(8,128)} fusion(f32[4096,8]{0,1:T(8,128)S(1)} %bitcast_convert_fusion.6, bf16[8,128,4096]{2,1,0:T(8,128)(2,1)} %get-tuple-element.289, pred[8,128]{1,0:T(8,128)(4,1)S(1)} %broadcast_compare_fusion.3), kind=kLoop, calls=%fused_computation.4.clone.1.clone | loop fusion | flops 16252928 | bytes 10617856 | tf_op jit(solution)/shard_map/while/body/eval_jaxpr/trc,tc->rc/dot_general | solution.py:36
  256.8 4.0 bitcast_add_fusion.3
  267.5 19.0 %while.22 = (s32[]{:T(128)}, bf16[256,4096]{1,0:T(8,128)(2,1)S(1)}, s32[8,2]{0,1:T(2,128)S(1)}, bf16[8,128,4096]{2,1,0:T(8,128)(2,1)}, s32[]{:T(128)}) while((s32[]{:T(128)}, bf16[256,4096]{1,0:T(8,128)(2,1)S(1)}, s32[8,2]{0,1:T(2,128)S(1)}, bf16[8,128,4096]{2,1,0:T(8,128)(2,1)}, s32[]{:T(128)}) %tuple.56), condition=%wide.while_cond, body=%wide.while_body.sunk | while | flops 2 | bytes 2098265 | solution.py:30
  286.6 8.2 %multiply_reduce_fusion.6 = f32[4096,128]{0,1:T(8,128)} fusion(f32[4096,8]{0,1:T(8,128)S(1)} %bitcast_convert_fusion.6, bf16[8,128,4096]{2,1,0:T(8,128)(2,1)} %get-tuple-element.289, pred[8,128]{1,0:T(8,128)(4,1)S(1)} %broadcast_compare_fusion.3), kind=kLoop, calls=%fused_computation.4.clone.1.clone | loop fusion | flops 16252928 | bytes 10617856 | tf_op jit(solution)/shard_map/while/body/eval_jaxpr/trc,tc->rc/dot_general | solution.py:36
  294.7 4.0 bitcast_add_fusion.3
  305.4 19.0 %while.22 = (s32[]{:T(128)}, bf16[256,4096]{1,0:T(8,128)(2,1)S(1)}, s32[8,2]{0,1:T(2,128)S(1)}, bf16[8,128,4096]{2,1,0:T(8,128)(2,1)}, s32[]{:T(128)}) while((s32[]{:T(128)}, bf16[256,4096]{1,0:T(8,128)(2,1)S(1)}, s32[8,2]{0,1:T(2,128)S(1)}, bf16[8,128,4096]{2,1,0:T(8,128)(2,1)}, s32[]{:T(128)}) %tuple.56), condition=%wide.while_cond, body=%wide.while_body.sunk | while | flops 2 | bytes 2098265 | solution.py:30
  324.4 8.2 %multiply_reduce_fusion.6 = f32[4096,128]{0,1:T(8,128)} fusion(f32[4096,8]{0,1:T(8,128)S(1)} %bitcast_convert_fusion.6, bf16[8,128,4096]{2,1,0:T(8,128)(2,1)} %get-tuple-element.289, pred[8,128]{1,0:T(8,128)(4,1)S(1)} %broadcast_compare_fusion.3), kind=kLoop, calls=%fused_computation.4.clone.1.clone | loop fusion | flops 16252928 | bytes 10617856 | tf_op jit(solution)/shard_map/while/body/eval_jaxpr/trc,tc->rc/dot_general | solution.py:36
  332.6 4.0 bitcast_add_fusion.3
  342.4 26.4 %reduce-scatter.2.cloned.1.call-done = f32[1024,64]{0,1:T(8,128)} async-done(((f32[4096,64]{0,1:T(8,128)}), f32[1024,64]{0,1:T(8,128)}) %reduce-scatter.2.cloned.1.call-update) | async-done | bytes 262160 | tf_op jit(solution)/shard_map/reduce_scatter | solution.py:50
  371.5 71.5 %all-reduce.3.cloned.1.call-done = f32[1024,64]{0,1:T(8,128)} async-done(((f32[1024,64]{0,1:T(8,128)}), f32[1024,64]{0,1:T(8,128)}) %all-reduce.3.cloned.1.call-update) | async-done | bytes 262160 | tf_op jit(solution)/shard_map/psum | solution.py:51
  (301 shorter events, 235.6 us)
Async XLA Ops:
  7.2 32.8 %copy-start.1 = (bf16[128,4096]{1,0:T(8,128)(2,1)S(1)}, bf16[128,4096]{1,0:T(8,128)(2,1)}, u32[]{:S(2)}) copy-start(bf16[128,4096]{1,0:T(8,128)(2,1)} %param.9) | copy-start | bytes 3145732
  7.2 361.6 %reduce-scatter.2.cloned.1.call-start = ((), (), s32[]{:S(2)}) async-start(), calls=%async_computation.1 | async-start | bytes 1310720 | tf_op jit(solution)/shard_map/reduce_scatter | solution.py:50
  9.1 12.2 %copy-start.2 = (bf16[128,4096]{1,0:T(8,128)(2,1)}, bf16[128,4096]{1,0:T(8,128)(2,1)S(1)}, u32[]{:S(2)}) copy-start(bf16[128,4096]{1,0:T(8,128)(2,1)S(1)} %multiply_convert_fusion) | copy-start | bytes 3145732
  9.1 28.1 %collective-permute-start = (bf16[128,4096]{1,0:T(8,128)(2,1)S(1)}, bf16[128,4096]{1,0:T(8,128)(2,1)}, u32[]{:S(2)}, u32[]{:S(2)}) collective-permute-start(bf16[128,4096]{1,0:T(8,128)(2,1)S(1)} %multiply_convert_fusion), channel_id=1, source_target_pairs={{1,0},{2,1},{3,2},{4,3},{5,4},{6,5},{7,6},{9,8},{10,9},{11,10},{12... | collective-permute-start | bytes 3145736 | tf_op jit(solution)/shard_map/ppermute | solution.py:10
  68.1 4.8 %copy-start = (bf16[8,128,4096]{2,1,0:T(8,128)(2,1)S(1)}, bf16[8,128,4096]{2,1,0:T(8,128)(2,1)}, u32[]{:S(2)}) copy-start(bf16[8,128,4096]{2,1,0:T(8,128)(2,1)} %get-tuple-element.289) | copy-start | bytes 25165828 | tf_op jit(solution)/shard_map/while
  105.3 5.4 %copy-start = (bf16[8,128,4096]{2,1,0:T(8,128)(2,1)S(1)}, bf16[8,128,4096]{2,1,0:T(8,128)(2,1)}, u32[]{:S(2)}) copy-start(bf16[8,128,4096]{2,1,0:T(8,128)(2,1)} %get-tuple-element.289) | copy-start | bytes 25165828 | tf_op jit(solution)/shard_map/while
  143.2 5.4 %copy-start = (bf16[8,128,4096]{2,1,0:T(8,128)(2,1)S(1)}, bf16[8,128,4096]{2,1,0:T(8,128)(2,1)}, u32[]{:S(2)}) copy-start(bf16[8,128,4096]{2,1,0:T(8,128)(2,1)} %get-tuple-element.289) | copy-start | bytes 25165828 | tf_op jit(solution)/shard_map/while
  181.1 5.4 %copy-start = (bf16[8,128,4096]{2,1,0:T(8,128)(2,1)S(1)}, bf16[8,128,4096]{2,1,0:T(8,128)(2,1)}, u32[]{:S(2)}) copy-start(bf16[8,128,4096]{2,1,0:T(8,128)(2,1)} %get-tuple-element.289) | copy-start | bytes 25165828 | tf_op jit(solution)/shard_map/while
  219.0 5.4 %copy-start = (bf16[8,128,4096]{2,1,0:T(8,128)(2,1)S(1)}, bf16[8,128,4096]{2,1,0:T(8,128)(2,1)}, u32[]{:S(2)}) copy-start(bf16[8,128,4096]{2,1,0:T(8,128)(2,1)} %get-tuple-element.289) | copy-start | bytes 25165828 | tf_op jit(solution)/shard_map/while
  256.8 5.4 %copy-start = (bf16[8,128,4096]{2,1,0:T(8,128)(2,1)S(1)}, bf16[8,128,4096]{2,1,0:T(8,128)(2,1)}, u32[]{:S(2)}) copy-start(bf16[8,128,4096]{2,1,0:T(8,128)(2,1)} %get-tuple-element.289) | copy-start | bytes 25165828 | tf_op jit(solution)/shard_map/while
  294.7 5.4 %copy-start = (bf16[8,128,4096]{2,1,0:T(8,128)(2,1)S(1)}, bf16[8,128,4096]{2,1,0:T(8,128)(2,1)}, u32[]{:S(2)}) copy-start(bf16[8,128,4096]{2,1,0:T(8,128)(2,1)} %get-tuple-element.289) | copy-start | bytes 25165828 | tf_op jit(solution)/shard_map/while
  332.6 5.4 %copy-start = (bf16[8,128,4096]{2,1,0:T(8,128)(2,1)S(1)}, bf16[8,128,4096]{2,1,0:T(8,128)(2,1)}, u32[]{:S(2)}) copy-start(bf16[8,128,4096]{2,1,0:T(8,128)(2,1)} %get-tuple-element.289) | copy-start | bytes 25165828 | tf_op jit(solution)/shard_map/while
  342.4 100.7 %all-reduce.3.cloned.1.call-start = ((), (), s32[]{:S(2)}) async-start(), calls=%async_computation.2 | async-start | bytes 524288 | tf_op jit(solution)/shard_map/psum | solution.py:51
Sparse Core Ops, SparseCore 0:
  342.5 26.2 reduce-scatter.1
  372.5 70.4 all-reduce.2
where the time goes:
time: 453 us; the launch traced here: 452 us
  local copies, waits for them, and re-layouts  169 us (37%)
  other arithmetic  142 us (31%)
  waiting for transfers between devices  114 us (25%)
  between operations  14.1 us (3%)
  blocking collectives  10.2 us (2%)
    gather x192, local copies, waits for them, and re-layouts  152 us
    psum x1, waiting for transfers between devices, body(): grad_filt = lax.psum(owned, 'ctx')  71.5 us
    dot_general x8, other arithmetic, one_group(): jnp.einsum('trc,tc->rc', windows, weights, preferred_element_type=jnp.flo...  65.2 us
    add x8, other arithmetic, one_group(): accum + jnp.einsum('trc,tc->rc', windows, weights, preferred_element_type...  31.5 us
    dot_general x8, other arithmetic, one_group(): jnp.einsum('trc,rc->tc', windows, conv_in, preferred_element_type=jnp.flo...  29.6 us
    reduce_scatter x1, waiting for transfers between devices, body(): owned = lax.psum_scatter(filt_terms, 'dp', scatter_dimension=0, tiled=True)  26.4 us
    ppermute x1, waiting for transfers between devices, from_behind(): lax.ppermute(value, axis, [(source, source + steps) for source in range(f...  15.9 us
    all_gather x1, blocking collectives, body(): whole_filter = lax.all_gather(filt, 'dp', axis=0, tiled=True)  10.2 us
  transfers between devices with their start and end apart: 3, of which 3 were waited for; matrix products, arithmetic and copies ran while one was open for 1% of the time, Pallas kernels for 0%

commit v1 on v0

v1 whole, which is shorter than its diff:
```python
import math

import jax
import jax.numpy as jnp
from jax import lax
from jax.experimental import pallas as pl
from jax.experimental.pallas import tpu as pltpu
from jax.sharding import PartitionSpec as P

LANE = 128


def half_wave(value):
    square = value * value
    total = jnp.zeros_like(value)
    for power in (13, 11, 9, 7, 5, 3, 1):
        sign = -1.0 if power % 4 == 3 else 1.0
        total = total * square + sign * (2 * math.pi) ** power / math.factorial(power)
    return total * value


def waves(turns):
    size = jnp.abs(turns)
    folded = jnp.minimum(size, 0.5 - size)
    return half_wave(0.25 - size), half_wave(jnp.where(turns < 0.0, -folded, folded))


def two_parts(value):
    high = value.astype(jnp.bfloat16)
    return high, (value - high.astype(jnp.float32)).astype(jnp.bfloat16)


def turns_of(order, offset, size):
    inverse = 1.0 / size.astype(jnp.float32)
    product = (order * offset).astype(jnp.float32)
    whole = jnp.floor(product * inverse + 0.5)
    return (product - whole * size.astype(jnp.float32)) * inverse, inverse


def iota(shape, axis):
    return lax.broadcasted_iota(jnp.int32, shape, axis)


def store_narrow(ref, taps, waves_of):
    bins = ref.shape[0] // 2
    first = iota((bins, 2 * taps), 1) < taps
    for which, wave in enumerate(waves_of):
        high, low = two_parts(wave)
        both = jnp.where(first, high.astype(jnp.float32), low.astype(jnp.float32))
        ref[which * bins:(which + 1) * bins, :] = both.astype(jnp.bfloat16)


def store_back(ref, which, wave):
    count, bins = wave.shape
    ref[0:count, which * bins:(which + 1) * bins], ref[count:2 * count, which * bins:(which + 1) * bins] = two_parts(wave)


def basis_kernel(end_ref, first_ref, rows_ref, taps_ref, input_ref, filter_ref,
                 halo_rows_ref, halo_tail_ref, halo_taps_ref, halo_input_ref, halo_filter_ref, down_ref, across_ref):
    rows, taps = input_ref.shape[0] // 2, filter_ref.shape[0] // 2
    bins = rows
    for ref in (down_ref, across_ref):
        ref[...] = jnp.zeros_like(ref)
        ref[2] = jnp.ones_like(ref[2])

    def document(state):
        start, base, _ = state
        end = jnp.minimum(end_ref[start] - first_ref[0], rows)
        length = end - start
        lags = jnp.minimum(taps, length)
        size = length + lags - 1
        size = size + 1 - lax.rem(size, 2)
        count = (size + 1) // 2
        for ref, axis in ((down_ref, 0), (across_ref, 1)):
            at = iota(ref.shape[1:], axis)
            mine = (at >= base) & (at < base + count)
            for which, value in enumerate((start, end, size, at - base, lags)):
                ref[which] = jnp.where(mine, value, ref[which])
        return end, base + count, start

    start_state = (jnp.int32(0), jnp.int32(0), jnp.int32(0))
    _, _, last_start = lax.while_loop(lambda state: state[0] < rows, document, start_state)

    start, end, size, order, lags = [down_ref[which] for which in range(5)]
    for block in range(rows // LANE):
        at = iota(start.shape, 1) + block * LANE
        inside = (at >= start) & (at < end)
        for which, wave in enumerate(waves(turns_of(order, at - start, size)[0])):
            high, low = two_parts(jnp.where(inside, wave, 0.0))
            below, lanes = which * bins, block * LANE
            rows_ref[below:below + bins, lanes:lanes + LANE] = high
            rows_ref[below:below + bins, rows + lanes:rows + lanes + LANE] = low
    narrow = start[:, 0:2 * taps].shape
    at = iota(narrow, 1)
    at = jnp.where(at < taps, at, at - taps)
    inside = at < lags[:, 0:2 * taps]
    turned = waves(turns_of(order[:, 0:2 * taps], at, size[:, 0:2 * taps])[0])
    store_narrow(taps_ref, taps, [jnp.where(inside, wave, 0.0) for wave in turned])

    start, end, size, order, lags = [across_ref[which, 0:1, :] for which in range(5)]
    for ref, count in ((input_ref, rows), (filter_ref, taps)):
        at = iota((count, bins), 0)
        if ref is input_ref:
            offset, inside = at - start, (at >= start) & (at < end)
        else:
            offset, inside = at, at < lags
        turns, inverse = turns_of(order, offset, size)
        weight = jnp.where(inside, jnp.where(order == 0, inverse, 2.0 * inverse), 0.0)
        for which, wave in enumerate(waves(turns)):
            store_back(ref, which, weight * wave)

    end = jnp.minimum(end_ref[rows - 1] - first_ref[0] - rows, taps - 1)
    begin = jnp.where(end > 0, last_start - (rows - taps), taps)
    size = jnp.full((taps, 2 * taps), 2 * taps - 1, jnp.int32)
    at = iota(size.shape, 1)
    at = jnp.where(at < taps, at, at - taps)
    turned = waves(turns_of(iota(size.shape, 0), at, size)[0])
    store_narrow(halo_taps_ref, taps, turned)
    store_narrow(halo_rows_ref, taps, [jnp.where(at < end, wave, 0.0) for wave in turned])
    store_narrow(halo_tail_ref, taps, [jnp.where(at >= begin, wave, 0.0) for wave in turned])
    size = jnp.full((taps, taps), 2 * taps - 1, jnp.int32)
    at, order = iota(size.shape, 0), iota(size.shape, 1)
    turns, inverse = turns_of(order, at - taps, size)
    weight = jnp.where(at > 0, jnp.where(order == 0, inverse, 2.0 * inverse), 0.0)
    for which, wave in enumerate(waves(turns)):
        store_back(halo_filter_ref, which, weight * wave)
        store_back(halo_input_ref, which, jnp.where(at >= begin, weight * wave, 0.0))


def product(left, right):
    return jnp.dot(left, right, preferred_element_type=jnp.float32)


def transform(basis_ref, twice_ref, value):
    twice(twice_ref, value)
    return product(basis_ref[...], twice_ref[...])


def correlate(left, right, basis_ref, z_ref):
    bins, count = left.shape[0] // 2, basis_ref.shape[0] // 2
    lc, ls, rc, rs = left[:bins], left[bins:], right[:bins], right[bins:]
    z_ref[0, 0:bins, :], z_ref[1, 0:bins, :] = two_parts(lc * rc + ls * rs)
    z_ref[0, bins:, :], z_ref[1, bins:, :] = two_parts(ls * rc - lc * rs)
    both = product(basis_ref[...], z_ref[0])
    return both[:count] + (both[count:] + product(basis_ref[0:count, :], z_ref[1]))


def twice(ref, value):
    count = value.shape[0]
    ref[0:count, :] = value
    ref[count:2 * count, :] = value


def gated(grad_out, gate):
    return (grad_out.astype(jnp.float32) * gate.astype(jnp.float32)).astype(jnp.bfloat16)


def in_turn(count, width, unit):
    together = 2 if count % 2 == 0 else 1

    def step(at, carry):
        for slot in range(together):
            which = at * together + slot
            unit(which, pl.ds(pl.multiple_of(which * width, LANE), width), slot)
        return carry

    lax.fori_loop(0, count // together, step, 0)


def place_pieces(place_ref, pieces, f_ref):
    order = iter(slots(f_ref.shape[0]))
    for piece in pieces:
        for which in range(piece.shape[0]):
            twice(f_ref.at[jnp.bitwise_xor(place_ref[0], next(order))], piece[which])


def own_filter_kernel(rows_ref, filter_ref, grad_out_ref, gate_ref, conv_in_ref, terms_ref, y_ref, x_ref, z_ref):
    width = y_ref.shape[2]

    def unit(which, lanes, slot):
        y_hat = transform(rows_ref, y_ref.at[slot], gated(grad_out_ref[:, lanes], gate_ref[:, lanes]))
        x_hat = transform(rows_ref, x_ref.at[slot], conv_in_ref[:, lanes])
        terms_ref[:, lanes] = correlate(y_hat, x_hat, filter_ref, z_ref.at[slot])

    in_turn(terms_ref.shape[1] // width, width, unit)


def own_input_kernel(place_ref, rows_ref, taps_ref, input_ref, grad_out_ref, gate_ref, *refs):
    pieces, (head_ref, tail_ref, y_ref, f_ref, z_ref) = refs[:-5], refs[-5:]
    channels, width = head_ref.shape[1], y_ref.shape[2]
    place_pieces(place_ref, pieces, f_ref)

    def unit(which, lanes, slot):
        y_hat = transform(rows_ref, y_ref.at[slot], gated(grad_out_ref[:, lanes], gate_ref[:, lanes]))
        grad_in = correlate(y_hat, product(taps_ref[...], f_ref[which]), input_ref, z_ref.at[slot])
        head_ref[:, lanes] = grad_in[:head_ref.shape[0]].astype(head_ref.dtype)
        tail_ref[:, lanes] = grad_in[head_ref.shape[0]:]

    in_turn(channels // width, width, unit)


def halo_filter_kernel(place_ref, rows_ref, tail_ref, filter_ref, own_ref, conv_in_ref, halo_ref, after_ref,
                       keep_ref, send_ref, y_ref, x_ref, z_ref, sum_ref):
    del after_ref
    taps, owners = own_ref.shape[0], y_ref.shape[0]
    rows, width = conv_in_ref.shape[0], y_ref.shape[2]
    for which in range(owners):
        lanes = pl.ds(which * width, width)
        y_hat = transform(rows_ref, y_ref.at[which], halo_ref[:, lanes])
        x_hat = transform(tail_ref, x_ref.at[which], conv_in_ref[rows - taps:, lanes])
        sum_ref[which] = own_ref[:, lanes] + correlate(y_hat, x_hat, filter_ref, z_ref.at[which])
    for pair in range(owners // 2):
        keep_ref[pair] = sum_ref[jnp.bitwise_xor(place_ref[0], 2 * pair)]
        send_ref[pair] = sum_ref[jnp.bitwise_xor(place_ref[0], 2 * pair + 1)].astype(send_ref.dtype)


def halo_input_kernel(place_ref, rows_ref, taps_ref, input_ref, after_ref, halo_ref, head_ref, tail_ref, *refs):
    pieces, (out_ref, passed_ref, y_ref, f_ref, z_ref) = refs[:-5], refs[-5:]
    step = pl.program_id(0)
    head = head_ref.shape[0]

    @pl.when(step == 0)
    def _():
        place_pieces(place_ref, pieces, f_ref)
        passed_ref[...] = after_ref[...]

    y_hat = transform(rows_ref, y_ref, halo_ref[...])
    value = correlate(y_hat, product(taps_ref[...], f_ref[step]), input_ref, z_ref)
    out_ref[0:head, :] = head_ref[...]
    out_ref[head:, :] = (tail_ref[...] + value).astype(out_ref.dtype)


def scalars():
    return pl.BlockSpec(memory_space=pltpu.SMEM)


def whole(array):
    return pl.BlockSpec(array.shape, lambda step: (0,) * len(array.shape))


def tiled(rows, tile, at=0):
    return pl.BlockSpec((rows, tile), lambda step: (at, step))


def scratch(rows, tile):
    return pltpu.VMEM((rows, tile), jnp.bfloat16)


def shaped(*shape, dtype=jnp.bfloat16):
    return jax.ShapeDtypeStruct(shape, dtype)


def params():
    return pltpu.CompilerParams(vmem_limit_bytes=24 * 1024 * 1024)


def cost(flops, moved):
    return pl.CostEstimate(flops=flops, bytes_accessed=moved, transcendentals=0)


def make_basis(doc_end, first, rows, taps):
    own = [shaped(2 * rows, 2 * rows), shaped(2 * rows, 2 * taps), shaped(2 * rows, 2 * rows), shaped(2 * taps, 2 * rows)]
    halo = [shaped(2 * taps, 2 * taps)] * 5
    return pl.pallas_call(
        basis_kernel,
        in_specs=[scalars(), scalars()],
        out_shape=own + halo,
        scratch_shapes=[pltpu.VMEM((5, rows, LANE), jnp.int32), pltpu.VMEM((5, 8, rows), jnp.int32)],
        compiler_params=params(),
        cost_estimate=cost(10000000, 1000000),
        name="basis",
    )(doc_end, first)


def inside(count):
    return [pl.BlockSpec(memory_space=pltpu.VMEM)] * count


def own_filter(bases, grad_out, gate, conv_in, taps, width):
    rows, channels = grad_out.shape
    return pl.pallas_call(
        own_filter_kernel,
        in_specs=inside(5),
        out_specs=inside(1)[0],
        out_shape=shaped(taps, channels, dtype=jnp.float32),
        scratch_shapes=[
            pltpu.VMEM((2, 2 * rows, width), jnp.bfloat16), pltpu.VMEM((2, 2 * rows, width), jnp.bfloat16),
            pltpu.VMEM((2, 2, 2 * rows, width), jnp.bfloat16),
        ],
        compiler_params=params(),
        cost_estimate=cost(20 * rows * rows * channels, (6 * rows + 4 * taps) * channels),
        name="own_filter",
    )(*bases, grad_out, gate, conv_in)


def own_input(place, bases, grad_out, gate, pieces, owners):
    rows, channels = grad_out.shape
    taps, width = pieces[0].shape[1:]
    return pl.pallas_call(
        own_input_kernel,
        in_specs=[scalars(), *inside(5 + len(pieces))],
        out_specs=inside(2),
        out_shape=[shaped(rows - taps, channels), shaped(taps, channels, dtype=jnp.float32)],
        scratch_shapes=[
            pltpu.VMEM((2, 2 * rows, width), jnp.bfloat16), pltpu.VMEM((owners, 2 * taps, width), jnp.bfloat16),
            pltpu.VMEM((2, 2, 2 * rows, width), jnp.bfloat16),
        ],
        compiler_params=params(),
        cost_estimate=cost(30 * rows * rows * channels, (6 * rows + 6 * taps) * channels),
        name="own_input",
    )(place, *bases, grad_out, gate, *pieces)


def halo_filter(place, bases, own, conv_in, halo, after, owners):
    rows, channels = conv_in.shape
    taps = halo.shape[0]
    width = channels // owners
    twice_held = pltpu.VMEM((owners, 2 * taps, width), jnp.bfloat16)
    return pl.pallas_call(
        halo_filter_kernel,
        in_specs=[scalars(), *inside(7)],
        out_specs=inside(2),
        out_shape=[shaped(owners // 2, taps, width, dtype=jnp.float32), shaped(owners // 2, taps, width)],
        scratch_shapes=[
            twice_held, twice_held, pltpu.VMEM((owners, 2, 2 * taps, width), jnp.bfloat16),
            pltpu.VMEM((owners, taps, width), jnp.float32),
        ],
        compiler_params=params(),
        cost_estimate=cost(28 * taps * taps * channels, 10 * taps * channels),
        name="halo_filter",
    )(place, *bases, own, conv_in, halo, after)


def halo_input(place, bases, after, halo, head, tail, pieces, owners):
    taps, channels = halo.shape
    width = channels // owners
    rows = head.shape[0] + taps
    return pl.pallas_call(
        halo_input_kernel,
        grid=(owners,),
        in_specs=[
            scalars(), *[whole(basis) for basis in bases], *inside(1), tiled(taps, width), tiled(rows - taps, width),
            tiled(taps, width), *[whole(piece) for piece in pieces],
        ],
        out_specs=[tiled(rows, width), *inside(1)],
        out_shape=[shaped(rows, channels), shaped(*after.shape, dtype=after.dtype)],
        scratch_shapes=[
            scratch(2 * taps, width), pltpu.VMEM((owners, 2 * taps, width), jnp.bfloat16),
            pltpu.VMEM((2, 2 * taps, width), jnp.bfloat16),
        ],
        compiler_params=params(),
        cost_estimate=cost(28 * taps * taps * channels, 10 * taps * channels),
        name="halo_input",
    )(place, *bases, after, halo, head, tail, *pieces)


def slots(owners):
    order, bit = [0], owners // 2
    while bit:
        order += [m + bit for m in order]
        bit //= 2
    return order


def swap(value, axis, bit):
    return lax.ppermute(value, axis, [(source, source ^ bit) for source in range(lax.axis_size(axis))])


def gather(value, axis):
    held, bit = [value[None]], lax.axis_size(axis) // 2
    while bit:
        held.append(swap(jnp.concatenate(held) if len(held) > 1 else held[0], axis, bit))
        bit //= 2
    return held


def narrow(value):
    return value.astype(jnp.bfloat16)


def widen(value):
    return value.astype(jnp.float32)


def body(grad_out, gate, conv_in, filt, doc_end):
    rows, channels = grad_out.shape
    taps = filt.shape[1]
    dp, ctx = lax.axis_size("dp"), lax.axis_size("ctx")
    owner, block = lax.axis_index("dp"), lax.axis_index("ctx")
    place = owner.reshape(1)
    first_row = ((owner * ctx + block) * rows).reshape(1)

    following = narrow(widen(grad_out[:taps]) * widen(gate[:taps]))
    halo = lax.ppermute(following, "ctx", [(source, source - 1) for source in range(1, ctx)])
    pieces = gather(filt.T, "dp")

    bases = make_basis(doc_end, first_row, rows, taps)
    halo_rows, halo_tail, halo_taps, halo_inverse_input, halo_inverse_filter = bases[4:]
    own = own_filter((bases[0], bases[3]), grad_out, gate, conv_in, taps, channels // dp)
    head, tail = own_input(place, bases[:3], grad_out, gate, pieces, dp)
    keep, send = halo_filter(place, (halo_rows, halo_tail, halo_inverse_filter), own, conv_in, halo, tail, dp)

    arrived, bit = swap(send, "dp", 1), 2
    while bit < dp:
        total = keep + widen(arrived)
        keep, arrived = total[0::2], swap(narrow(total[1::2]), "dp", bit)
        bit *= 2
    grad_in, keep = halo_input(
        place, (halo_rows, halo_taps, halo_inverse_input), keep, halo, head, tail, pieces, dp
    )
    total = (keep + widen(arrived))[0]
    half = taps // 2
    low = lax.rem(block, 2) == 0
    kept = jnp.where(low, total[:half], total[half:])
    total = kept + widen(swap(narrow(jnp.where(low, total[half:], total[:half])), "ctx", 1))
    bit = 2
    while bit < ctx:
        mine = narrow(total)
        total = widen(mine) + widen(swap(mine, "ctx", bit))
        bit *= 2
    mine = narrow(total)
    other = swap(mine, "ctx", 1)
    both = jnp.concatenate([jnp.where(low, mine, other), jnp.where(low, other, mine)])
    return (grad_in, widen(both).T)


def solution(mesh):
    placed = (
        P(("dp", "ctx"), None),
        P(("dp", "ctx"), None),
        P(("dp", "ctx"), None),
        P("dp", None),
        P(("dp", "ctx")),
    )
    return jax.shard_map(
        body,
        mesh=mesh,
        in_specs=placed,
        out_specs=(P(("dp", "ctx"), None), P("dp", None)),
        check_vma=False,
    )
```

time: 453 us -> 50.3 us (0.11)
  local copies, waits for them, and re-layouts: 169 us -> 5.72 us
  other arithmetic: 142 us -> 3.03 us
  waiting for transfers between devices: 114 us -> 13.6 us
  between operations: 14.1 us -> 0.81 us
  starting transfers between devices: 1.37 us -> 14.3 us
  Pallas kernels: 0 us -> 12.5 us
  blocking collectives: 10.2 us -> 0 us
    gather x192 -> x0, local copies, waits for them, and re-layouts: 152 us -> none
    dot_general x16 -> x0, other arithmetic: 94.8 us -> none  [the longest x8 65.2 us: one_group(): jnp.einsum('trc,tc->rc', windows, weights, preferred_element_type=jnp.flo...]
    psum x1 -> x0, waiting for transfers between devices: 71.5 us -> none  [body(): grad_filt = lax.psum(owned, 'ctx')]
    add x16 -> x2, other arithmetic: 31.6 us -> 0.09 us  [the longest x1 0.05 us: body(): total = keep + widen(arrived)]
    reduce_scatter x1 -> x0, waiting for transfers between devices: 26.4 us -> none  [body(): owned = lax.psum_scatter(filt_terms, 'dp', scatter_dimension=0, tiled=True)]
    ppermute x1 -> x9, starting transfers between devices: 1.29 us -> 14.3 us  [the longest x8 13 us: swap(): lax.ppermute(value, axis, [(source, source ^ bit) for source in range(lax...]
    pallas_call x0 -> x5, Pallas kernels: none -> 12.5 us  [the longest x1 3.37 us: halo_input(): pl.pallas_call(halo_input_kernel, grid=(owners,), in_specs=[scalars(), *[...]
    all_gather x1 -> x0, blocking collectives: 10.2 us -> none  [body(): whole_filter = lax.all_gather(filt, 'dp', axis=0, tiled=True)]
  transfers between devices with their start and end apart: 3 -> 9, of which waited for: 3 -> 8; matrix products, arithmetic and copies ran while one was open for 1% -> 4% of each run, Pallas kernels for 0% -> 21%
where the time goes in v1:
time: 50.3 us; the launch traced here: 49.9 us
  starting transfers between devices  14.3 us (28%)
  waiting for transfers between devices  13.6 us (27%)
  Pallas kernels  12.5 us (25%)
  local copies, waits for them, and re-layouts  5.72 us (11%)
  other arithmetic  3.03 us (6%)
  between operations  0.81 us (2%)
    ppermute x8, starting transfers between devices, swap(): lax.ppermute(value, axis, [(source, source ^ bit) for source in range(lax...  13 us
    ppermute x8, waiting for transfers between devices, swap(): lax.ppermute(value, axis, [(source, source ^ bit) for source in range(lax...  12 us
    unnamed x18, local copies, waits for them, and re-layouts  5.68 us
    pallas_call x1, Pallas kernels, halo_input(): pl.pallas_call(halo_input_kernel, grid=(owners,), in_specs=[scalars(), *[...  3.37 us
    pallas_call x1, Pallas kernels, own_input(): pl.pallas_call(own_input_kernel, in_specs=[scalars(), *inside(5 + len(pie...  3.12 us
    pallas_call x1, Pallas kernels, own_filter(): pl.pallas_call(own_filter_kernel, in_specs=inside(5), out_specs=inside(1)...  2.94 us
    convert_element_type x5, other arithmetic, narrow(): return value.astype(jnp.bfloat16)  2.19 us
    pallas_call x1, Pallas kernels, halo_filter(): pl.pallas_call(halo_filter_kernel, in_specs=[scalars(), *inside(7)], out_...  1.77 us
  transfers between devices with their start and end apart: 9, of which 8 were waited for; matrix products, arithmetic and copies ran while one was open for 4% of the time, Pallas kernels for 21%

profile of v1, /device:TPU:0, one launch (start us, length us, event | category | flops | bytes accessed | tf_op | source)
XLA Modules:
  0.0 49.9 jit_solution(699845097417948381)
XLA Ops:
  0.6 3.0 %collective-permute-start.1 = (bf16[1,64,1024]{2,1,0:T(8,128)(2,1)}, bf16[1,64,1024]{2,1,0:T(8,128)(2,1)S(1)}, u32[]{:S(2)}, u32[]{:S(2)}) collective-permute-start(bf16[1,64,1024]{2,1,0:T(8,128)(2,1)} %bitcast.13), channel_id=1, source_target_pairs={{0,16},{8,24},{16,0},{24,8},{1,17},{9,25},{17,1},{25,9},{2,18},{10... | collective-permute-start | bytes 393224 | tf_op jit(solution)/shard_map/ppermute | solution.py:366
  3.7 2.1 %multiply_convert_fusion = bf16[64,4096]{1,0:T(8,128)(2,1)} fusion(bf16[128,4096]{1,0:T(8,128)(2,1)} %gate_ref.3, bf16[128,4096]{1,0:T(8,128)(2,1)} %grad_out_ref.3), kind=kLoop, calls=%fused_computation | loop fusion | flops 1048576 | bytes 1572864 | tf_op jit(solution)/shard_map/convert_element_type | solution.py:378
  5.8 1.3 %collective-permute-start = (bf16[64,4096]{1,0:T(8,128)(2,1)}, bf16[64,4096]{1,0:T(8,128)(2,1)S(1)}, u32[]{:S(2)}, u32[]{:S(2)}) collective-permute-start(bf16[64,4096]{1,0:T(8,128)(2,1)} %multiply_convert_fusion), channel_id=1, source_target_pairs={{1,0},{2,1},{3,2},{4,3},{5,4},{6,5},{7,6},{9,8},{10,9},{11,10},{12... | collective-permute-start | bytes 1572872 | tf_op jit(solution)/shard_map/ppermute | solution.py:394
  8.1 1.3 %basis.1 = (bf16[256,256]{1,0:T(8,128)(2,1)S(1)}, bf16[256,128]{1,0:T(8,128)(2,1)S(1)}, bf16[256,256]{1,0:T(8,128)(2,1)S(1)}, bf16[128,256]{1,0:T(8,128)(2,1)S(1...) custom-call(s32[128]{0:T(128)S(1)} %copy-done.8, ...), custom_call_target="tpu_custom_call" | custom-call | flops 10000000 | bytes 1000000 | tf_op jit(solution)/shard_map/basis/pallas_call | solution.py:264
  9.5 1.2 %copy-done.2 = bf16[128,4096]{1,0:T(8,128)(2,1)S(1)} copy-done((bf16[128,4096]{1,0:T(8,128)(2,1)S(1)}, bf16[128,4096]{1,0:T(8,128)(2,1)}, u32[]{:S(2)}) %copy-start.2) | copy-done | bytes 1048600
  10.7 1.2 %copy-done.4 = bf16[128,4096]{1,0:T(8,128)(2,1)S(1)} copy-done((bf16[128,4096]{1,0:T(8,128)(2,1)S(1)}, bf16[128,4096]{1,0:T(8,128)(2,1)}, u32[]{:S(2)}) %copy-start.4) | copy-done | bytes 1048600
  11.9 2.9 %own_filter.1.own_ref = f32[64,4096]{1,0:T(8,128)S(1)} custom-call(bf16[256,256]{1,0:T(8,128)(2,1)S(1)} %get-tuple-element.22.rows_ref, bf16[128,256]{1,0:T(8,128)(2,1)S(1)} %get-tuple-element.23.filter_ref, bf16[128,4096]{1,0:T(8,128)(2,1)S(1)} %copy-done.2, bf16[128,4096]{1,0:T(8,128)(2,1)S(1)} %copy-done.4, bf16[128,4096]{1,0:T(8,128)(2,1)S(1)} %copy-done), custom_call_target="tpu_custom_call" | custom-call | flops 1342177280 | bytes 4194304 | tf_op jit(solution)/shard_map/own_filter/pallas_call | solution.py:281
  15.6 0.9 %copy-done.6 = bf16[2,64,1024]{2,1,0:T(8,128)(2,1)S(1)} copy-done((bf16[2,64,1024]{2,1,0:T(8,128)(2,1)S(1)}, bf16[2,64,1024]{2,1,0:T(8,128)(2,1)}, u32[]{:S(2)}) %copy-start.6) | copy-done | bytes 262168
  16.5 3.1 %own_input.1 = (bf16[64,4096]{1,0:T(8,128)(2,1)S(1)}, f32[64,4096]{1,0:T(8,128)S(1)}) custom-call(s32[1]{0:T(128)} %bitcast.place_ref, bf16[256,256]{1,0:T(8,128)(2,1)S(1)} %get-tuple-element.22.rows_ref, bf16[256,128]{1,0:T(8,128)(2,1)S(1)} %get-tuple-element.24.taps_ref, bf16[256,256]{1,0:T(8,128)(2,1)S(1)} %get-tuple-element.25.input_ref, ...), custom_call_target="tpu_custom_call" | custom-call | flops 2013265920 | bytes 4718592 | tf_op jit(solution)/shard_map/own_input/pallas_call | solution.py:299
  19.7 1.6 %collective-permute-done.halo_ref = bf16[64,4096]{1,0:T(8,128)(2,1)S(1)} collective-permute-done((bf16[64,4096]{1,0:T(8,128)(2,1)}, bf16[64,4096]{1,0:T(8,128)(2,1)S(1)}, u32[]{:S(2)}, u32[]{:S(2)}) %collective-permute-start) | collective-permute-done | bytes 524320 | tf_op jit(solution)/shard_map/ppermute | solution.py:394
  21.2 1.8 %halo_filter.1 = (f32[2,64,1024]{2,1,0:T(8,128)S(1)}, bf16[2,64,1024]{2,1,0:T(8,128)(2,1)S(1)}) custom-call(s32[1]{0:T(128)} %bitcast.place_ref, bf16[128,128]{1,0:T(8,128)(2,1)S(1)} %get-tuple-element.17.rows_ref, bf16[128,128]{1,0:T(8,128)(2,1)S(1)} %get-tuple-element.20.tail_ref, bf16[128,128]{1,0:T(8,128)(2,1)S(1)} %get-tuple-element.21.filter_ref, ...), custom_call_target="tpu_custom_call" | custom-call | flops 469762048 | bytes 2621440 | tf_op jit(solution)/shard_map/halo_filter/pallas_call | solution.py:319
  23.1 1.5 %collective-permute-done.3 = bf16[2,64,1024]{2,1,0:T(8,128)(2,1)S(1)} collective-permute-done((bf16[2,64,1024]{2,1,0:T(8,128)(2,1)S(1)}, bf16[2,64,1024]{2,1,0:T(8,128)(2,1)S(1)}, u32[]{:S(2)}, u32[]{:S(2)}) %collective-permute-start.3) | collective-permute-done | bytes 262176 | tf_op jit(solution)/shard_map/ppermute | solution.py:366
  25.2 0.9 %copy-done.7 = bf16[2,64,1024]{2,1,0:T(8,128)(2,1)S(1)} copy-done((bf16[2,64,1024]{2,1,0:T(8,128)(2,1)S(1)}, bf16[2,64,1024]{2,1,0:T(8,128)(2,1)}, u32[]{:S(2)}) %copy-start.7) | copy-done | bytes 262168
  26.1 3.4 %halo_input.1 = (bf16[128,4096]{1,0:T(8,128)(2,1)}, f32[1,64,1024]{2,1,0:T(8,128)S(1)}) custom-call(s32[1]{0:T(128)} %bitcast.place_ref, bf16[128,128]{1,0:T(8,128)(2,1)S(1)} %get-tuple-element.17.rows_ref, bf16[128,128]{1,0:T(8,128)(2,1)S(1)} %get-tuple-element.18.taps_ref, bf16[128,128]{1,0:T(8,128)(2,1)S(1)} %get-tuple-element.19.input_ref, ...), custom_call_target="tpu_custom_call" | custom-call | flops 469762048 | bytes 2621440 | tf_op jit(solution)/shard_map/halo_input/pallas_call | solution.py:338
  29.5 0.8 %collective-permute-done.4 = bf16[1,64,1024]{2,1,0:T(8,128)(2,1)S(1)} collective-permute-done((bf16[1,64,1024]{2,1,0:T(8,128)(2,1)S(1)}, bf16[1,64,1024]{2,1,0:T(8,128)(2,1)S(1)}, u32[]{:S(2)}, u32[]{:S(2)}) %collective-permute-start.4) | collective-permute-done | bytes 131104 | tf_op jit(solution)/shard_map/ppermute | solution.py:366
  30.4 2.5 %collective-permute-start.5 = (bf16[32,1024]{1,0:T(8,128)(2,1)S(1)}, bf16[32,1024]{1,0:T(8,128)(2,1)S(1)}, u32[]{:S(2)}, u32[]{:S(2)}) collective-permute-start(bf16[32,1024]{1,0:T(8,128)(2,1)S(1)} %fusion.1), channel_id=1, source_target_pairs={{0,1},{1,0},{2,3},{3,2},{4,5},{5,4},{6,7},{7,6},{8,9},{9,8},{10,11... | collective-permute-start | bytes 196616 | tf_op jit(solution)/shard_map/ppermute | solution.py:366
  32.8 2.2 %collective-permute-done.5 = bf16[32,1024]{1,0:T(8,128)(2,1)S(1)} collective-permute-done((bf16[32,1024]{1,0:T(8,128)(2,1)S(1)}, bf16[32,1024]{1,0:T(8,128)(2,1)S(1)}, u32[]{:S(2)}, u32[]{:S(2)}) %collective-permute-start.5) | collective-permute-done | bytes 65568 | tf_op jit(solution)/shard_map/ppermute | solution.py:366
  35.1 1.8 %collective-permute-start.6 = (bf16[32,1024]{1,0:T(8,128)(2,1)S(1)}, bf16[32,1024]{1,0:T(8,128)(2,1)S(1)}, u32[]{:S(2)}, u32[]{:S(2)}) collective-permute-start(bf16[32,1024]{1,0:T(8,128)(2,1)S(1)} %fusion), channel_id=1, source_target_pairs={{0,2},{1,3},{2,0},{3,1},{4,6},{5,7},{6,4},{7,5},{8,10},{9,11},{10,... | collective-permute-start | bytes 196616 | tf_op jit(solution)/shard_map/ppermute | solution.py:366
  36.9 2.6 %collective-permute-done.6 = bf16[32,1024]{1,0:T(8,128)(2,1)S(1)} collective-permute-done((bf16[32,1024]{1,0:T(8,128)(2,1)S(1)}, bf16[32,1024]{1,0:T(8,128)(2,1)S(1)}, u32[]{:S(2)}, u32[]{:S(2)}) %collective-permute-start.6) | collective-permute-done | bytes 65568 | tf_op jit(solution)/shard_map/ppermute | solution.py:366
  39.5 3.0 %collective-permute-start.7 = (bf16[32,1024]{1,0:T(8,128)(2,1)S(1)}, bf16[32,1024]{1,0:T(8,128)(2,1)S(1)}, u32[]{:S(2)}, u32[]{:S(2)}) collective-permute-start(bf16[32,1024]{1,0:T(8,128)(2,1)S(1)} %add_convert_fusion.1), channel_id=1, source_target_pairs={{0,4},{1,5},{2,6},{3,7},{4,0},{5,1},{6,2},{7,3},{8,12},{9,13},{10,... | collective-permute-start | bytes 196616 | tf_op jit(solution)/shard_map/ppermute | solution.py:366
  42.5 2.2 %collective-permute-done.7 = bf16[32,1024]{1,0:T(8,128)(2,1)S(1)} collective-permute-done((bf16[32,1024]{1,0:T(8,128)(2,1)S(1)}, bf16[32,1024]{1,0:T(8,128)(2,1)S(1)}, u32[]{:S(2)}, u32[]{:S(2)}) %collective-permute-start.7) | collective-permute-done | bytes 65568 | tf_op jit(solution)/shard_map/ppermute | solution.py:366
  44.8 2.1 %collective-permute-start.8 = (bf16[32,1024]{1,0:T(8,128)(2,1)S(1)}, bf16[32,1024]{1,0:T(8,128)(2,1)S(1)}, u32[]{:S(2)}, u32[]{:S(2)}) collective-permute-start(bf16[32,1024]{1,0:T(8,128)(2,1)S(1)} %add_convert_fusion), channel_id=1, source_target_pairs={{0,1},{1,0},{2,3},{3,2},{4,5},{5,4},{6,7},{7,6},{8,9},{9,8},{10,11... | collective-permute-start | bytes 196616 | tf_op jit(solution)/shard_map/ppermute | solution.py:366
  46.9 2.2 %collective-permute-done.8 = bf16[32,1024]{1,0:T(8,128)(2,1)S(1)} collective-permute-done((bf16[32,1024]{1,0:T(8,128)(2,1)S(1)}, bf16[32,1024]{1,0:T(8,128)(2,1)S(1)}, u32[]{:S(2)}, u32[]{:S(2)}) %collective-permute-start.8) | collective-permute-done | bytes 65568 | tf_op jit(solution)/shard_map/ppermute | solution.py:366
  49.2 0.7 %convert_bitcast_fusion = f32[1024,64]{0,1:T(8,128)} fusion(bf16[32,1024]{1,0:T(8,128)(2,1)S(1)} %get-tuple-element.33, bf16[32,1024]{1,0:T(8,128)(2,1)S(1)} %get-tuple-element.32), kind=kLoop, calls=%fused_computation.4 | loop fusion | flops 262144 | bytes 393216 | tf_op jit(solution)/shard_map/transpose | solution.py:424
  (29 shorter events, 2.5 us)
Async XLA Ops:
  0.6 6.7 %copy-start.1 = (bf16[1024,64]{0,1:T(8,128)(2,1)S(1)}, bf16[1024,64]{0,1:T(8,128)(2,1)}, u32[]{:S(2)}) copy-start(bf16[1024,64]{0,1:T(8,128)(2,1)} %param.8) | copy-start | bytes 393220
  0.6 8.8 %copy-start = (bf16[128,4096]{1,0:T(8,128)(2,1)S(1)}, bf16[128,4096]{1,0:T(8,128)(2,1)}, u32[]{:S(2)}) copy-start(bf16[128,4096]{1,0:T(8,128)(2,1)} %conv_in_ref.3) | copy-start | bytes 3145732
  0.6 6.7 %collective-permute-start.1 = (bf16[1,64,1024]{2,1,0:T(8,128)(2,1)}, bf16[1,64,1024]{2,1,0:T(8,128)(2,1)S(1)}, u32[]{:S(2)}, u32[]{:S(2)}) collective-permute-start(bf16[1,64,1024]{2,1,0:T(8,128)(2,1)} %bitcast.13), channel_id=1, source_target_pairs={{0,16},{8,24},{16,0},{24,8},{1,17},{9,25},{17,1},{25,9},{2,18},{10... | collective-permute-start | bytes 393224 | tf_op jit(solution)/shard_map/ppermute | solution.py:366
  5.8 15.5 %collective-permute-start = (bf16[64,4096]{1,0:T(8,128)(2,1)}, bf16[64,4096]{1,0:T(8,128)(2,1)S(1)}, u32[]{:S(2)}, u32[]{:S(2)}) collective-permute-start(bf16[64,4096]{1,0:T(8,128)(2,1)} %multiply_convert_fusion), channel_id=1, source_target_pairs={{1,0},{2,1},{3,2},{4,3},{5,4},{6,5},{7,6},{9,8},{10,9},{11,10},{12... | collective-permute-start | bytes 1572872 | tf_op jit(solution)/shard_map/ppermute | solution.py:394
  7.4 7.5 %collective-permute-start.2 = (bf16[2,64,1024]{2,1,0:T(8,128)(2,1)S(1)}, bf16[2,64,1024]{2,1,0:T(8,128)(2,1)S(1)}, u32[]{:S(2)}, u32[]{:S(2)}) collective-permute-start(bf16[2,64,1024]{2,1,0:T(8,128)(2,1)S(1)} %pad_maximum_fusion), channel_id=1, source_target_pairs={{0,8},{8,0},{16,24},{24,16},{1,9},{9,1},{17,25},{25,17},{2,10},{10... | collective-permute-start | bytes 786440 | tf_op jit(solution)/shard_map/ppermute | solution.py:366
  7.5 0.7 %copy-start.8 = (s32[128]{0:T(128)S(1)}, s32[128]{0:T(128)}, u32[]{:S(2)}) copy-start(s32[128]{0:T(128)} %end_ref.1) | copy-start | bytes 1540
  9.5 1.2 %copy-start.2 = (bf16[128,4096]{1,0:T(8,128)(2,1)S(1)}, bf16[128,4096]{1,0:T(8,128)(2,1)}, u32[]{:S(2)}) copy-start(bf16[128,4096]{1,0:T(8,128)(2,1)} %grad_out_ref.3) | copy-start | bytes 3145732
  10.7 1.2 %copy-start.4 = (bf16[128,4096]{1,0:T(8,128)(2,1)S(1)}, bf16[128,4096]{1,0:T(8,128)(2,1)}, u32[]{:S(2)}) copy-start(bf16[128,4096]{1,0:T(8,128)(2,1)} %gate_ref.3) | copy-start | bytes 3145732
  11.9 3.7 %copy-start.3 = (bf16[128,4096]{1,0:T(8,128)(2,1)S(1)}, bf16[128,4096]{1,0:T(8,128)(2,1)}, u32[]{:S(2)}) copy-start(bf16[128,4096]{1,0:T(8,128)(2,1)} %grad_out_ref.3) | copy-start | bytes 3145732
  14.9 0.7 %copy-start.5 = (bf16[2,64,1024]{2,1,0:T(8,128)(2,1)}, bf16[2,64,1024]{2,1,0:T(8,128)(2,1)S(1)}, u32[]{:S(2)}) copy-start(bf16[2,64,1024]{2,1,0:T(8,128)(2,1)S(1)} %collective-permute-done.2.refs_2_) | copy-start | bytes 786436
  15.6 1.0 %copy-start.6 = (bf16[2,64,1024]{2,1,0:T(8,128)(2,1)S(1)}, bf16[2,64,1024]{2,1,0:T(8,128)(2,1)}, u32[]{:S(2)}) copy-start(bf16[2,64,1024]{2,1,0:T(8,128)(2,1)} %copy-done.5) | copy-start | bytes 786436
  23.0 1.6 %collective-permute-start.3 = (bf16[2,64,1024]{2,1,0:T(8,128)(2,1)S(1)}, bf16[2,64,1024]{2,1,0:T(8,128)(2,1)S(1)}, u32[]{:S(2)}, u32[]{:S(2)}) collective-permute-start(bf16[2,64,1024]{2,1,0:T(8,128)(2,1)S(1)} %get-tuple-element.28), channel_id=1, source_target_pairs={{0,8},{8,0},{16,24},{24,16},{1,9},{9,1},{17,25},{25,17},{2,10},{10... | collective-permute-start | bytes 786440 | tf_op jit(solution)/shard_map/ppermute | solution.py:366
  24.7 5.6 %collective-permute-start.4 = (bf16[1,64,1024]{2,1,0:T(8,128)(2,1)S(1)}, bf16[1,64,1024]{2,1,0:T(8,128)(2,1)S(1)}, u32[]{:S(2)}, u32[]{:S(2)}) collective-permute-start(bf16[1,64,1024]{2,1,0:T(8,128)(2,1)S(1)} %slice.46), channel_id=1, source_target_pairs={{0,16},{8,24},{16,0},{24,8},{1,17},{9,25},{17,1},{25,9},{2,18},{10... | collective-permute-start | bytes 393224 | tf_op jit(solution)/shard_map/ppermute | solution.py:366
  25.1 0.9 %copy-start.7 = (bf16[2,64,1024]{2,1,0:T(8,128)(2,1)S(1)}, bf16[2,64,1024]{2,1,0:T(8,128)(2,1)}, u32[]{:S(2)}) copy-start(bf16[2,64,1024]{2,1,0:T(8,128)(2,1)} %copy-done.5) | copy-start | bytes 786436
  30.4 4.7 %collective-permute-start.5 = (bf16[32,1024]{1,0:T(8,128)(2,1)S(1)}, bf16[32,1024]{1,0:T(8,128)(2,1)S(1)}, u32[]{:S(2)}, u32[]{:S(2)}) collective-permute-start(bf16[32,1024]{1,0:T(8,128)(2,1)S(1)} %fusion.1), channel_id=1, source_target_pairs={{0,1},{1,0},{2,3},{3,2},{4,5},{5,4},{6,7},{7,6},{8,9},{9,8},{10,11... | collective-permute-start | bytes 196616 | tf_op jit(solution)/shard_map/ppermute | solution.py:366
  35.1 4.3 %collective-permute-start.6 = (bf16[32,1024]{1,0:T(8,128)(2,1)S(1)}, bf16[32,1024]{1,0:T(8,128)(2,1)S(1)}, u32[]{:S(2)}, u32[]{:S(2)}) collective-permute-start(bf16[32,1024]{1,0:T(8,128)(2,1)S(1)} %fusion), channel_id=1, source_target_pairs={{0,2},{1,3},{2,0},{3,1},{4,6},{5,7},{6,4},{7,5},{8,10},{9,11},{10,... | collective-permute-start | bytes 196616 | tf_op jit(solution)/shard_map/ppermute | solution.py:366
  39.5 5.3 %collective-permute-start.7 = (bf16[32,1024]{1,0:T(8,128)(2,1)S(1)}, bf16[32,1024]{1,0:T(8,128)(2,1)S(1)}, u32[]{:S(2)}, u32[]{:S(2)}) collective-permute-start(bf16[32,1024]{1,0:T(8,128)(2,1)S(1)} %add_convert_fusion.1), channel_id=1, source_target_pairs={{0,4},{1,5},{2,6},{3,7},{4,0},{5,1},{6,2},{7,3},{8,12},{9,13},{10,... | collective-permute-start | bytes 196616 | tf_op jit(solution)/shard_map/ppermute | solution.py:366
  44.8 4.4 %collective-permute-start.8 = (bf16[32,1024]{1,0:T(8,128)(2,1)S(1)}, bf16[32,1024]{1,0:T(8,128)(2,1)S(1)}, u32[]{:S(2)}, u32[]{:S(2)}) collective-permute-start(bf16[32,1024]{1,0:T(8,128)(2,1)S(1)} %add_convert_fusion), channel_id=1, source_target_pairs={{0,1},{1,0},{2,3},{3,2},{4,5},{5,4},{6,7},{7,6},{8,9},{9,8},{10,11... | collective-permute-start | bytes 196616 | tf_op jit(solution)/shard_map/ppermute | solution.py:366

commit v2 on v1

--- a/solution.py
+++ b/solution.py
@@ -167,83 +167,79 @@
     lax.fori_loop(0, count // together, step, 0)
 
 
-def place_pieces(place_ref, pieces, f_ref):
-    order = iter(slots(f_ref.shape[0]))
-    for piece in pieces:
-        for which in range(piece.shape[0]):
-            twice(f_ref.at[jnp.bitwise_xor(place_ref[0], next(order))], piece[which])
-
-
-def own_filter_kernel(rows_ref, filter_ref, grad_out_ref, gate_ref, conv_in_ref, terms_ref, y_ref, x_ref, z_ref):
-    width = y_ref.shape[2]
+def own_filter_kernel(rows_ref, filter_ref, last_ref, grad_out_ref, gate_ref, conv_in_ref, terms_ref, grad_y_ref, tail_ref,
+                      y_ref, x_ref, t_ref, z_ref):
+    width, taps, rows = y_ref.shape[2], terms_ref.shape[0], grad_y_ref.shape[0]
 
     def unit(which, lanes, slot):
-        y_hat = transform(rows_ref, y_ref.at[slot], gated(grad_out_ref[:, lanes], gate_ref[:, lanes]))
+        grad_y = gated(grad_out_ref[:, lanes], gate_ref[:, lanes])
+        grad_y_ref[:, lanes] = grad_y
+        y_hat = transform(rows_ref, y_ref.at[slot], grad_y)
         x_hat = transform(rows_ref, x_ref.at[slot], conv_in_ref[:, lanes])
+        tail_ref[:, lanes] = transform(last_ref, t_ref.at[slot], conv_in_ref[rows - taps:, lanes])
         terms_ref[:, lanes] = correlate(y_hat, x_hat, filter_ref, z_ref.at[slot])
 
     in_turn(terms_ref.shape[1] // width, width, unit)
 
 
-def own_input_kernel(place_ref, rows_ref, taps_ref, input_ref, grad_out_ref, gate_ref, *refs):
-    pieces, (head_ref, tail_ref, y_ref, f_ref, z_ref) = refs[:-5], refs[-5:]
+def own_input_kernel(place_ref, rows_ref, taps_ref, input_ref, grad_y_ref, *refs):
+    pieces, (head_ref, tail_ref, filt_ref, y_ref, f_ref, z_ref, sems) = refs[:-7], refs[-7:]
     channels, width = head_ref.shape[1], y_ref.shape[2]
-    place_pieces(place_ref, pieces, f_ref)
+    copies = []
+    for m, piece in enumerate(pieces):
+        owner = jnp.bitwise_xor(place_ref[0], m)
+        lanes = pl.ds(pl.multiple_of(owner * width, LANE), width)
+        copies.append(pltpu.make_async_copy(piece, filt_ref.at[:, lanes], sems.at[m]))
+        copies[-1].start()
+    for copy in copies:
+        copy.wait()
 
     def unit(which, lanes, slot):
-        y_hat = transform(rows_ref, y_ref.at[slot], gated(grad_out_ref[:, lanes], gate_ref[:, lanes]))
-        grad_in = correlate(y_hat, product(taps_ref[...], f_ref[which]), input_ref, z_ref.at[slot])
+        y_hat = transform(rows_ref, y_ref.at[slot], grad_y_ref[:, lanes])
+        f_hat = transform(taps_ref, f_ref.at[slot], filt_ref[:, lanes])
+        grad_in = correlate(y_hat, f_hat, input_ref, z_ref.at[slot])
         head_ref[:, lanes] = grad_in[:head_ref.shape[0]].astype(head_ref.dtype)
         tail_ref[:, lanes] = grad_in[head_ref.shape[0]:]
 
     in_turn(channels // width, width, unit)
 
 
-def halo_filter_kernel(place_ref, rows_ref, tail_ref, filter_ref, own_ref, conv_in_ref, halo_ref, after_ref,
-                       keep_ref, send_ref, y_ref, x_ref, z_ref, sum_ref):
+def halo_filter_kernel(place_ref, rows_ref, filter_ref, own_ref, x_hat_ref, halo_ref, after_ref,
+                       keep_ref, send_ref, y_ref, z_ref, sum_ref):
     del after_ref
-    taps, owners = own_ref.shape[0], y_ref.shape[0]
-    rows, width = conv_in_ref.shape[0], y_ref.shape[2]
+    owners, _, width = y_ref.shape
     for which in range(owners):
         lanes = pl.ds(which * width, width)
         y_hat = transform(rows_ref, y_ref.at[which], halo_ref[:, lanes])
-        x_hat = transform(tail_ref, x_ref.at[which], conv_in_ref[rows - taps:, lanes])
-        sum_ref[which] = own_ref[:, lanes] + correlate(y_hat, x_hat, filter_ref, z_ref.at[which])
+        sum_ref[which] = own_ref[:, lanes] + correlate(y_hat, x_hat_ref[:, lanes], filter_ref, z_ref.at[which])
     for pair in range(owners // 2):
         keep_ref[pair] = sum_ref[jnp.bitwise_xor(place_ref[0], 2 * pair)]
         send_ref[pair] = sum_ref[jnp.bitwise_xor(place_ref[0], 2 * pair + 1)].astype(send_ref.dtype)
 
 
-def halo_input_kernel(place_ref, rows_ref, taps_ref, input_ref, after_ref, halo_ref, head_ref, tail_ref, *refs):
-    pieces, (out_ref, passed_ref, y_ref, f_ref, z_ref) = refs[:-5], refs[-5:]
-    step = pl.program_id(0)
-    head = head_ref.shape[0]
-
-    @pl.when(step == 0)
-    def _():
-        place_pieces(place_ref, pieces, f_ref)
-        passed_ref[...] = after_ref[...]
-
-    y_hat = transform(rows_ref, y_ref, halo_ref[...])
-    value = correlate(y_hat, product(taps_ref[...], f_ref[step]), input_ref, z_ref)
-    out_ref[0:head, :] = head_ref[...]
-    out_ref[head:, :] = (tail_ref[...] + value).astype(out_ref.dtype)
+def halo_input_kernel(rows_ref, taps_ref, input_ref, after_ref, halo_ref, head_ref, tail_ref, filt_ref,
+                      out_ref, passed_ref, y_ref, f_ref, z_ref, last_ref, sems):
+    head, (owners, _, width) = head_ref.shape[0], y_ref.shape
+    taps = halo_ref.shape[0]
+    copies = [pltpu.make_async_copy(head_ref, out_ref.at[pl.ds(0, head), :], sems.at[owners])]
+    copies[0].start()
+    passed_ref[...] = after_ref[...]
+    for which in range(owners):
+        lanes = pl.ds(which * width, width)
+        y_hat = transform(rows_ref, y_ref.at[which], halo_ref[:, lanes])
+        f_hat = transform(taps_ref, f_ref.at[which], filt_ref[:, lanes])
+        value = tail_ref[:, lanes] + correlate(y_hat, f_hat, input_ref, z_ref.at[which])
+        last_ref[:, lanes] = value.astype(last_ref.dtype)
+        copies.append(pltpu.make_async_copy(
+            last_ref.at[:, lanes], out_ref.at[pl.ds(head, taps), lanes], sems.at[which]
+        ))
+        copies[-1].start()
+    for copy in copies:
+        copy.wait()
 
 
 def scalars():
     return pl.BlockSpec(memory_space=pltpu.SMEM)
-
-
-def whole(array):
-    return pl.BlockSpec(array.shape, lambda step: (0,) * len(array.shape))
-
-
-def tiled(rows, tile, at=0):
-    return pl.BlockSpec((rows, tile), lambda step: (at, step))
-
-
-def scratch(rows, tile):
-    return pltpu.VMEM((rows, tile), jnp.bfloat16)
 
 
 def shaped(*shape, dtype=jnp.bfloat16):
@@ -276,16 +272,27 @@
     return [pl.BlockSpec(memory_space=pltpu.VMEM)] * count
 
 
+def outside(count):
+    return [pl.BlockSpec(memory_space=pltpu.HBM)] * count
+
+
+def held(*shape):
+    return pltpu.VMEM(shape, jnp.bfloat16)
+
+
 def own_filter(bases, grad_out, gate, conv_in, taps, width):
     rows, channels = grad_out.shape
     return pl.pallas_call(
         own_filter_kernel,
-        in_specs=inside(5),
-        out_specs=inside(1)[0],
-        out_shape=shaped(taps, channels, dtype=jnp.float32),
+        in_specs=inside(6),
+        out_specs=inside(3),
+        out_shape=[
+            shaped(taps, channels, dtype=jnp.float32), shaped(rows, channels),
+            shaped(2 * taps, channels, dtype=jnp.float32),
+        ],
         scratch_shapes=[
-            pltpu.VMEM((2, 2 * rows, width), jnp.bfloat16), pltpu.VMEM((2, 2 * rows, width), jnp.bfloat16),
-            pltpu.VMEM((2, 2, 2 * rows, width), jnp.bfloat16),
+            held(2, 2 * rows, width), held(2, 2 * rows, width), held(2, 2 * taps, width),
+            held(2, 2, 2 * rows, width),
         ],
         compiler_params=params(),
         cost_estimate=cost(20 * rows * rows * channels, (6 * rows + 4 * taps) * channels),
@@ -293,85 +300,65 @@
     )(*bases, grad_out, gate, conv_in)
 
 
-def own_input(place, bases, grad_out, gate, pieces, owners):
-    rows, channels = grad_out.shape
-    taps, width = pieces[0].shape[1:]
+def own_input(place, bases, grad_y, pieces):
+    rows, channels = grad_y.shape
+    taps, width = pieces[0].shape
     return pl.pallas_call(
         own_input_kernel,
-        in_specs=[scalars(), *inside(5 + len(pieces))],
-        out_specs=inside(2),
-        out_shape=[shaped(rows - taps, channels), shaped(taps, channels, dtype=jnp.float32)],
+        in_specs=[scalars(), *inside(4), *outside(len(pieces))],
+        out_specs=inside(3),
+        out_shape=[
+            shaped(rows - taps, channels), shaped(taps, channels, dtype=jnp.float32), shaped(taps, channels)
+        ],
         scratch_shapes=[
-            pltpu.VMEM((2, 2 * rows, width), jnp.bfloat16), pltpu.VMEM((owners, 2 * taps, width), jnp.bfloat16),
-            pltpu.VMEM((2, 2, 2 * rows, width), jnp.bfloat16),
+            held(2, 2 * rows, width), held(2, 2 * taps, width), held(2, 2, 2 * rows, width),
+            pltpu.SemaphoreType.DMA((len(pieces),)),
         ],
         compiler_params=params(),
         cost_estimate=cost(30 * rows * rows * channels, (6 * rows + 6 * taps) * channels),
         name="own_input",
-    )(place, *bases, grad_out, gate, *pieces)
-
-
-def halo_filter(place, bases, own, conv_in, halo, after, owners):
-    rows, channels = conv_in.shape
-    taps = halo.shape[0]
+    )(place, *bases, grad_y, *pieces)
+
+
+def halo_filter(place, bases, own, x_hat, halo, after, owners):
+    taps, channels = halo.shape
     width = channels // owners
-    twice_held = pltpu.VMEM((owners, 2 * taps, width), jnp.bfloat16)
     return pl.pallas_call(
         halo_filter_kernel,
-        in_specs=[scalars(), *inside(7)],
+        in_specs=[scalars(), *inside(6)],
         out_specs=inside(2),
         out_shape=[shaped(owners // 2, taps, width, dtype=jnp.float32), shaped(owners // 2, taps, width)],
         scratch_shapes=[
-            twice_held, twice_held, pltpu.VMEM((owners, 2, 2 * taps, width), jnp.bfloat16),
+            held(owners, 2 * taps, width), held(owners, 2, 2 * taps, width),
             pltpu.VMEM((owners, taps, width), jnp.float32),
         ],
         compiler_params=params(),
-        cost_estimate=cost(28 * taps * taps * channels, 10 * taps * channels),
+        cost_estimate=cost(20 * taps * taps * channels, 10 * taps * channels),
         name="halo_filter",
-    )(place, *bases, own, conv_in, halo, after)
-
-
-def halo_input(place, bases, after, halo, head, tail, pieces, owners):
+    )(place, *bases, own, x_hat, halo, after)
+
+
+def halo_input(bases, after, halo, head, tail, filt, owners):
     taps, channels = halo.shape
     width = channels // owners
     rows = head.shape[0] + taps
     return pl.pallas_call(
         halo_input_kernel,
-        grid=(owners,),
-        in_specs=[
-            scalars(), *[whole(basis) for basis in bases], *inside(1), tiled(taps, width), tiled(rows - taps, width),
-            tiled(taps, width), *[whole(piece) for piece in pieces],
-        ],
-        out_specs=[tiled(rows, width), *inside(1)],
+        in_specs=inside(8),
+        out_specs=[pl.BlockSpec(memory_space=pl.ANY), *inside(1)],
         out_shape=[shaped(rows, channels), shaped(*after.shape, dtype=after.dtype)],
         scratch_shapes=[
-            scratch(2 * taps, width), pltpu.VMEM((owners, 2 * taps, width), jnp.bfloat16),
-            pltpu.VMEM((2, 2 * taps, width), jnp.bfloat16),
+            held(owners, 2 * taps, width), held(owners, 2 * taps, width), held(owners, 2, 2 * taps, width),
+            held(taps, channels), pltpu.SemaphoreType.DMA((owners + 1,)),
         ],
         compiler_params=params(),
         cost_estimate=cost(28 * taps * taps * channels, 10 * taps * channels),
         name="halo_input",
-    )(place, *bases, after, halo, head, tail, *pieces)
-
-
-def slots(owners):
-    order, bit = [0], owners // 2
-    while bit:
-        order += [m + bit for m in order]
-        bit //= 2
-    return order
+    )(*bases, after, halo, head, tail, filt)
 
 
 def swap(value, axis, bit):
     return lax.ppermute(value, axis, [(source, source ^ bit) for source in range(lax.axis_size(axis))])
-
-
-def gather(value, axis):
-    held, bit = [value[None]], lax.axis_size(axis) // 2
-    while bit:
-        held.append(swap(jnp.concatenate(held) if len(held) > 1 else held[0], axis, bit))
-        bit //= 2
-    return held
 
 
 def narrow(value):
@@ -392,13 +379,14 @@
 
     following = narrow(widen(grad_out[:taps]) * widen(gate[:taps]))
     halo = lax.ppermute(following, "ctx", [(source, source - 1) for source in range(1, ctx)])
-    pieces = gather(filt.T, "dp")
+    mine = filt.T
+    pieces = [mine] + [swap(mine, "dp", m) for m in range(1, dp)]
 
     bases = make_basis(doc_end, first_row, rows, taps)
     halo_rows, halo_tail, halo_taps, halo_inverse_input, halo_inverse_filter = bases[4:]
-    own = own_filter((bases[0], bases[3]), grad_out, gate, conv_in, taps, channels // dp)
-    head, tail = own_input(place, bases[:3], grad_out, gate, pieces, dp)
-    keep, send = halo_filter(place, (halo_rows, halo_tail, halo_inverse_filter), own, conv_in, halo, tail, dp)
+    own, grad_y, x_hat = own_filter((bases[0], bases[3], halo_tail), grad_out, gate, conv_in, taps, channels // dp)
+    head, tail, whole_filter = own_input(place, bases[:3], grad_y, pieces)
+    keep, send = halo_filter(place, (halo_rows, halo_inverse_filter), own, x_hat, halo, tail, dp)
 
     arrived, bit = swap(send, "dp", 1), 2
     while bit < dp:
@@ -406,7 +394,7 @@
         keep, arrived = total[0::2], swap(narrow(total[1::2]), "dp", bit)
         bit *= 2
     grad_in, keep = halo_input(
-        place, (halo_rows, halo_taps, halo_inverse_input), keep, halo, head, tail, pieces, dp
+        (halo_rows, halo_taps, halo_inverse_input), keep, halo, head, tail, whole_filter, dp
     )
     total = (keep + widen(arrived))[0]
     half = taps // 2

time: 50.3 us -> 49.5 us (0.984)
  starting transfers between devices: 14.3 us -> 16.2 us
  local copies, waits for them, and re-layouts: 5.72 us -> 4.36 us
  Pallas kernels: 12.5 us -> 11.5 us
    ppermute x8 -> x9, starting transfers between devices: 13 us -> 14.9 us  [swap(): lax.ppermute(value, axis, [(source, source ^ bit) for source in range(lax...]
    unnamed x18 -> x10, local copies, waits for them, and re-layouts: 5.68 us -> 4.33 us
    pallas_call x4, Pallas kernels: 11.2 us -> 10.1 us  [the longest x1 3.09 us: own_input(): pl.pallas_call(own_input_kernel, in_specs=[scalars(), *inside(4), *outsid...]
    ppermute x1, waiting for transfers between devices: 1.59 us -> 0.65 us  [body(): lax.ppermute(following, 'ctx', [(source, source - 1) for source in range(...]
    ppermute x8 -> x9, waiting for transfers between devices: 12 us -> 12.9 us  [swap(): lax.ppermute(value, axis, [(source, source ^ bit) for source in range(lax...]
  transfers between devices with their start and end apart: 9 -> 10, of which waited for: 8 -> 7; matrix products, arithmetic and copies ran while one was open for 4% -> 0% of each run, Pallas kernels for 21% -> 20%
where the time goes in v2:
time: 49.5 us; the launch traced here: 49.3 us
  starting transfers between devices  16.2 us (33%)
  waiting for transfers between devices  13.5 us (27%)
  Pallas kernels  11.5 us (23%)
  local copies, waits for them, and re-layouts  4.36 us (9%)
  other arithmetic  3 us (6%)
  between operations  0.78 us (2%)
    ppermute x9, starting transfers between devices, swap(): lax.ppermute(value, axis, [(source, source ^ bit) for source in range(lax...  14.9 us
    ppermute x9, waiting for transfers between devices, swap(): lax.ppermute(value, axis, [(source, source ^ bit) for source in range(lax...  12.9 us
    unnamed x10, local copies, waits for them, and re-layouts  4.33 us
    pallas_call x1, Pallas kernels, own_input(): pl.pallas_call(own_input_kernel, in_specs=[scalars(), *inside(4), *outsid...  3.09 us
    pallas_call x1, Pallas kernels, own_filter(): pl.pallas_call(own_filter_kernel, in_specs=inside(6), out_specs=inside(3)...  3.01 us
    pallas_call x1, Pallas kernels, halo_input(): pl.pallas_call(halo_input_kernel, in_specs=inside(8), out_specs=[pl.Block...  2.42 us
    convert_element_type x5, other arithmetic, narrow(): return value.astype(jnp.bfloat16)  2.19 us
    pallas_call x1, Pallas kernels, halo_filter(): pl.pallas_call(halo_filter_kernel, in_specs=[scalars(), *inside(6)], out_...  1.55 us
  transfers between devices with their start and end apart: 10, of which 7 were waited for; matrix products, arithmetic and copies ran while one was open for 0% of the time, Pallas kernels for 20%

profile of v2, /device:TPU:0, one launch (start us, length us, event | category | flops | bytes accessed | tf_op | source)
XLA Modules:
  0.0 49.3 jit_solution(4202175200967536393)
XLA Ops:
  0.6 2.1 %multiply_convert_fusion = bf16[64,4096]{1,0:T(8,128)(2,1)} fusion(bf16[128,4096]{1,0:T(8,128)(2,1)} %gate_ref.1, bf16[128,4096]{1,0:T(8,128)(2,1)} %grad_out_ref.1), kind=kLoop, calls=%fused_computation | loop fusion | flops 1048576 | bytes 1572864 | tf_op jit(solution)/shard_map/convert_element_type | solution.py:365
  2.7 1.3 %collective-permute-start = (bf16[64,4096]{1,0:T(8,128)(2,1)}, bf16[64,4096]{1,0:T(8,128)(2,1)S(1)}, u32[]{:S(2)}, u32[]{:S(2)}) collective-permute-start(bf16[64,4096]{1,0:T(8,128)(2,1)} %multiply_convert_fusion), channel_id=1, source_target_pairs={{1,0},{2,1},{3,2},{4,3},{5,4},{6,5},{7,6},{9,8},{10,9},{11,10},{12... | collective-permute-start | bytes 1572872 | tf_op jit(solution)/shard_map/ppermute | solution.py:381
  4.6 2.6 %collective-permute-start.2 = (bf16[64,1024]{1,0:T(8,128)(2,1)}, bf16[64,1024]{1,0:T(8,128)(2,1)S(1)}, u32[]{:S(2)}, u32[]{:S(2)}) collective-permute-start(bf16[64,1024]{1,0:T(8,128)(2,1)} %bitcast.12), channel_id=1, source_target_pairs={{0,16},{8,24},{16,0},{24,8},{1,17},{9,25},{17,1},{25,9},{2,18},{10... | collective-permute-start | bytes 393224 | tf_op jit(solution)/shard_map/ppermute | solution.py:361
  7.2 0.7 %copy-done.4 = s32[128]{0:T(128)S(1)} copy-done((s32[128]{0:T(128)S(1)}, s32[128]{0:T(128)}, u32[]{:S(2)}) %copy-start.4) | copy-done | bytes 536
  7.8 1.4 %basis.1 = (bf16[256,256]{1,0:T(8,128)(2,1)S(1)}, bf16[256,128]{1,0:T(8,128)(2,1)S(1)}, bf16[256,256]{1,0:T(8,128)(2,1)S(1)}, bf16[128,256]{1,0:T(8,128)(2,1)S(1...) custom-call(s32[128]{0:T(128)S(1)} %copy-done.4, ...), custom_call_target="tpu_custom_call" | custom-call | flops 10000000 | bytes 1000000 | tf_op jit(solution)/shard_map/basis/pallas_call | solution.py:260
  9.3 1.2 %copy-done = bf16[128,4096]{1,0:T(8,128)(2,1)S(1)} copy-done((bf16[128,4096]{1,0:T(8,128)(2,1)S(1)}, bf16[128,4096]{1,0:T(8,128)(2,1)}, u32[]{:S(2)}) %copy-start) | copy-done | bytes 1048600
  10.5 1.2 %copy-done.1 = bf16[128,4096]{1,0:T(8,128)(2,1)S(1)} copy-done((bf16[128,4096]{1,0:T(8,128)(2,1)S(1)}, bf16[128,4096]{1,0:T(8,128)(2,1)}, u32[]{:S(2)}) %copy-start.1) | copy-done | bytes 1048600
  11.7 1.2 %copy-done.2 = bf16[128,4096]{1,0:T(8,128)(2,1)S(1)} copy-done((bf16[128,4096]{1,0:T(8,128)(2,1)S(1)}, bf16[128,4096]{1,0:T(8,128)(2,1)}, u32[]{:S(2)}) %copy-start.2) | copy-done | bytes 1048600
  12.9 3.0 %own_filter.1 = (f32[64,4096]{1,0:T(8,128)S(1)}, bf16[128,4096]{1,0:T(8,128)(2,1)S(1)}, f32[128,4096]{1,0:T(8,128)S(1)}) custom-call(bf16[256,256]{1,0:T(8,128)(2,1)S(1)} %get-tuple-element.25.rows_ref, bf16[128,256]{1,0:T(8,128)(2,1)S(1)} %get-tuple-element.26.filter_ref, bf16[128,128]{1,0:T(8,128)(2,1)S(1)} %get-tuple-element.27.last_ref, ...), custom_call_target="tpu_custom_call" | custom-call | flops 1342177280 | bytes 4194304 | tf_op jit(solution)/shard_map/own_filter/pallas_call | solution.py:285
  16.0 3.1 %own_input.1 = (bf16[64,4096]{1,0:T(8,128)(2,1)S(1)}, f32[64,4096]{1,0:T(8,128)S(1)}, bf16[64,4096]{1,0:T(8,128)(2,1)S(1)}) custom-call(s32[1]{0:T(128)} %bitcast.1.place_ref, bf16[256,256]{1,0:T(8,128)(2,1)S(1)} %get-tuple-element.25.rows_ref, bf16[256,128]{1,0:T(8,128)(2,1)S(1)} %get-tuple-element.30.taps_ref, ...), custom_call_target="tpu_custom_call" | custom-call | flops 2013265920 | bytes 4718592 | tf_op jit(solution)/shard_map/own_input/pallas_call | solution.py:306
  19.7 1.5 %halo_filter.1 = (f32[2,64,1024]{2,1,0:T(8,128)S(1)}, bf16[2,64,1024]{2,1,0:T(8,128)(2,1)S(1)}) custom-call(s32[1]{0:T(128)} %bitcast.1.place_ref, bf16[128,128]{1,0:T(8,128)(2,1)S(1)} %get-tuple-element.21.rows_ref, bf16[128,128]{1,0:T(8,128)(2,1)S(1)} %get-tuple-element.24.filter_ref, f32[64,4096]{1,0:T(8,128)S(1)} %get-tuple-element.28.own_ref, ...), custom_call_target="tpu_custom_call" | custom-call | flops 335544320 | bytes 2621440 | tf_op jit(solution)/shard_map/halo_filter/pallas_call | solution.py:326
  21.4 1.5 %collective-permute-done.4 = bf16[2,64,1024]{2,1,0:T(8,128)(2,1)S(1)} collective-permute-done((bf16[2,64,1024]{2,1,0:T(8,128)(2,1)S(1)}, bf16[2,64,1024]{2,1,0:T(8,128)(2,1)S(1)}, u32[]{:S(2)}, u32[]{:S(2)}) %collective-permute-start.4) | collective-permute-done | bytes 262176 | tf_op jit(solution)/shard_map/ppermute | solution.py:361
  23.0 1.8 %collective-permute-start.5 = (bf16[1,64,1024]{2,1,0:T(8,128)(2,1)S(1)}, bf16[1,64,1024]{2,1,0:T(8,128)(2,1)S(1)}, u32[]{:S(2)}, u32[]{:S(2)}) collective-permute-start(bf16[1,64,1024]{2,1,0:T(8,128)(2,1)S(1)} %slice.46), channel_id=1, source_target_pairs={{0,16},{8,24},{16,0},{24,8},{1,17},{9,25},{17,1},{25,9},{2,18},{10... | collective-permute-start | bytes 393224 | tf_op jit(solution)/shard_map/ppermute | solution.py:361
  24.8 2.4 %halo_input.1 = (bf16[128,4096]{1,0:T(8,128)(2,1)}, f32[1,64,1024]{2,1,0:T(8,128)S(1)}) custom-call(bf16[128,128]{1,0:T(8,128)(2,1)S(1)} %get-tuple-element.21.rows_ref, bf16[128,128]{1,0:T(8,128)(2,1)S(1)} %get-tuple-element.22.taps_ref, bf16[128,128]{1,0:T(8,128)(2,1)S(1)} %get-tuple-element.23.input_ref, f32[1,64,1024]{2,1,0:T(8,128)S(1)} %slice.31.after_ref, ...), custom_call_target="tpu_custom_call" | custom-call | flops 469762048 | bytes 2621440 | tf_op jit(solution)/shard_map/halo_input/pallas_call | solution.py:345
  27.2 1.4 %collective-permute-done.5 = bf16[1,64,1024]{2,1,0:T(8,128)(2,1)S(1)} collective-permute-done((bf16[1,64,1024]{2,1,0:T(8,128)(2,1)S(1)}, bf16[1,64,1024]{2,1,0:T(8,128)(2,1)S(1)}, u32[]{:S(2)}, u32[]{:S(2)}) %collective-permute-start.5) | collective-permute-done | bytes 131104 | tf_op jit(solution)/shard_map/ppermute | solution.py:361
  28.6 2.7 %collective-permute-start.6 = (bf16[32,1024]{1,0:T(8,128)(2,1)S(1)}, bf16[32,1024]{1,0:T(8,128)(2,1)S(1)}, u32[]{:S(2)}, u32[]{:S(2)}) collective-permute-start(bf16[32,1024]{1,0:T(8,128)(2,1)S(1)} %fusion.1), channel_id=1, source_target_pairs={{0,1},{1,0},{2,3},{3,2},{4,5},{5,4},{6,7},{7,6},{8,9},{9,8},{10,11... | collective-permute-start | bytes 196616 | tf_op jit(solution)/shard_map/ppermute | solution.py:361
  31.3 2.2 %collective-permute-done.6 = bf16[32,1024]{1,0:T(8,128)(2,1)S(1)} collective-permute-done((bf16[32,1024]{1,0:T(8,128)(2,1)S(1)}, bf16[32,1024]{1,0:T(8,128)(2,1)S(1)}, u32[]{:S(2)}, u32[]{:S(2)}) %collective-permute-start.6) | collective-permute-done | bytes 65568 | tf_op jit(solution)/shard_map/ppermute | solution.py:361
  33.6 2.8 %collective-permute-start.7 = (bf16[32,1024]{1,0:T(8,128)(2,1)S(1)}, bf16[32,1024]{1,0:T(8,128)(2,1)S(1)}, u32[]{:S(2)}, u32[]{:S(2)}) collective-permute-start(bf16[32,1024]{1,0:T(8,128)(2,1)S(1)} %fusion), channel_id=1, source_target_pairs={{0,2},{1,3},{2,0},{3,1},{4,6},{5,7},{6,4},{7,5},{8,10},{9,11},{10,... | collective-permute-start | bytes 196616 | tf_op jit(solution)/shard_map/ppermute | solution.py:361
  36.4 2.2 %collective-permute-done.7 = bf16[32,1024]{1,0:T(8,128)(2,1)S(1)} collective-permute-done((bf16[32,1024]{1,0:T(8,128)(2,1)S(1)}, bf16[32,1024]{1,0:T(8,128)(2,1)S(1)}, u32[]{:S(2)}, u32[]{:S(2)}) %collective-permute-start.7) | collective-permute-done | bytes 65568 | tf_op jit(solution)/shard_map/ppermute | solution.py:361
  38.7 3.3 %collective-permute-start.8 = (bf16[32,1024]{1,0:T(8,128)(2,1)S(1)}, bf16[32,1024]{1,0:T(8,128)(2,1)S(1)}, u32[]{:S(2)}, u32[]{:S(2)}) collective-permute-start(bf16[32,1024]{1,0:T(8,128)(2,1)S(1)} %add_convert_fusion.1), channel_id=1, source_target_pairs={{0,4},{1,5},{2,6},{3,7},{4,0},{5,1},{6,2},{7,3},{8,12},{9,13},{10,... | collective-permute-start | bytes 196616 | tf_op jit(solution)/shard_map/ppermute | solution.py:361
  42.0 2.2 %collective-permute-done.8 = bf16[32,1024]{1,0:T(8,128)(2,1)S(1)} collective-permute-done((bf16[32,1024]{1,0:T(8,128)(2,1)S(1)}, bf16[32,1024]{1,0:T(8,128)(2,1)S(1)}, u32[]{:S(2)}, u32[]{:S(2)}) %collective-permute-start.8) | collective-permute-done | bytes 65568 | tf_op jit(solution)/shard_map/ppermute | solution.py:361
  44.2 1.1 %collective-permute-start.9 = (bf16[32,1024]{1,0:T(8,128)(2,1)S(1)}, bf16[32,1024]{1,0:T(8,128)(2,1)S(1)}, u32[]{:S(2)}, u32[]{:S(2)}) collective-permute-start(bf16[32,1024]{1,0:T(8,128)(2,1)S(1)} %add_convert_fusion), channel_id=1, source_target_pairs={{0,1},{1,0},{2,3},{3,2},{4,5},{5,4},{6,7},{7,6},{8,9},{9,8},{10,11... | collective-permute-start | bytes 196616 | tf_op jit(solution)/shard_map/ppermute | solution.py:361
  45.4 3.2 %collective-permute-done.9 = bf16[32,1024]{1,0:T(8,128)(2,1)S(1)} collective-permute-done((bf16[32,1024]{1,0:T(8,128)(2,1)S(1)}, bf16[32,1024]{1,0:T(8,128)(2,1)S(1)}, u32[]{:S(2)}, u32[]{:S(2)}) %collective-permute-start.9) | collective-permute-done | bytes 65568 | tf_op jit(solution)/shard_map/ppermute | solution.py:361
  48.6 0.7 %convert_bitcast_fusion = f32[1024,64]{0,1:T(8,128)} fusion(bf16[32,1024]{1,0:T(8,128)(2,1)S(1)} %get-tuple-element.41, bf16[32,1024]{1,0:T(8,128)(2,1)S(1)} %get-tuple-element.40), kind=kLoop, calls=%fused_computation.3 | loop fusion | flops 262144 | bytes 393216 | tf_op jit(solution)/shard_map/transpose | solution.py:412
  (22 shorter events, 1.5 us)
Async XLA Ops:
  2.7 17.0 %collective-permute-start = (bf16[64,4096]{1,0:T(8,128)(2,1)}, bf16[64,4096]{1,0:T(8,128)(2,1)S(1)}, u32[]{:S(2)}, u32[]{:S(2)}) collective-permute-start(bf16[64,4096]{1,0:T(8,128)(2,1)} %multiply_convert_fusion), channel_id=1, source_target_pairs={{1,0},{2,1},{3,2},{4,3},{5,4},{6,5},{7,6},{9,8},{10,9},{11,10},{12... | collective-permute-start | bytes 1572872 | tf_op jit(solution)/shard_map/ppermute | solution.py:381
  4.0 11.9 %collective-permute-start.1 = (bf16[64,1024]{1,0:T(8,128)(2,1)}, bf16[64,1024]{1,0:T(8,128)(2,1)S(1)}, u32[]{:S(2)}, u32[]{:S(2)}) collective-permute-start(bf16[64,1024]{1,0:T(8,128)(2,1)} %bitcast.11), channel_id=1, source_target_pairs={{0,8},{8,0},{16,24},{24,16},{1,9},{9,1},{17,25},{25,17},{2,10},{10... | collective-permute-start | bytes 393224 | tf_op jit(solution)/shard_map/ppermute | solution.py:361
  4.6 11.4 %collective-permute-start.2 = (bf16[64,1024]{1,0:T(8,128)(2,1)}, bf16[64,1024]{1,0:T(8,128)(2,1)S(1)}, u32[]{:S(2)}, u32[]{:S(2)}) collective-permute-start(bf16[64,1024]{1,0:T(8,128)(2,1)} %bitcast.12), channel_id=1, source_target_pairs={{0,16},{8,24},{16,0},{24,8},{1,17},{9,25},{17,1},{25,9},{2,18},{10... | collective-permute-start | bytes 393224 | tf_op jit(solution)/shard_map/ppermute | solution.py:361
  7.1 8.9 %collective-permute-start.3 = (bf16[64,1024]{1,0:T(8,128)(2,1)}, bf16[64,1024]{1,0:T(8,128)(2,1)S(1)}, u32[]{:S(2)}, u32[]{:S(2)}) collective-permute-start(bf16[64,1024]{1,0:T(8,128)(2,1)} %bitcast.13), channel_id=1, source_target_pairs={{0,24},{8,16},{16,8},{24,0},{1,25},{9,17},{17,9},{25,1},{2,26},{10... | collective-permute-start | bytes 393224 | tf_op jit(solution)/shard_map/ppermute | solution.py:361
  7.2 0.7 %copy-start.4 = (s32[128]{0:T(128)S(1)}, s32[128]{0:T(128)}, u32[]{:S(2)}) copy-start(s32[128]{0:T(128)} %end_ref.1) | copy-start | bytes 1540
  9.2 1.2 %copy-start = (bf16[128,4096]{1,0:T(8,128)(2,1)S(1)}, bf16[128,4096]{1,0:T(8,128)(2,1)}, u32[]{:S(2)}) copy-start(bf16[128,4096]{1,0:T(8,128)(2,1)} %grad_out_ref.1) | copy-start | bytes 3145732
  10.5 1.2 %copy-start.1 = (bf16[128,4096]{1,0:T(8,128)(2,1)S(1)}, bf16[128,4096]{1,0:T(8,128)(2,1)}, u32[]{:S(2)}) copy-start(bf16[128,4096]{1,0:T(8,128)(2,1)} %gate_ref.1) | copy-start | bytes 3145732
  11.7 1.2 %copy-start.2 = (bf16[128,4096]{1,0:T(8,128)(2,1)S(1)}, bf16[128,4096]{1,0:T(8,128)(2,1)}, u32[]{:S(2)}) copy-start(bf16[128,4096]{1,0:T(8,128)(2,1)} %conv_in_ref.1) | copy-start | bytes 3145732
  12.9 3.1 %copy-start.3 = (bf16[1024,64]{0,1:T(8,128)(2,1)S(1)}, bf16[1024,64]{0,1:T(8,128)(2,1)}, u32[]{:S(2)}) copy-start(bf16[1024,64]{0,1:T(8,128)(2,1)} %param.8) | copy-start | bytes 393220
  21.3 1.6 %collective-permute-start.4 = (bf16[2,64,1024]{2,1,0:T(8,128)(2,1)S(1)}, bf16[2,64,1024]{2,1,0:T(8,128)(2,1)S(1)}, u32[]{:S(2)}, u32[]{:S(2)}) collective-permute-start(bf16[2,64,1024]{2,1,0:T(8,128)(2,1)S(1)} %get-tuple-element.35), channel_id=1, source_target_pairs={{0,8},{8,0},{16,24},{24,16},{1,9},{9,1},{17,25},{25,17},{2,10},{10... | collective-permute-start | bytes 786440 | tf_op jit(solution)/shard_map/ppermute | solution.py:361
  23.0 5.6 %collective-permute-start.5 = (bf16[1,64,1024]{2,1,0:T(8,128)(2,1)S(1)}, bf16[1,64,1024]{2,1,0:T(8,128)(2,1)S(1)}, u32[]{:S(2)}, u32[]{:S(2)}) collective-permute-start(bf16[1,64,1024]{2,1,0:T(8,128)(2,1)S(1)} %slice.46), channel_id=1, source_target_pairs={{0,16},{8,24},{16,0},{24,8},{1,17},{9,25},{17,1},{25,9},{2,18},{10... | collective-permute-start | bytes 393224 | tf_op jit(solution)/shard_map/ppermute | solution.py:361
  28.6 4.9 %collective-permute-start.6 = (bf16[32,1024]{1,0:T(8,128)(2,1)S(1)}, bf16[32,1024]{1,0:T(8,128)(2,1)S(1)}, u32[]{:S(2)}, u32[]{:S(2)}) collective-permute-start(bf16[32,1024]{1,0:T(8,128)(2,1)S(1)} %fusion.1), channel_id=1, source_target_pairs={{0,1},{1,0},{2,3},{3,2},{4,5},{5,4},{6,7},{7,6},{8,9},{9,8},{10,11... | collective-permute-start | bytes 196616 | tf_op jit(solution)/shard_map/ppermute | solution.py:361
  33.6 5.1 %collective-permute-start.7 = (bf16[32,1024]{1,0:T(8,128)(2,1)S(1)}, bf16[32,1024]{1,0:T(8,128)(2,1)S(1)}, u32[]{:S(2)}, u32[]{:S(2)}) collective-permute-start(bf16[32,1024]{1,0:T(8,128)(2,1)S(1)} %fusion), channel_id=1, source_target_pairs={{0,2},{1,3},{2,0},{3,1},{4,6},{5,7},{6,4},{7,5},{8,10},{9,11},{10,... | collective-permute-start | bytes 196616 | tf_op jit(solution)/shard_map/ppermute | solution.py:361
  38.7 5.5 %collective-permute-start.8 = (bf16[32,1024]{1,0:T(8,128)(2,1)S(1)}, bf16[32,1024]{1,0:T(8,128)(2,1)S(1)}, u32[]{:S(2)}, u32[]{:S(2)}) collective-permute-start(bf16[32,1024]{1,0:T(8,128)(2,1)S(1)} %add_convert_fusion.1), channel_id=1, source_target_pairs={{0,4},{1,5},{2,6},{3,7},{4,0},{5,1},{6,2},{7,3},{8,12},{9,13},{10,... | collective-permute-start | bytes 196616 | tf_op jit(solution)/shard_map/ppermute | solution.py:361
  44.2 4.3 %collective-permute-start.9 = (bf16[32,1024]{1,0:T(8,128)(2,1)S(1)}, bf16[32,1024]{1,0:T(8,128)(2,1)S(1)}, u32[]{:S(2)}, u32[]{:S(2)}) collective-permute-start(bf16[32,1024]{1,0:T(8,128)(2,1)S(1)} %add_convert_fusion), channel_id=1, source_target_pairs={{0,1},{1,0},{2,3},{3,2},{4,5},{5,4},{6,7},{7,6},{8,9},{9,8},{10,11... | collective-permute-start | bytes 196616 | tf_op jit(solution)/shard_map/ppermute | solution.py:361

commit v3 on v2

--- a/solution.py
+++ b/solution.py
@@ -247,7 +247,7 @@
 
 
 def params():
-    return pltpu.CompilerParams(vmem_limit_bytes=24 * 1024 * 1024)
+    return pltpu.CompilerParams(vmem_limit_bytes=14 * 1024 * 1024)
 
 
 def cost(flops, moved):
@@ -263,7 +263,7 @@
         out_shape=own + halo,
         scratch_shapes=[pltpu.VMEM((5, rows, LANE), jnp.int32), pltpu.VMEM((5, 8, rows), jnp.int32)],
         compiler_params=params(),
-        cost_estimate=cost(10000000, 1000000),
+        cost_estimate=cost(1500000000, 1000000),
         name="basis",
     )(doc_end, first)
 

time: 49.5 us -> 48.5 us (0.980)
  local copies, waits for them, and re-layouts: 4.36 us -> 1.24 us
  waiting for transfers between devices: 13.5 us -> 16.3 us
  starting transfers between devices: 16.2 us -> 15.6 us
    unnamed x10, local copies, waits for them, and re-layouts: 4.33 us -> 1.2 us
    ppermute x1, waiting for transfers between devices: 0.65 us -> 2.64 us  [body(): lax.ppermute(following, 'ctx', [(source, source - 1) for source in range(...]
    ppermute x9, waiting for transfers between devices: 12.9 us -> 13.7 us  [swap(): lax.ppermute(value, axis, [(source, source ^ bit) for source in range(lax...]
    ppermute x9, starting transfers between devices: 14.9 us -> 14.3 us  [swap(): lax.ppermute(value, axis, [(source, source ^ bit) for source in range(lax...]
  transfers between devices with their start and end apart: 10 -> 10, of which waited for: 7 -> 8; matrix products, arithmetic and copies ran while one was open for 0% -> 0% of each run, Pallas kernels for 20% -> 20%
where the time goes in v3:
time: 48.5 us; the launch traced here: 48.4 us
  waiting for transfers between devices  16.3 us (34%)
  starting transfers between devices  15.6 us (32%)
  Pallas kernels  11.4 us (24%)
  other arithmetic  3 us (6%)
  local copies, waits for them, and re-layouts  1.24 us (3%)
  between operations  0.76 us (2%)
    ppermute x9, starting transfers between devices, swap(): lax.ppermute(value, axis, [(source, source ^ bit) for source in range(lax...  14.3 us
    ppermute x9, waiting for transfers between devices, swap(): lax.ppermute(value, axis, [(source, source ^ bit) for source in range(lax...  13.7 us
    pallas_call x1, Pallas kernels, own_input(): pl.pallas_call(own_input_kernel, in_specs=[scalars(), *inside(4), *outsid...  3.12 us
    pallas_call x1, Pallas kernels, own_filter(): pl.pallas_call(own_filter_kernel, in_specs=inside(6), out_specs=inside(3)...  3.02 us
    ppermute x1, waiting for transfers between devices, body(): lax.ppermute(following, 'ctx', [(source, source - 1) for source in range(...  2.64 us
    pallas_call x1, Pallas kernels, halo_input(): pl.pallas_call(halo_input_kernel, in_specs=inside(8), out_specs=[pl.Block...  2.42 us
    convert_element_type x5, other arithmetic, narrow(): return value.astype(jnp.bfloat16)  2.19 us
    pallas_call x1, Pallas kernels, halo_filter(): pl.pallas_call(halo_filter_kernel, in_specs=[scalars(), *inside(6)], out_...  1.55 us
  transfers between devices with their start and end apart: 10, of which 8 were waited for; matrix products, arithmetic and copies ran while one was open for 0% of the time, Pallas kernels for 20%

profile of v3, /device:TPU:0, one launch (start us, length us, event | category | flops | bytes accessed | tf_op | source)
XLA Modules:
  0.0 48.4 jit_solution(7918231738197425607)
XLA Ops:
  0.6 2.1 %multiply_convert_fusion = bf16[64,4096]{1,0:T(8,128)(2,1)} fusion(bf16[128,4096]{1,0:T(8,128)(2,1)} %gate_ref.1, bf16[128,4096]{1,0:T(8,128)(2,1)} %grad_out_ref.1), kind=kLoop, calls=%fused_computation | loop fusion | flops 1048576 | bytes 1572864 | tf_op jit(solution)/shard_map/convert_element_type | solution.py:365
  2.7 1.3 %collective-permute-start = (bf16[64,4096]{1,0:T(8,128)(2,1)}, bf16[64,4096]{1,0:T(8,128)(2,1)S(1)}, u32[]{:S(2)}, u32[]{:S(2)}) collective-permute-start(bf16[64,4096]{1,0:T(8,128)(2,1)} %multiply_convert_fusion), channel_id=1, source_target_pairs={{1,0},{2,1},{3,2},{4,3},{5,4},{6,5},{7,6},{9,8},{10,9},{11,10},{12... | collective-permute-start | bytes 1572872 | tf_op jit(solution)/shard_map/ppermute | solution.py:381
  4.0 0.5 %collective-permute-start.1 = (bf16[64,1024]{1,0:T(8,128)(2,1)}, bf16[64,1024]{1,0:T(8,128)(2,1)S(1)}, u32[]{:S(2)}, u32[]{:S(2)}) collective-permute-start(bf16[64,1024]{1,0:T(8,128)(2,1)} %bitcast.11), channel_id=1, source_target_pairs={{0,8},{8,0},{16,24},{24,16},{1,9},{9,1},{17,25},{25,17},{2,10},{10... | collective-permute-start | bytes 393224 | tf_op jit(solution)/shard_map/ppermute | solution.py:361
  4.6 2.6 %collective-permute-start.2 = (bf16[64,1024]{1,0:T(8,128)(2,1)}, bf16[64,1024]{1,0:T(8,128)(2,1)S(1)}, u32[]{:S(2)}, u32[]{:S(2)}) collective-permute-start(bf16[64,1024]{1,0:T(8,128)(2,1)} %bitcast.12), channel_id=1, source_target_pairs={{0,16},{8,24},{16,0},{24,8},{1,17},{9,25},{17,1},{25,9},{2,18},{10... | collective-permute-start | bytes 393224 | tf_op jit(solution)/shard_map/ppermute | solution.py:361
  7.2 0.7 %copy-done.4 = s32[128]{0:T(128)S(1)} copy-done((s32[128]{0:T(128)S(1)}, s32[128]{0:T(128)}, u32[]{:S(2)}) %copy-start.4) | copy-done | bytes 536
  7.8 1.3 %basis.1 = (bf16[256,256]{1,0:T(8,128)(2,1)S(1)}, bf16[256,128]{1,0:T(8,128)(2,1)S(1)}, bf16[256,256]{1,0:T(8,128)(2,1)S(1)}, bf16[128,256]{1,0:T(8,128)(2,1)S(1...) custom-call(s32[128]{0:T(128)S(1)} %copy-done.4, ...), custom_call_target="tpu_custom_call" | custom-call | flops 1500000000 | bytes 1000000 | tf_op jit(solution)/shard_map/basis/pallas_call | solution.py:260
  9.7 3.0 %own_filter.1 = (f32[64,4096]{1,0:T(8,128)S(1)}, bf16[128,4096]{1,0:T(8,128)(2,1)S(1)}, f32[128,4096]{1,0:T(8,128)S(1)}) custom-call(bf16[256,256]{1,0:T(8,128)(2,1)S(1)} %get-tuple-element.25.rows_ref, bf16[128,256]{1,0:T(8,128)(2,1)S(1)} %get-tuple-element.26.filter_ref, bf16[128,128]{1,0:T(8,128)(2,1)S(1)} %get-tuple-element.27.last_ref, ...), custom_call_target="tpu_custom_call" | custom-call | flops 1342177280 | bytes 4194304 | tf_op jit(solution)/shard_map/own_filter/pallas_call | solution.py:285
  12.7 1.2 %collective-permute-done.3.refs_3_ = bf16[64,1024]{1,0:T(8,128)(2,1)S(1)} collective-permute-done((bf16[64,1024]{1,0:T(8,128)(2,1)}, bf16[64,1024]{1,0:T(8,128)(2,1)S(1)}, u32[]{:S(2)}, u32[]{:S(2)}) %collective-permute-start.3) | collective-permute-done | bytes 131104 | tf_op jit(solution)/shard_map/ppermute | solution.py:361
  14.0 3.1 %own_input.1 = (bf16[64,4096]{1,0:T(8,128)(2,1)S(1)}, f32[64,4096]{1,0:T(8,128)S(1)}, bf16[64,4096]{1,0:T(8,128)(2,1)S(1)}) custom-call(s32[1]{0:T(128)} %bitcast.1.place_ref, bf16[256,256]{1,0:T(8,128)(2,1)S(1)} %get-tuple-element.25.rows_ref, bf16[256,128]{1,0:T(8,128)(2,1)S(1)} %get-tuple-element.30.taps_ref, ...), custom_call_target="tpu_custom_call" | custom-call | flops 2013265920 | bytes 4718592 | tf_op jit(solution)/shard_map/own_input/pallas_call | solution.py:306
  17.1 2.6 %collective-permute-done.halo_ref = bf16[64,4096]{1,0:T(8,128)(2,1)S(1)} collective-permute-done((bf16[64,4096]{1,0:T(8,128)(2,1)}, bf16[64,4096]{1,0:T(8,128)(2,1)S(1)}, u32[]{:S(2)}, u32[]{:S(2)}) %collective-permute-start) | collective-permute-done | bytes 524320 | tf_op jit(solution)/shard_map/ppermute | solution.py:381
  19.7 1.5 %halo_filter.1 = (f32[2,64,1024]{2,1,0:T(8,128)S(1)}, bf16[2,64,1024]{2,1,0:T(8,128)(2,1)S(1)}) custom-call(s32[1]{0:T(128)} %bitcast.1.place_ref, bf16[128,128]{1,0:T(8,128)(2,1)S(1)} %get-tuple-element.21.rows_ref, bf16[128,128]{1,0:T(8,128)(2,1)S(1)} %get-tuple-element.24.filter_ref, f32[64,4096]{1,0:T(8,128)S(1)} %get-tuple-element.28.own_ref, ...), custom_call_target="tpu_custom_call" | custom-call | flops 335544320 | bytes 2621440 | tf_op jit(solution)/shard_map/halo_filter/pallas_call | solution.py:326
  21.4 1.5 %collective-permute-done.4 = bf16[2,64,1024]{2,1,0:T(8,128)(2,1)S(1)} collective-permute-done((bf16[2,64,1024]{2,1,0:T(8,128)(2,1)S(1)}, bf16[2,64,1024]{2,1,0:T(8,128)(2,1)S(1)}, u32[]{:S(2)}, u32[]{:S(2)}) %collective-permute-start.4) | collective-permute-done | bytes 262176 | tf_op jit(solution)/shard_map/ppermute | solution.py:361
  23.0 1.8 %collective-permute-start.5 = (bf16[1,64,1024]{2,1,0:T(8,128)(2,1)S(1)}, bf16[1,64,1024]{2,1,0:T(8,128)(2,1)S(1)}, u32[]{:S(2)}, u32[]{:S(2)}) collective-permute-start(bf16[1,64,1024]{2,1,0:T(8,128)(2,1)S(1)} %slice.46), channel_id=1, source_target_pairs={{0,16},{8,24},{16,0},{24,8},{1,17},{9,25},{17,1},{25,9},{2,18},{10... | collective-permute-start | bytes 393224 | tf_op jit(solution)/shard_map/ppermute | solution.py:361
  24.8 2.4 %halo_input.1 = (bf16[128,4096]{1,0:T(8,128)(2,1)}, f32[1,64,1024]{2,1,0:T(8,128)S(1)}) custom-call(bf16[128,128]{1,0:T(8,128)(2,1)S(1)} %get-tuple-element.21.rows_ref, bf16[128,128]{1,0:T(8,128)(2,1)S(1)} %get-tuple-element.22.taps_ref, bf16[128,128]{1,0:T(8,128)(2,1)S(1)} %get-tuple-element.23.input_ref, f32[1,64,1024]{2,1,0:T(8,128)S(1)} %slice.31.after_ref, ...), custom_call_target="tpu_custom_call" | custom-call | flops 469762048 | bytes 2621440 | tf_op jit(solution)/shard_map/halo_input/pallas_call | solution.py:345
  27.2 1.4 %collective-permute-done.5 = bf16[1,64,1024]{2,1,0:T(8,128)(2,1)S(1)} collective-permute-done((bf16[1,64,1024]{2,1,0:T(8,128)(2,1)S(1)}, bf16[1,64,1024]{2,1,0:T(8,128)(2,1)S(1)}, u32[]{:S(2)}, u32[]{:S(2)}) %collective-permute-start.5) | collective-permute-done | bytes 131104 | tf_op jit(solution)/shard_map/ppermute | solution.py:361
  28.6 2.7 %collective-permute-start.6 = (bf16[32,1024]{1,0:T(8,128)(2,1)S(1)}, bf16[32,1024]{1,0:T(8,128)(2,1)S(1)}, u32[]{:S(2)}, u32[]{:S(2)}) collective-permute-start(bf16[32,1024]{1,0:T(8,128)(2,1)S(1)} %fusion.1), channel_id=1, source_target_pairs={{0,1},{1,0},{2,3},{3,2},{4,5},{5,4},{6,7},{7,6},{8,9},{9,8},{10,11... | collective-permute-start | bytes 196616 | tf_op jit(solution)/shard_map/ppermute | solution.py:361
  31.3 2.2 %collective-permute-done.6 = bf16[32,1024]{1,0:T(8,128)(2,1)S(1)} collective-permute-done((bf16[32,1024]{1,0:T(8,128)(2,1)S(1)}, bf16[32,1024]{1,0:T(8,128)(2,1)S(1)}, u32[]{:S(2)}, u32[]{:S(2)}) %collective-permute-start.6) | collective-permute-done | bytes 65568 | tf_op jit(solution)/shard_map/ppermute | solution.py:361
  33.6 1.6 %collective-permute-start.7 = (bf16[32,1024]{1,0:T(8,128)(2,1)S(1)}, bf16[32,1024]{1,0:T(8,128)(2,1)S(1)}, u32[]{:S(2)}, u32[]{:S(2)}) collective-permute-start(bf16[32,1024]{1,0:T(8,128)(2,1)S(1)} %fusion), channel_id=1, source_target_pairs={{0,2},{1,3},{2,0},{3,1},{4,6},{5,7},{6,4},{7,5},{8,10},{9,11},{10,... | collective-permute-start | bytes 196616 | tf_op jit(solution)/shard_map/ppermute | solution.py:361
  35.2 2.7 %collective-permute-done.7 = bf16[32,1024]{1,0:T(8,128)(2,1)S(1)} collective-permute-done((bf16[32,1024]{1,0:T(8,128)(2,1)S(1)}, bf16[32,1024]{1,0:T(8,128)(2,1)S(1)}, u32[]{:S(2)}, u32[]{:S(2)}) %collective-permute-start.7) | collective-permute-done | bytes 65568 | tf_op jit(solution)/shard_map/ppermute | solution.py:361
  37.9 2.9 %collective-permute-start.8 = (bf16[32,1024]{1,0:T(8,128)(2,1)S(1)}, bf16[32,1024]{1,0:T(8,128)(2,1)S(1)}, u32[]{:S(2)}, u32[]{:S(2)}) collective-permute-start(bf16[32,1024]{1,0:T(8,128)(2,1)S(1)} %add_convert_fusion.1), channel_id=1, source_target_pairs={{0,4},{1,5},{2,6},{3,7},{4,0},{5,1},{6,2},{7,3},{8,12},{9,13},{10,... | collective-permute-start | bytes 196616 | tf_op jit(solution)/shard_map/ppermute | solution.py:361
  40.8 2.4 %collective-permute-done.8 = bf16[32,1024]{1,0:T(8,128)(2,1)S(1)} collective-permute-done((bf16[32,1024]{1,0:T(8,128)(2,1)S(1)}, bf16[32,1024]{1,0:T(8,128)(2,1)S(1)}, u32[]{:S(2)}, u32[]{:S(2)}) %collective-permute-start.8) | collective-permute-done | bytes 65568 | tf_op jit(solution)/shard_map/ppermute | solution.py:361
  43.2 2.2 %collective-permute-start.9 = (bf16[32,1024]{1,0:T(8,128)(2,1)S(1)}, bf16[32,1024]{1,0:T(8,128)(2,1)S(1)}, u32[]{:S(2)}, u32[]{:S(2)}) collective-permute-start(bf16[32,1024]{1,0:T(8,128)(2,1)S(1)} %add_convert_fusion), channel_id=1, source_target_pairs={{0,1},{1,0},{2,3},{3,2},{4,5},{5,4},{6,7},{7,6},{8,9},{9,8},{10,11... | collective-permute-start | bytes 196616 | tf_op jit(solution)/shard_map/ppermute | solution.py:361
  45.4 2.2 %collective-permute-done.9 = bf16[32,1024]{1,0:T(8,128)(2,1)S(1)} collective-permute-done((bf16[32,1024]{1,0:T(8,128)(2,1)S(1)}, bf16[32,1024]{1,0:T(8,128)(2,1)S(1)}, u32[]{:S(2)}, u32[]{:S(2)}) %collective-permute-start.9) | collective-permute-done | bytes 65568 | tf_op jit(solution)/shard_map/ppermute | solution.py:361
  47.6 0.7 %convert_bitcast_fusion = f32[1024,64]{0,1:T(8,128)} fusion(bf16[32,1024]{1,0:T(8,128)(2,1)S(1)} %get-tuple-element.41, bf16[32,1024]{1,0:T(8,128)(2,1)S(1)} %get-tuple-element.40), kind=kLoop, calls=%fused_computation.3 | loop fusion | flops 262144 | bytes 393216 | tf_op jit(solution)/shard_map/transpose | solution.py:412
  (22 shorter events, 0.9 us)
Async XLA Ops:
  2.7 17.0 %collective-permute-start = (bf16[64,4096]{1,0:T(8,128)(2,1)}, bf16[64,4096]{1,0:T(8,128)(2,1)S(1)}, u32[]{:S(2)}, u32[]{:S(2)}) collective-permute-start(bf16[64,4096]{1,0:T(8,128)(2,1)} %multiply_convert_fusion), channel_id=1, source_target_pairs={{1,0},{2,1},{3,2},{4,3},{5,4},{6,5},{7,6},{9,8},{10,9},{11,10},{12... | collective-permute-start | bytes 1572872 | tf_op jit(solution)/shard_map/ppermute | solution.py:381
  4.0 8.7 %collective-permute-start.1 = (bf16[64,1024]{1,0:T(8,128)(2,1)}, bf16[64,1024]{1,0:T(8,128)(2,1)S(1)}, u32[]{:S(2)}, u32[]{:S(2)}) collective-permute-start(bf16[64,1024]{1,0:T(8,128)(2,1)} %bitcast.11), channel_id=1, source_target_pairs={{0,8},{8,0},{16,24},{24,16},{1,9},{9,1},{17,25},{25,17},{2,10},{10... | collective-permute-start | bytes 393224 | tf_op jit(solution)/shard_map/ppermute | solution.py:361
  4.6 8.2 %collective-permute-start.2 = (bf16[64,1024]{1,0:T(8,128)(2,1)}, bf16[64,1024]{1,0:T(8,128)(2,1)S(1)}, u32[]{:S(2)}, u32[]{:S(2)}) collective-permute-start(bf16[64,1024]{1,0:T(8,128)(2,1)} %bitcast.12), channel_id=1, source_target_pairs={{0,16},{8,24},{16,0},{24,8},{1,17},{9,25},{17,1},{25,9},{2,18},{10... | collective-permute-start | bytes 393224 | tf_op jit(solution)/shard_map/ppermute | solution.py:361
  7.1 6.8 %collective-permute-start.3 = (bf16[64,1024]{1,0:T(8,128)(2,1)}, bf16[64,1024]{1,0:T(8,128)(2,1)S(1)}, u32[]{:S(2)}, u32[]{:S(2)}) collective-permute-start(bf16[64,1024]{1,0:T(8,128)(2,1)} %bitcast.13), channel_id=1, source_target_pairs={{0,24},{8,16},{16,8},{24,0},{1,25},{9,17},{17,9},{25,1},{2,26},{10... | collective-permute-start | bytes 393224 | tf_op jit(solution)/shard_map/ppermute | solution.py:361
  7.2 0.7 %copy-start.4 = (s32[128]{0:T(128)S(1)}, s32[128]{0:T(128)}, u32[]{:S(2)}) copy-start(s32[128]{0:T(128)} %end_ref.1) | copy-start | bytes 1540
  7.8 1.3 %copy-start = (bf16[128,4096]{1,0:T(8,128)(2,1)S(1)}, bf16[128,4096]{1,0:T(8,128)(2,1)}, u32[]{:S(2)}) copy-start(bf16[128,4096]{1,0:T(8,128)(2,1)} %grad_out_ref.1) | copy-start | bytes 3145732
  7.8 1.5 %copy-start.1 = (bf16[128,4096]{1,0:T(8,128)(2,1)S(1)}, bf16[128,4096]{1,0:T(8,128)(2,1)}, u32[]{:S(2)}) copy-start(bf16[128,4096]{1,0:T(8,128)(2,1)} %gate_ref.1) | copy-start | bytes 3145732
  7.8 1.9 %copy-start.2 = (bf16[128,4096]{1,0:T(8,128)(2,1)S(1)}, bf16[128,4096]{1,0:T(8,128)(2,1)}, u32[]{:S(2)}) copy-start(bf16[128,4096]{1,0:T(8,128)(2,1)} %conv_in_ref.1) | copy-start | bytes 3145732
  9.7 4.3 %copy-start.3 = (bf16[1024,64]{0,1:T(8,128)(2,1)S(1)}, bf16[1024,64]{0,1:T(8,128)(2,1)}, u32[]{:S(2)}) copy-start(bf16[1024,64]{0,1:T(8,128)(2,1)} %param.8) | copy-start | bytes 393220
  21.3 1.6 %collective-permute-start.4 = (bf16[2,64,1024]{2,1,0:T(8,128)(2,1)S(1)}, bf16[2,64,1024]{2,1,0:T(8,128)(2,1)S(1)}, u32[]{:S(2)}, u32[]{:S(2)}) collective-permute-start(bf16[2,64,1024]{2,1,0:T(8,128)(2,1)S(1)} %get-tuple-element.35), channel_id=1, source_target_pairs={{0,8},{8,0},{16,24},{24,16},{1,9},{9,1},{17,25},{25,17},{2,10},{10... | collective-permute-start | bytes 786440 | tf_op jit(solution)/shard_map/ppermute | solution.py:361
  23.0 5.6 %collective-permute-start.5 = (bf16[1,64,1024]{2,1,0:T(8,128)(2,1)S(1)}, bf16[1,64,1024]{2,1,0:T(8,128)(2,1)S(1)}, u32[]{:S(2)}, u32[]{:S(2)}) collective-permute-start(bf16[1,64,1024]{2,1,0:T(8,128)(2,1)S(1)} %slice.46), channel_id=1, source_target_pairs={{0,16},{8,24},{16,0},{24,8},{1,17},{9,25},{17,1},{25,9},{2,18},{10... | collective-permute-start | bytes 393224 | tf_op jit(solution)/shard_map/ppermute | solution.py:361
  28.6 4.9 %collective-permute-start.6 = (bf16[32,1024]{1,0:T(8,128)(2,1)S(1)}, bf16[32,1024]{1,0:T(8,128)(2,1)S(1)}, u32[]{:S(2)}, u32[]{:S(2)}) collective-permute-start(bf16[32,1024]{1,0:T(8,128)(2,1)S(1)} %fusion.1), channel_id=1, source_target_pairs={{0,1},{1,0},{2,3},{3,2},{4,5},{5,4},{6,7},{7,6},{8,9},{9,8},{10,11... | collective-permute-start | bytes 196616 | tf_op jit(solution)/shard_map/ppermute | solution.py:361
  33.6 4.3 %collective-permute-start.7 = (bf16[32,1024]{1,0:T(8,128)(2,1)S(1)}, bf16[32,1024]{1,0:T(8,128)(2,1)S(1)}, u32[]{:S(2)}, u32[]{:S(2)}) collective-permute-start(bf16[32,1024]{1,0:T(8,128)(2,1)S(1)} %fusion), channel_id=1, source_target_pairs={{0,2},{1,3},{2,0},{3,1},{4,6},{5,7},{6,4},{7,5},{8,10},{9,11},{10,... | collective-permute-start | bytes 196616 | tf_op jit(solution)/shard_map/ppermute | solution.py:361
  37.9 5.2 %collective-permute-start.8 = (bf16[32,1024]{1,0:T(8,128)(2,1)S(1)}, bf16[32,1024]{1,0:T(8,128)(2,1)S(1)}, u32[]{:S(2)}, u32[]{:S(2)}) collective-permute-start(bf16[32,1024]{1,0:T(8,128)(2,1)S(1)} %add_convert_fusion.1), channel_id=1, source_target_pairs={{0,4},{1,5},{2,6},{3,7},{4,0},{5,1},{6,2},{7,3},{8,12},{9,13},{10,... | collective-permute-start | bytes 196616 | tf_op jit(solution)/shard_map/ppermute | solution.py:361
  43.2 4.4 %collective-permute-start.9 = (bf16[32,1024]{1,0:T(8,128)(2,1)S(1)}, bf16[32,1024]{1,0:T(8,128)(2,1)S(1)}, u32[]{:S(2)}, u32[]{:S(2)}) collective-permute-start(bf16[32,1024]{1,0:T(8,128)(2,1)S(1)} %add_convert_fusion), channel_id=1, source_target_pairs={{0,1},{1,0},{2,3},{3,2},{4,5},{5,4},{6,7},{7,6},{8,9},{9,8},{10,11... | collective-permute-start | bytes 196616 | tf_op jit(solution)/shard_map/ppermute | solution.py:361

commit v4 on v3

--- a/solution.py
+++ b/solution.py
@@ -218,7 +218,8 @@
 
 
 def halo_input_kernel(rows_ref, taps_ref, input_ref, after_ref, halo_ref, head_ref, tail_ref, filt_ref,
-                      out_ref, passed_ref, y_ref, f_ref, z_ref, last_ref, sems):
+                      order_ref, out_ref, passed_ref, y_ref, f_ref, z_ref, last_ref, sems):
+    del order_ref
     head, (owners, _, width) = head_ref.shape[0], y_ref.shape
     taps = halo_ref.shape[0]
     copies = [pltpu.make_async_copy(head_ref, out_ref.at[pl.ds(0, head), :], sems.at[owners])]
@@ -338,13 +339,13 @@
     )(place, *bases, own, x_hat, halo, after)
 
 
-def halo_input(bases, after, halo, head, tail, filt, owners):
+def halo_input(bases, after, halo, head, tail, filt, order, owners):
     taps, channels = halo.shape
     width = channels // owners
     rows = head.shape[0] + taps
     return pl.pallas_call(
         halo_input_kernel,
-        in_specs=inside(8),
+        in_specs=[*inside(8), *outside(1)],
         out_specs=[pl.BlockSpec(memory_space=pl.ANY), *inside(1)],
         out_shape=[shaped(rows, channels), shaped(*after.shape, dtype=after.dtype)],
         scratch_shapes=[
@@ -354,7 +355,7 @@
         compiler_params=params(),
         cost_estimate=cost(28 * taps * taps * channels, 10 * taps * channels),
         name="halo_input",
-    )(*bases, after, halo, head, tail, filt)
+    )(*bases, after, halo, head, tail, filt, order)
 
 
 def swap(value, axis, bit):
@@ -388,19 +389,22 @@
     head, tail, whole_filter = own_input(place, bases[:3], grad_y, pieces)
     keep, send = halo_filter(place, (halo_rows, halo_inverse_filter), own, x_hat, halo, tail, dp)
 
-    arrived, bit = swap(send, "dp", 1), 2
-    while bit < dp:
-        total = keep + widen(arrived)
-        keep, arrived = total[0::2], swap(narrow(total[1::2]), "dp", bit)
+    bit = 1
+    while bit < dp // 2:
+        total = keep + widen(swap(send, "dp", bit))
+        keep, send = total[0::2], narrow(total[1::2])
         bit *= 2
-    grad_in, keep = halo_input(
-        (halo_rows, halo_taps, halo_inverse_input), keep, halo, head, tail, whole_filter, dp
-    )
-    total = (keep + widen(arrived))[0]
     half = taps // 2
     low = lax.rem(block, 2) == 0
-    kept = jnp.where(low, total[:half], total[half:])
-    total = kept + widen(swap(narrow(jnp.where(low, total[half:], total[:half])), "ctx", 1))
+    home = lambda value: jnp.where(low, value[0, :half], value[0, half:])
+    away = lambda value: jnp.where(low, value[0, half:], value[0, :half])
+    arrived_away, arrived_home = swap(away(send), "dp", bit), swap(home(send), "dp", bit)
+    passing = narrow(away(keep) + widen(arrived_away))
+    arrived = swap(passing, "ctx", 1)
+    grad_in, kept = halo_input(
+        (halo_rows, halo_taps, halo_inverse_input), home(keep), halo, head, tail, whole_filter, passing, dp
+    )
+    total = kept + widen(arrived_home) + widen(arrived)
     bit = 2
     while bit < ctx:
         mine = narrow(total)

time: 48.5 us -> 50.1 us (1.033)
  starting transfers between devices: 15.6 us -> 17.4 us
  waiting for transfers between devices: 16.3 us -> 15.1 us
  other arithmetic: 3 us -> 4 us
    ppermute x9 -> x10, starting transfers between devices: 14.3 us -> 16.1 us  [swap(): lax.ppermute(value, axis, [(source, source ^ bit) for source in range(lax...]
    ppermute x9 -> x10, waiting for transfers between devices: 13.7 us -> 12.5 us  [swap(): lax.ppermute(value, axis, [(source, source ^ bit) for source in range(lax...]
    another operation x0 -> x1, other arithmetic: none -> 1.03 us
  transfers between devices with their start and end apart: 10 -> 11, of which waited for: 8 -> 7; matrix products, arithmetic and copies ran while one was open for 0% -> 0% of each run, Pallas kernels for 20% -> 20%
where the time goes in v4:
time: 50.1 us; the launch traced here: 49.9 us
  starting transfers between devices  17.4 us (35%)
  waiting for transfers between devices  15.1 us (30%)
  Pallas kernels  11.4 us (23%)
  other arithmetic  4 us (8%)
  local copies, waits for them, and re-layouts  1.15 us (2%)
  between operations  0.78 us (2%)
    ppermute x10, starting transfers between devices, swap(): lax.ppermute(value, axis, [(source, source ^ bit) for source in range(lax...  16.1 us
    ppermute x10, waiting for transfers between devices, swap(): lax.ppermute(value, axis, [(source, source ^ bit) for source in range(lax...  12.5 us
    pallas_call x1, Pallas kernels, own_input(): pl.pallas_call(own_input_kernel, in_specs=[scalars(), *inside(4), *outsid...  3.11 us
    pallas_call x1, Pallas kernels, own_filter(): pl.pallas_call(own_filter_kernel, in_specs=inside(6), out_specs=inside(3)...  3.03 us
    ppermute x1, waiting for transfers between devices, body(): lax.ppermute(following, 'ctx', [(source, source - 1) for source in range(...  2.65 us
    pallas_call x1, Pallas kernels, halo_input(): pl.pallas_call(halo_input_kernel, in_specs=[*inside(8), *outside(1)], out...  2.41 us
    convert_element_type x5, other arithmetic, narrow(): return value.astype(jnp.bfloat16)  2.2 us
    pallas_call x1, Pallas kernels, halo_filter(): pl.pallas_call(halo_filter_kernel, in_specs=[scalars(), *inside(6)], out_...  1.55 us
  transfers between devices with their start and end apart: 11, of which 7 were waited for; matrix products, arithmetic and copies ran while one was open for 0% of the time, Pallas kernels for 20%

profile of v4, /device:TPU:0, one launch (start us, length us, event | category | flops | bytes accessed | tf_op | source)
XLA Modules:
  0.0 49.9 jit_solution(13925561942290252227)
XLA Ops:
  0.6 2.1 %multiply_convert_fusion = bf16[64,4096]{1,0:T(8,128)(2,1)} fusion(bf16[128,4096]{1,0:T(8,128)(2,1)} %gate_ref.1, bf16[128,4096]{1,0:T(8,128)(2,1)} %grad_out_ref.1), kind=kLoop, calls=%fused_computation | loop fusion | flops 1048576 | bytes 1572864 | tf_op jit(solution)/shard_map/convert_element_type | solution.py:366
  2.7 1.3 %collective-permute-start = (bf16[64,4096]{1,0:T(8,128)(2,1)}, bf16[64,4096]{1,0:T(8,128)(2,1)S(1)}, u32[]{:S(2)}, u32[]{:S(2)}) collective-permute-start(bf16[64,4096]{1,0:T(8,128)(2,1)} %multiply_convert_fusion), channel_id=1, source_target_pairs={{1,0},{2,1},{3,2},{4,3},{5,4},{6,5},{7,6},{9,8},{10,9},{11,10},{12... | collective-permute-start | bytes 1572872 | tf_op jit(solution)/shard_map/ppermute | solution.py:382
  4.0 0.5 %collective-permute-start.1 = (bf16[64,1024]{1,0:T(8,128)(2,1)}, bf16[64,1024]{1,0:T(8,128)(2,1)S(1)}, u32[]{:S(2)}, u32[]{:S(2)}) collective-permute-start(bf16[64,1024]{1,0:T(8,128)(2,1)} %bitcast.15), channel_id=1, source_target_pairs={{0,8},{8,0},{16,24},{24,16},{1,9},{9,1},{17,25},{25,17},{2,10},{10... | collective-permute-start | bytes 393224 | tf_op jit(solution)/shard_map/ppermute | solution.py:362
  4.6 2.6 %collective-permute-start.2 = (bf16[64,1024]{1,0:T(8,128)(2,1)}, bf16[64,1024]{1,0:T(8,128)(2,1)S(1)}, u32[]{:S(2)}, u32[]{:S(2)}) collective-permute-start(bf16[64,1024]{1,0:T(8,128)(2,1)} %bitcast.16), channel_id=1, source_target_pairs={{0,16},{8,24},{16,0},{24,8},{1,17},{9,25},{17,1},{25,9},{2,18},{10... | collective-permute-start | bytes 393224 | tf_op jit(solution)/shard_map/ppermute | solution.py:362
  7.2 0.7 %copy-done.4 = s32[128]{0:T(128)S(1)} copy-done((s32[128]{0:T(128)S(1)}, s32[128]{0:T(128)}, u32[]{:S(2)}) %copy-start.4) | copy-done | bytes 536
  7.8 1.3 %basis.1 = (bf16[256,256]{1,0:T(8,128)(2,1)S(1)}, bf16[256,128]{1,0:T(8,128)(2,1)S(1)}, bf16[256,256]{1,0:T(8,128)(2,1)S(1)}, bf16[128,256]{1,0:T(8,128)(2,1)S(1...) custom-call(s32[128]{0:T(128)S(1)} %copy-done.4, ...), custom_call_target="tpu_custom_call" | custom-call | flops 1500000000 | bytes 1000000 | tf_op jit(solution)/shard_map/basis/pallas_call | solution.py:261
  9.7 3.0 %own_filter.1 = (f32[64,4096]{1,0:T(8,128)S(1)}, bf16[128,4096]{1,0:T(8,128)(2,1)S(1)}, f32[128,4096]{1,0:T(8,128)S(1)}) custom-call(bf16[256,256]{1,0:T(8,128)(2,1)S(1)} %get-tuple-element.25.rows_ref, bf16[128,256]{1,0:T(8,128)(2,1)S(1)} %get-tuple-element.26.filter_ref, bf16[128,128]{1,0:T(8,128)(2,1)S(1)} %get-tuple-element.27.last_ref, ...), custom_call_target="tpu_custom_call" | custom-call | flops 1342177280 | bytes 4194304 | tf_op jit(solution)/shard_map/own_filter/pallas_call | solution.py:286
  12.8 1.2 %collective-permute-done.3.refs_3_ = bf16[64,1024]{1,0:T(8,128)(2,1)S(1)} collective-permute-done((bf16[64,1024]{1,0:T(8,128)(2,1)}, bf16[64,1024]{1,0:T(8,128)(2,1)S(1)}, u32[]{:S(2)}, u32[]{:S(2)}) %collective-permute-start.3) | collective-permute-done | bytes 131104 | tf_op jit(solution)/shard_map/ppermute | solution.py:362
  14.0 3.1 %own_input.1 = (bf16[64,4096]{1,0:T(8,128)(2,1)S(1)}, f32[64,4096]{1,0:T(8,128)S(1)}, bf16[64,4096]{1,0:T(8,128)(2,1)S(1)}) custom-call(s32[1]{0:T(128)} %bitcast.1.place_ref, bf16[256,256]{1,0:T(8,128)(2,1)S(1)} %get-tuple-element.25.rows_ref, bf16[256,128]{1,0:T(8,128)(2,1)S(1)} %get-tuple-element.30.taps_ref, ...), custom_call_target="tpu_custom_call" | custom-call | flops 2013265920 | bytes 4718592 | tf_op jit(solution)/shard_map/own_input/pallas_call | solution.py:307
  17.1 2.7 %collective-permute-done.halo_ref = bf16[64,4096]{1,0:T(8,128)(2,1)S(1)} collective-permute-done((bf16[64,4096]{1,0:T(8,128)(2,1)}, bf16[64,4096]{1,0:T(8,128)(2,1)S(1)}, u32[]{:S(2)}, u32[]{:S(2)}) %collective-permute-start) | collective-permute-done | bytes 524320 | tf_op jit(solution)/shard_map/ppermute | solution.py:382
  19.7 1.5 %halo_filter.1 = (f32[2,64,1024]{2,1,0:T(8,128)S(1)}, bf16[2,64,1024]{2,1,0:T(8,128)(2,1)S(1)}) custom-call(s32[1]{0:T(128)} %bitcast.1.place_ref, bf16[128,128]{1,0:T(8,128)(2,1)S(1)} %get-tuple-element.21.rows_ref, bf16[128,128]{1,0:T(8,128)(2,1)S(1)} %get-tuple-element.24.filter_ref, f32[64,4096]{1,0:T(8,128)S(1)} %get-tuple-element.28.own_ref, ...), custom_call_target="tpu_custom_call" | custom-call | flops 335544320 | bytes 2621440 | tf_op jit(solution)/shard_map/halo_filter/pallas_call | solution.py:327
  21.4 1.6 %collective-permute-done.4 = bf16[2,64,1024]{2,1,0:T(8,128)(2,1)} collective-permute-done((bf16[2,64,1024]{2,1,0:T(8,128)(2,1)S(1)}, bf16[2,64,1024]{2,1,0:T(8,128)(2,1)}, u32[]{:S(2)}, u32[]{:S(2)}) %collective-permute-start.4) | collective-permute-done | bytes 262176 | tf_op jit(solution)/shard_map/ppermute | solution.py:362
  23.0 1.0 %fusion.1 = (bf16[2,64,1024]{2,1,0:T(8,128)(2,1)S(1)}, f32[2,64,1024]{2,1,0:T(8,128)S(1)}) fusion(f32[2,64,1024]{2,1,0:T(8,128)S(1)} %get-tuple-element.34, bf16[2,64,1024]{2,1,0:T(8,128)(2,1)} %collective-permute-done.4), kind=kLoop, calls=%fused_computation.13 | loop fusion | flops 393216 | bytes 1572864 | tf_op jit(solution)/shard_map/convert.1
  24.1 1.8 %collective-permute-start.5 = (bf16[32,1024]{1,0:T(8,128)(2,1)S(1)}, bf16[32,1024]{1,0:T(8,128)(2,1)S(1)}, u32[]{:S(2)}, u32[]{:S(2)}) collective-permute-start(bf16[32,1024]{1,0:T(8,128)(2,1)S(1)} %get-tuple-element.43), channel_id=1, source_target_pairs={{0,16},{8,24},{16,0},{24,8},{1,17},{9,25},{17,1},{25,9},{2,18},{10... | collective-permute-start | bytes 196616 | tf_op jit(solution)/shard_map/ppermute | solution.py:362
  26.2 2.4 %collective-permute-done.5 = bf16[32,1024]{1,0:T(8,128)(2,1)S(1)} collective-permute-done((bf16[32,1024]{1,0:T(8,128)(2,1)S(1)}, bf16[32,1024]{1,0:T(8,128)(2,1)S(1)}, u32[]{:S(2)}, u32[]{:S(2)}) %collective-permute-start.5) | collective-permute-done | bytes 65568 | tf_op jit(solution)/shard_map/ppermute | solution.py:362
  28.6 2.9 %collective-permute-start.7 = (bf16[32,1024]{1,0:T(8,128)(2,1)S(1)}, bf16[32,1024]{1,0:T(8,128)(2,1)S(1)}, u32[]{:S(2)}, u32[]{:S(2)}) collective-permute-start(bf16[32,1024]{1,0:T(8,128)(2,1)S(1)} %fusion.order_ref), channel_id=1, source_target_pairs={{0,1},{1,0},{2,3},{3,2},{4,5},{5,4},{6,7},{7,6},{8,9},{9,8},{10,11... | collective-permute-start | bytes 196616 | tf_op jit(solution)/shard_map/ppermute | solution.py:362
  31.6 2.4 %halo_input.1 = (bf16[128,4096]{1,0:T(8,128)(2,1)}, f32[32,1024]{1,0:T(8,128)S(1)}) custom-call(bf16[128,128]{1,0:T(8,128)(2,1)S(1)} %get-tuple-element.21.rows_ref, bf16[128,128]{1,0:T(8,128)(2,1)S(1)} %get-tuple-element.22.taps_ref, bf16[128,128]{1,0:T(8,128)(2,1)S(1)} %get-tuple-element.23.input_ref, f32[32,1024]{1,0:T(8,128)S(1)} %select_bitcast_fusion.after_ref, ...), custom_call_target="tpu_custom_call" | custom-call | flops 469762048 | bytes 2621440 | tf_op jit(solution)/shard_map/halo_input/pallas_call | solution.py:346
  34.0 1.6 %collective-permute-start.8 = (bf16[32,1024]{1,0:T(8,128)(2,1)S(1)}, bf16[32,1024]{1,0:T(8,128)(2,1)S(1)}, u32[]{:S(2)}, u32[]{:S(2)}) collective-permute-start(bf16[32,1024]{1,0:T(8,128)(2,1)S(1)} %add_convert_fusion.2), channel_id=1, source_target_pairs={{0,2},{1,3},{2,0},{3,1},{4,6},{5,7},{6,4},{7,5},{8,10},{9,11},{10,... | collective-permute-start | bytes 196616 | tf_op jit(solution)/shard_map/ppermute | solution.py:362
  35.7 2.7 %collective-permute-done.8 = bf16[32,1024]{1,0:T(8,128)(2,1)S(1)} collective-permute-done((bf16[32,1024]{1,0:T(8,128)(2,1)S(1)}, bf16[32,1024]{1,0:T(8,128)(2,1)S(1)}, u32[]{:S(2)}, u32[]{:S(2)}) %collective-permute-start.8) | collective-permute-done | bytes 65568 | tf_op jit(solution)/shard_map/ppermute | solution.py:362
  38.4 3.0 %collective-permute-start.9 = (bf16[32,1024]{1,0:T(8,128)(2,1)S(1)}, bf16[32,1024]{1,0:T(8,128)(2,1)S(1)}, u32[]{:S(2)}, u32[]{:S(2)}) collective-permute-start(bf16[32,1024]{1,0:T(8,128)(2,1)S(1)} %add_convert_fusion.1), channel_id=1, source_target_pairs={{0,4},{1,5},{2,6},{3,7},{4,0},{5,1},{6,2},{7,3},{8,12},{9,13},{10,... | collective-permute-start | bytes 196616 | tf_op jit(solution)/shard_map/ppermute | solution.py:362
  41.4 2.2 %collective-permute-done.9 = bf16[32,1024]{1,0:T(8,128)(2,1)S(1)} collective-permute-done((bf16[32,1024]{1,0:T(8,128)(2,1)S(1)}, bf16[32,1024]{1,0:T(8,128)(2,1)S(1)}, u32[]{:S(2)}, u32[]{:S(2)}) %collective-permute-start.9) | collective-permute-done | bytes 65568 | tf_op jit(solution)/shard_map/ppermute | solution.py:362
  43.7 3.3 %collective-permute-start.10 = (bf16[32,1024]{1,0:T(8,128)(2,1)S(1)}, bf16[32,1024]{1,0:T(8,128)(2,1)S(1)}, u32[]{:S(2)}, u32[]{:S(2)}) collective-permute-start(bf16[32,1024]{1,0:T(8,128)(2,1)S(1)} %add_convert_fusion), channel_id=1, source_target_pairs={{0,1},{1,0},{2,3},{3,2},{4,5},{5,4},{6,7},{7,6},{8,9},{9,8},{10,11... | collective-permute-start | bytes 196616 | tf_op jit(solution)/shard_map/ppermute | solution.py:362
  46.9 2.2 %collective-permute-done.10 = bf16[32,1024]{1,0:T(8,128)(2,1)S(1)} collective-permute-done((bf16[32,1024]{1,0:T(8,128)(2,1)S(1)}, bf16[32,1024]{1,0:T(8,128)(2,1)S(1)}, u32[]{:S(2)}, u32[]{:S(2)}) %collective-permute-start.10) | collective-permute-done | bytes 65568 | tf_op jit(solution)/shard_map/ppermute | solution.py:362
  49.2 0.7 %convert_bitcast_fusion = f32[1024,64]{0,1:T(8,128)} fusion(bf16[32,1024]{1,0:T(8,128)(2,1)S(1)} %get-tuple-element.45, bf16[32,1024]{1,0:T(8,128)(2,1)S(1)} %get-tuple-element.44), kind=kLoop, calls=%fused_computation.2 | loop fusion | flops 262144 | bytes 393216 | tf_op jit(solution)/shard_map/transpose | solution.py:416
  (23 shorter events, 1.1 us)
Async XLA Ops:
  2.7 17.0 %collective-permute-start = (bf16[64,4096]{1,0:T(8,128)(2,1)}, bf16[64,4096]{1,0:T(8,128)(2,1)S(1)}, u32[]{:S(2)}, u32[]{:S(2)}) collective-permute-start(bf16[64,4096]{1,0:T(8,128)(2,1)} %multiply_convert_fusion), channel_id=1, source_target_pairs={{1,0},{2,1},{3,2},{4,3},{5,4},{6,5},{7,6},{9,8},{10,9},{11,10},{12... | collective-permute-start | bytes 1572872 | tf_op jit(solution)/shard_map/ppermute | solution.py:382
  4.0 8.7 %collective-permute-start.1 = (bf16[64,1024]{1,0:T(8,128)(2,1)}, bf16[64,1024]{1,0:T(8,128)(2,1)S(1)}, u32[]{:S(2)}, u32[]{:S(2)}) collective-permute-start(bf16[64,1024]{1,0:T(8,128)(2,1)} %bitcast.15), channel_id=1, source_target_pairs={{0,8},{8,0},{16,24},{24,16},{1,9},{9,1},{17,25},{25,17},{2,10},{10... | collective-permute-start | bytes 393224 | tf_op jit(solution)/shard_map/ppermute | solution.py:362
  4.6 8.2 %collective-permute-start.2 = (bf16[64,1024]{1,0:T(8,128)(2,1)}, bf16[64,1024]{1,0:T(8,128)(2,1)S(1)}, u32[]{:S(2)}, u32[]{:S(2)}) collective-permute-start(bf16[64,1024]{1,0:T(8,128)(2,1)} %bitcast.16), channel_id=1, source_target_pairs={{0,16},{8,24},{16,0},{24,8},{1,17},{9,25},{17,1},{25,9},{2,18},{10... | collective-permute-start | bytes 393224 | tf_op jit(solution)/shard_map/ppermute | solution.py:362
  7.1 6.8 %collective-permute-start.3 = (bf16[64,1024]{1,0:T(8,128)(2,1)}, bf16[64,1024]{1,0:T(8,128)(2,1)S(1)}, u32[]{:S(2)}, u32[]{:S(2)}) collective-permute-start(bf16[64,1024]{1,0:T(8,128)(2,1)} %bitcast.17), channel_id=1, source_target_pairs={{0,24},{8,16},{16,8},{24,0},{1,25},{9,17},{17,9},{25,1},{2,26},{10... | collective-permute-start | bytes 393224 | tf_op jit(solution)/shard_map/ppermute | solution.py:362
  7.2 0.7 %copy-start.4 = (s32[128]{0:T(128)S(1)}, s32[128]{0:T(128)}, u32[]{:S(2)}) copy-start(s32[128]{0:T(128)} %end_ref.1) | copy-start | bytes 1540
  7.8 1.4 %copy-start = (bf16[128,4096]{1,0:T(8,128)(2,1)S(1)}, bf16[128,4096]{1,0:T(8,128)(2,1)}, u32[]{:S(2)}) copy-start(bf16[128,4096]{1,0:T(8,128)(2,1)} %grad_out_ref.1) | copy-start | bytes 3145732
  7.8 1.5 %copy-start.1 = (bf16[128,4096]{1,0:T(8,128)(2,1)S(1)}, bf16[128,4096]{1,0:T(8,128)(2,1)}, u32[]{:S(2)}) copy-start(bf16[128,4096]{1,0:T(8,128)(2,1)} %gate_ref.1) | copy-start | bytes 3145732
  7.8 1.9 %copy-start.2 = (bf16[128,4096]{1,0:T(8,128)(2,1)S(1)}, bf16[128,4096]{1,0:T(8,128)(2,1)}, u32[]{:S(2)}) copy-start(bf16[128,4096]{1,0:T(8,128)(2,1)} %conv_in_ref.1) | copy-start | bytes 3145732
  9.7 4.3 %copy-start.3 = (bf16[1024,64]{0,1:T(8,128)(2,1)S(1)}, bf16[1024,64]{0,1:T(8,128)(2,1)}, u32[]{:S(2)}) copy-start(bf16[1024,64]{0,1:T(8,128)(2,1)} %param.8) | copy-start | bytes 393220
  21.3 1.7 %collective-permute-start.4 = (bf16[2,64,1024]{2,1,0:T(8,128)(2,1)S(1)}, bf16[2,64,1024]{2,1,0:T(8,128)(2,1)}, u32[]{:S(2)}, u32[]{:S(2)}) collective-permute-start(bf16[2,64,1024]{2,1,0:T(8,128)(2,1)S(1)} %get-tuple-element.35), channel_id=1, source_target_pairs={{0,8},{8,0},{16,24},{24,16},{1,9},{9,1},{17,25},{25,17},{2,10},{10... | collective-permute-start | bytes 786440 | tf_op jit(solution)/shard_map/ppermute | solution.py:362
  24.1 4.5 %collective-permute-start.5 = (bf16[32,1024]{1,0:T(8,128)(2,1)S(1)}, bf16[32,1024]{1,0:T(8,128)(2,1)S(1)}, u32[]{:S(2)}, u32[]{:S(2)}) collective-permute-start(bf16[32,1024]{1,0:T(8,128)(2,1)S(1)} %get-tuple-element.43), channel_id=1, source_target_pairs={{0,16},{8,24},{16,0},{24,8},{1,17},{9,25},{17,1},{25,9},{2,18},{10... | collective-permute-start | bytes 196616 | tf_op jit(solution)/shard_map/ppermute | solution.py:362
  25.8 8.1 %collective-permute-start.6 = (bf16[32,1024]{1,0:T(8,128)(2,1)S(1)}, bf16[32,1024]{1,0:T(8,128)(2,1)S(1)}, u32[]{:S(2)}, u32[]{:S(2)}) collective-permute-start(bf16[32,1024]{1,0:T(8,128)(2,1)S(1)} %get-tuple-element.42), channel_id=1, source_target_pairs={{0,16},{8,24},{16,0},{24,8},{1,17},{9,25},{17,1},{25,9},{2,18},{10... | collective-permute-start | bytes 196616 | tf_op jit(solution)/shard_map/ppermute | solution.py:362
  28.6 5.4 %collective-permute-start.7 = (bf16[32,1024]{1,0:T(8,128)(2,1)S(1)}, bf16[32,1024]{1,0:T(8,128)(2,1)S(1)}, u32[]{:S(2)}, u32[]{:S(2)}) collective-permute-start(bf16[32,1024]{1,0:T(8,128)(2,1)S(1)} %fusion.order_ref), channel_id=1, source_target_pairs={{0,1},{1,0},{2,3},{3,2},{4,5},{5,4},{6,7},{7,6},{8,9},{9,8},{10,11... | collective-permute-start | bytes 196616 | tf_op jit(solution)/shard_map/ppermute | solution.py:362
  34.0 4.3 %collective-permute-start.8 = (bf16[32,1024]{1,0:T(8,128)(2,1)S(1)}, bf16[32,1024]{1,0:T(8,128)(2,1)S(1)}, u32[]{:S(2)}, u32[]{:S(2)}) collective-permute-start(bf16[32,1024]{1,0:T(8,128)(2,1)S(1)} %add_convert_fusion.2), channel_id=1, source_target_pairs={{0,2},{1,3},{2,0},{3,1},{4,6},{5,7},{6,4},{7,5},{8,10},{9,11},{10,... | collective-permute-start | bytes 196616 | tf_op jit(solution)/shard_map/ppermute | solution.py:362
  38.4 5.2 %collective-permute-start.9 = (bf16[32,1024]{1,0:T(8,128)(2,1)S(1)}, bf16[32,1024]{1,0:T(8,128)(2,1)S(1)}, u32[]{:S(2)}, u32[]{:S(2)}) collective-permute-start(bf16[32,1024]{1,0:T(8,128)(2,1)S(1)} %add_convert_fusion.1), channel_id=1, source_target_pairs={{0,4},{1,5},{2,6},{3,7},{4,0},{5,1},{6,2},{7,3},{8,12},{9,13},{10,... | collective-permute-start | bytes 196616 | tf_op jit(solution)/shard_map/ppermute | solution.py:362
  43.7 5.5 %collective-permute-start.10 = (bf16[32,1024]{1,0:T(8,128)(2,1)S(1)}, bf16[32,1024]{1,0:T(8,128)(2,1)S(1)}, u32[]{:S(2)}, u32[]{:S(2)}) collective-permute-start(bf16[32,1024]{1,0:T(8,128)(2,1)S(1)} %add_convert_fusion), channel_id=1, source_target_pairs={{0,1},{1,0},{2,3},{3,2},{4,5},{5,4},{6,7},{7,6},{8,9},{9,8},{10,11... | collective-permute-start | bytes 196616 | tf_op jit(solution)/shard_map/ppermute | solution.py:362

commit v5 on v4

--- a/solution.py
+++ b/solution.py
@@ -215,6 +215,15 @@
     for pair in range(owners // 2):
         keep_ref[pair] = sum_ref[jnp.bitwise_xor(place_ref[0], 2 * pair)]
         send_ref[pair] = sum_ref[jnp.bitwise_xor(place_ref[0], 2 * pair + 1)].astype(send_ref.dtype)
+
+
+def split_kernel(home_ref, keep_ref, arrived_ref, away_ref, stay_ref, kept_away_ref, kept_stay_ref):
+    part = away_ref.shape[0]
+    home = pl.multiple_of(home_ref[0], part)
+    for offset, send_ref, kept_ref in ((part - home, away_ref, kept_away_ref), (home, stay_ref, kept_stay_ref)):
+        rows = pl.ds(pl.multiple_of(offset, part), part)
+        kept_ref[...] = keep_ref[0, rows, :] + arrived_ref[0, rows, :].astype(jnp.float32)
+        send_ref[...] = (keep_ref[1, rows, :] + arrived_ref[1, rows, :].astype(jnp.float32)).astype(send_ref.dtype)
 
 
 def halo_input_kernel(rows_ref, taps_ref, input_ref, after_ref, halo_ref, head_ref, tail_ref, filt_ref,
@@ -339,6 +348,20 @@
     )(place, *bases, own, x_hat, halo, after)
 
 
+def split(home, keep, arrived):
+    _, taps, width = keep.shape
+    halves = [shaped(taps // 2, width)] * 2 + [shaped(taps // 2, width, dtype=jnp.float32)] * 2
+    return pl.pallas_call(
+        split_kernel,
+        in_specs=[scalars(), *inside(2)],
+        out_specs=inside(4),
+        out_shape=halves,
+        compiler_params=params(),
+        cost_estimate=cost(4 * taps * width, 16 * taps * width),
+        name="split",
+    )(home, keep, arrived)
+
+
 def halo_input(bases, after, halo, head, tail, filt, order, owners):
     taps, channels = halo.shape
     width = channels // owners
@@ -390,19 +413,18 @@
     keep, send = halo_filter(place, (halo_rows, halo_inverse_filter), own, x_hat, halo, tail, dp)
 
     bit = 1
-    while bit < dp // 2:
+    while bit < dp // 4:
         total = keep + widen(swap(send, "dp", bit))
         keep, send = total[0::2], narrow(total[1::2])
         bit *= 2
-    half = taps // 2
     low = lax.rem(block, 2) == 0
-    home = lambda value: jnp.where(low, value[0, :half], value[0, half:])
-    away = lambda value: jnp.where(low, value[0, half:], value[0, :half])
-    arrived_away, arrived_home = swap(away(send), "dp", bit), swap(home(send), "dp", bit)
-    passing = narrow(away(keep) + widen(arrived_away))
+    home = jnp.where(low, 0, taps // 2).reshape(1)
+    away, stay, kept_away, kept = split(home, keep, swap(send, "dp", bit))
+    arrived_away, arrived_home = swap(away, "dp", 2 * bit), swap(stay, "dp", 2 * bit)
+    passing = narrow(kept_away + widen(arrived_away))
     arrived = swap(passing, "ctx", 1)
     grad_in, kept = halo_input(
-        (halo_rows, halo_taps, halo_inverse_input), home(keep), halo, head, tail, whole_filter, passing, dp
+        (halo_rows, halo_taps, halo_inverse_input), kept, halo, head, tail, whole_filter, passing, dp
     )
     total = kept + widen(arrived_home) + widen(arrived)
     bit = 2

time: 50.1 us -> 50.9 us (1.016)
  local copies, waits for them, and re-layouts: 1.15 us -> 5.83 us
  waiting for transfers between devices: 15.1 us -> 12.3 us
  other arithmetic: 4 us -> 2.94 us
  Pallas kernels: 11.4 us -> 12.2 us
  starting transfers between devices: 17.4 us -> 16.7 us
    unnamed x10 -> x22, local copies, waits for them, and re-layouts: 1.15 us -> 5.83 us
    ppermute x1, waiting for transfers between devices: 2.65 us -> 0.01 us  [body(): lax.ppermute(following, 'ctx', [(source, source - 1) for source in range(...]
    another operation x1 -> x0, other arithmetic: 1.03 us -> none
    ppermute x10, starting transfers between devices: 16.1 us -> 15.4 us  [swap(): lax.ppermute(value, axis, [(source, source ^ bit) for source in range(lax...]
    pallas_call x1, Pallas kernels: 1.55 us -> 2.24 us  [halo_filter(): pl.pallas_call(halo_filter_kernel, in_specs=[scalars(), *inside(6)], out_...]
  transfers between devices with their start and end apart: 11 -> 11, of which waited for: 7 -> 5; matrix products, arithmetic and copies ran while one was open for 0% -> 0% of each run, Pallas kernels for 20% -> 19%
where the time goes in v5:
time: 50.9 us; the launch traced here: 50.7 us
  starting transfers between devices  16.7 us (33%)
  waiting for transfers between devices  12.3 us (24%)
  Pallas kernels  12.2 us (24%)
  local copies, waits for them, and re-layouts  5.83 us (11%)
  other arithmetic  2.94 us (6%)
  between operations  0.76 us (1%)
    ppermute x10, starting transfers between devices, swap(): lax.ppermute(value, axis, [(source, source ^ bit) for source in range(lax...  15.4 us
    ppermute x10, waiting for transfers between devices, swap(): lax.ppermute(value, axis, [(source, source ^ bit) for source in range(lax...  12.3 us
    unnamed x22, local copies, waits for them, and re-layouts  5.83 us
    pallas_call x1, Pallas kernels, own_input(): pl.pallas_call(own_input_kernel, in_specs=[scalars(), *inside(4), *outsid...  3.11 us
    pallas_call x1, Pallas kernels, own_filter(): pl.pallas_call(own_filter_kernel, in_specs=inside(6), out_specs=inside(3)...  3.01 us
    pallas_call x1, Pallas kernels, halo_input(): pl.pallas_call(halo_input_kernel, in_specs=[*inside(8), *outside(1)], out...  2.4 us
    pallas_call x1, Pallas kernels, halo_filter(): pl.pallas_call(halo_filter_kernel, in_specs=[scalars(), *inside(6)], out_...  2.24 us
    convert_element_type x5, other arithmetic, narrow(): return value.astype(jnp.bfloat16)  2.2 us
  transfers between devices with their start and end apart: 11, of which 5 were waited for; matrix products, arithmetic and copies ran while one was open for 0% of the time, Pallas kernels for 19%

profile of v5, /device:TPU:0, one launch (start us, length us, event | category | flops | bytes accessed | tf_op | source)
XLA Modules:
  0.0 50.7 jit_solution(17732979414160485395)
XLA Ops:
  0.6 2.1 %multiply_convert_fusion = bf16[64,4096]{1,0:T(8,128)(2,1)} fusion(bf16[128,4096]{1,0:T(8,128)(2,1)} %gate_ref.1, bf16[128,4096]{1,0:T(8,128)(2,1)} %grad_out_ref.1), kind=kLoop, calls=%fused_computation | loop fusion | flops 1048576 | bytes 1572864 | tf_op jit(solution)/shard_map/convert_element_type | solution.py:389
  2.7 1.3 %collective-permute-start = (bf16[64,4096]{1,0:T(8,128)(2,1)}, bf16[64,4096]{1,0:T(8,128)(2,1)S(1)}, u32[]{:S(2)}, u32[]{:S(2)}) collective-permute-start(bf16[64,4096]{1,0:T(8,128)(2,1)} %multiply_convert_fusion), channel_id=1, source_target_pairs={{1,0},{2,1},{3,2},{4,3},{5,4},{6,5},{7,6},{9,8},{10,9},{11,10},{12... | collective-permute-start | bytes 1572872 | tf_op jit(solution)/shard_map/ppermute | solution.py:405
  4.6 2.6 %collective-permute-start.2 = (bf16[64,1024]{1,0:T(8,128)(2,1)}, bf16[64,1024]{1,0:T(8,128)(2,1)S(1)}, u32[]{:S(2)}, u32[]{:S(2)}) collective-permute-start(bf16[64,1024]{1,0:T(8,128)(2,1)} %bitcast.7), channel_id=1, source_target_pairs={{0,16},{8,24},{16,0},{24,8},{1,17},{9,25},{17,1},{25,9},{2,18},{10... | collective-permute-start | bytes 393224 | tf_op jit(solution)/shard_map/ppermute | solution.py:385
  7.2 0.7 %copy-done.10 = s32[128]{0:T(128)S(1)} copy-done((s32[128]{0:T(128)S(1)}, s32[128]{0:T(128)}, u32[]{:S(2)}) %copy-start.10) | copy-done | bytes 536
  7.8 1.3 %basis.1 = (bf16[256,256]{1,0:T(8,128)(2,1)S(1)}, bf16[256,128]{1,0:T(8,128)(2,1)S(1)}, bf16[256,256]{1,0:T(8,128)(2,1)S(1)}, bf16[128,256]{1,0:T(8,128)(2,1)S(1...) custom-call(s32[128]{0:T(128)S(1)} %copy-done.10, ...), custom_call_target="tpu_custom_call" | custom-call | flops 1500000000 | bytes 1000000 | tf_op jit(solution)/shard_map/basis/pallas_call | solution.py:270
  9.7 3.0 %own_filter.1 = (f32[64,4096]{1,0:T(8,128)S(1)}, bf16[128,4096]{1,0:T(8,128)(2,1)S(1)}, f32[128,4096]{1,0:T(8,128)S(1)}) custom-call(bf16[256,256]{1,0:T(8,128)(2,1)S(1)} %get-tuple-element.29.rows_ref, bf16[128,256]{1,0:T(8,128)(2,1)S(1)} %get-tuple-element.30.filter_ref, bf16[128,128]{1,0:T(8,128)(2,1)S(1)} %get-tuple-element.31.last_ref, ...), custom_call_target="tpu_custom_call" | custom-call | flops 1342177280 | bytes 4194304 | tf_op jit(solution)/shard_map/own_filter/pallas_call | solution.py:295
  13.4 0.7 %copy-done.6 = bf16[64,1024]{1,0:T(8,128)(2,1)} copy-done((bf16[64,1024]{1,0:T(8,128)(2,1)}, bf16[64,1024]{1,0:T(8,128)(2,1)S(1)}, u32[]{:S(2)}) %copy-start.6) | copy-done | bytes 131096
  14.1 0.6 %copy-done.8 = bf16[64,1024]{1,0:T(8,128)(2,1)} copy-done((bf16[64,1024]{1,0:T(8,128)(2,1)}, bf16[64,1024]{1,0:T(8,128)(2,1)S(1)}, u32[]{:S(2)}) %copy-start.8) | copy-done | bytes 131096
  14.7 0.9 %copy-done.5 = bf16[64,1024]{1,0:T(8,128)(2,1)S(1)} copy-done((bf16[64,1024]{1,0:T(8,128)(2,1)S(1)}, bf16[64,1024]{1,0:T(8,128)(2,1)}, u32[]{:S(2)}) %copy-start.5) | copy-done | bytes 131096
  15.6 0.9 %copy-done.7 = bf16[64,1024]{1,0:T(8,128)(2,1)S(1)} copy-done((bf16[64,1024]{1,0:T(8,128)(2,1)S(1)}, bf16[64,1024]{1,0:T(8,128)(2,1)}, u32[]{:S(2)}) %copy-start.7) | copy-done | bytes 131096
  16.5 0.9 %copy-done.9 = bf16[64,1024]{1,0:T(8,128)(2,1)S(1)} copy-done((bf16[64,1024]{1,0:T(8,128)(2,1)S(1)}, bf16[64,1024]{1,0:T(8,128)(2,1)}, u32[]{:S(2)}) %copy-start.9) | copy-done | bytes 131096
  17.4 3.1 %own_input.1 = (bf16[64,4096]{1,0:T(8,128)(2,1)S(1)}, f32[64,4096]{1,0:T(8,128)S(1)}, bf16[64,4096]{1,0:T(8,128)(2,1)S(1)}) custom-call(s32[1]{0:T(128)} %bitcast.2.place_ref, bf16[256,256]{1,0:T(8,128)(2,1)S(1)} %get-tuple-element.29.rows_ref, bf16[256,128]{1,0:T(8,128)(2,1)S(1)} %get-tuple-element.34.taps_ref, ...), custom_call_target="tpu_custom_call" | custom-call | flops 2013265920 | bytes 4718592 | tf_op jit(solution)/shard_map/own_input/pallas_call | solution.py:316
  20.6 2.2 %halo_filter.1 = (f32[2,64,1024]{2,1,0:T(8,128)S(1)}, bf16[2,64,1024]{2,1,0:T(8,128)(2,1)}) custom-call(s32[1]{0:T(128)} %bitcast.2.place_ref, bf16[128,128]{1,0:T(8,128)(2,1)S(1)} %get-tuple-element.25.rows_ref, bf16[128,128]{1,0:T(8,128)(2,1)S(1)} %get-tuple-element.28.filter_ref, f32[64,4096]{1,0:T(8,128)S(1)} %get-tuple-element.32.own_ref, ...), custom_call_target="tpu_custom_call" | custom-call | flops 335544320 | bytes 2621440 | tf_op jit(solution)/shard_map/halo_filter/pallas_call | solution.py:336
  23.1 1.5 %collective-permute-done.4.arrived_ref = bf16[2,64,1024]{2,1,0:T(8,128)(2,1)S(1)} collective-permute-done((bf16[2,64,1024]{2,1,0:T(8,128)(2,1)}, bf16[2,64,1024]{2,1,0:T(8,128)(2,1)S(1)}, u32[]{:S(2)}, u32[]{:S(2)}) %collective-permute-start.4) | collective-permute-done | bytes 262176 | tf_op jit(solution)/shard_map/ppermute | solution.py:385
  24.6 1.8 %collective-permute-start.5 = (bf16[32,1024]{1,0:T(8,128)(2,1)S(1)}, bf16[32,1024]{1,0:T(8,128)(2,1)S(1)}, u32[]{:S(2)}, u32[]{:S(2)}) collective-permute-start(bf16[32,1024]{1,0:T(8,128)(2,1)S(1)} %get-tuple-element.44), channel_id=1, source_target_pairs={{0,16},{8,24},{16,0},{24,8},{1,17},{9,25},{17,1},{25,9},{2,18},{10... | collective-permute-start | bytes 196616 | tf_op jit(solution)/shard_map/ppermute | solution.py:385
  26.7 2.3 %collective-permute-done.5 = bf16[32,1024]{1,0:T(8,128)(2,1)S(1)} collective-permute-done((bf16[32,1024]{1,0:T(8,128)(2,1)S(1)}, bf16[32,1024]{1,0:T(8,128)(2,1)S(1)}, u32[]{:S(2)}, u32[]{:S(2)}) %collective-permute-start.5) | collective-permute-done | bytes 65568 | tf_op jit(solution)/shard_map/ppermute | solution.py:385
  29.0 2.7 %collective-permute-start.7 = (bf16[32,1024]{1,0:T(8,128)(2,1)S(1)}, bf16[32,1024]{1,0:T(8,128)(2,1)S(1)}, u32[]{:S(2)}, u32[]{:S(2)}) collective-permute-start(bf16[32,1024]{1,0:T(8,128)(2,1)S(1)} %add_convert_fusion.3.order_ref), channel_id=1, source_target_pairs={{0,1},{1,0},{2,3},{3,2},{4,5},{5,4},{6,7},{7,6},{8,9},{9,8},{10,11... | collective-permute-start | bytes 196616 | tf_op jit(solution)/shard_map/ppermute | solution.py:385
  31.7 2.4 %halo_input.1 = (bf16[128,4096]{1,0:T(8,128)(2,1)}, f32[32,1024]{1,0:T(8,128)S(1)}) custom-call(bf16[128,128]{1,0:T(8,128)(2,1)S(1)} %get-tuple-element.25.rows_ref, bf16[128,128]{1,0:T(8,128)(2,1)S(1)} %get-tuple-element.26.taps_ref, bf16[128,128]{1,0:T(8,128)(2,1)S(1)} %get-tuple-element.27.input_ref, f32[32,1024]{1,0:T(8,128)S(1)} %get-tuple-element.40.after_ref, ...), custom_call_target="tpu_custom_call" | custom-call | flops 469762048 | bytes 2621440 | tf_op jit(solution)/shard_map/halo_input/pallas_call | solution.py:369
  34.2 3.4 %collective-permute-start.8 = (bf16[32,1024]{1,0:T(8,128)(2,1)S(1)}, bf16[32,1024]{1,0:T(8,128)(2,1)S(1)}, u32[]{:S(2)}, u32[]{:S(2)}) collective-permute-start(bf16[32,1024]{1,0:T(8,128)(2,1)S(1)} %add_convert_fusion.2), channel_id=1, source_target_pairs={{0,2},{1,3},{2,0},{3,1},{4,6},{5,7},{6,4},{7,5},{8,10},{9,11},{10,... | collective-permute-start | bytes 196616 | tf_op jit(solution)/shard_map/ppermute | solution.py:385
  37.5 2.2 %collective-permute-done.8 = bf16[32,1024]{1,0:T(8,128)(2,1)S(1)} collective-permute-done((bf16[32,1024]{1,0:T(8,128)(2,1)S(1)}, bf16[32,1024]{1,0:T(8,128)(2,1)S(1)}, u32[]{:S(2)}, u32[]{:S(2)}) %collective-permute-start.8) | collective-permute-done | bytes 65568 | tf_op jit(solution)/shard_map/ppermute | solution.py:385
  39.8 3.5 %collective-permute-start.9 = (bf16[32,1024]{1,0:T(8,128)(2,1)S(1)}, bf16[32,1024]{1,0:T(8,128)(2,1)S(1)}, u32[]{:S(2)}, u32[]{:S(2)}) collective-permute-start(bf16[32,1024]{1,0:T(8,128)(2,1)S(1)} %add_convert_fusion.1), channel_id=1, source_target_pairs={{0,4},{1,5},{2,6},{3,7},{4,0},{5,1},{6,2},{7,3},{8,12},{9,13},{10,... | collective-permute-start | bytes 196616 | tf_op jit(solution)/shard_map/ppermute | solution.py:385
  43.3 2.2 %collective-permute-done.9 = bf16[32,1024]{1,0:T(8,128)(2,1)S(1)} collective-permute-done((bf16[32,1024]{1,0:T(8,128)(2,1)S(1)}, bf16[32,1024]{1,0:T(8,128)(2,1)S(1)}, u32[]{:S(2)}, u32[]{:S(2)}) %collective-permute-start.9) | collective-permute-done | bytes 65568 | tf_op jit(solution)/shard_map/ppermute | solution.py:385
  45.9 4.1 %collective-permute-done.10 = bf16[32,1024]{1,0:T(8,128)(2,1)S(1)} collective-permute-done((bf16[32,1024]{1,0:T(8,128)(2,1)S(1)}, bf16[32,1024]{1,0:T(8,128)(2,1)S(1)}, u32[]{:S(2)}, u32[]{:S(2)}) %collective-permute-start.10) | collective-permute-done | bytes 65568 | tf_op jit(solution)/shard_map/ppermute | solution.py:385
  49.9 0.7 %convert_bitcast_fusion = f32[1024,64]{0,1:T(8,128)} fusion(bf16[32,1024]{1,0:T(8,128)(2,1)S(1)} %get-tuple-element.49, bf16[32,1024]{1,0:T(8,128)(2,1)S(1)} %get-tuple-element.48), kind=kLoop, calls=%fused_computation.1 | loop fusion | flops 262144 | bytes 393216 | tf_op jit(solution)/shard_map/transpose | solution.py:438
  (33 shorter events, 2.8 us)
Async XLA Ops:
  2.7 17.8 %collective-permute-start = (bf16[64,4096]{1,0:T(8,128)(2,1)}, bf16[64,4096]{1,0:T(8,128)(2,1)S(1)}, u32[]{:S(2)}, u32[]{:S(2)}) collective-permute-start(bf16[64,4096]{1,0:T(8,128)(2,1)} %multiply_convert_fusion), channel_id=1, source_target_pairs={{1,0},{2,1},{3,2},{4,3},{5,4},{6,5},{7,6},{9,8},{10,9},{11,10},{12... | collective-permute-start | bytes 1572872 | tf_op jit(solution)/shard_map/ppermute | solution.py:405
  4.0 8.7 %collective-permute-start.1 = (bf16[64,1024]{1,0:T(8,128)(2,1)}, bf16[64,1024]{1,0:T(8,128)(2,1)S(1)}, u32[]{:S(2)}, u32[]{:S(2)}) collective-permute-start(bf16[64,1024]{1,0:T(8,128)(2,1)} %bitcast.6), channel_id=1, source_target_pairs={{0,8},{8,0},{16,24},{24,16},{1,9},{9,1},{17,25},{25,17},{2,10},{10... | collective-permute-start | bytes 393224 | tf_op jit(solution)/shard_map/ppermute | solution.py:385
  4.6 8.8 %collective-permute-start.2 = (bf16[64,1024]{1,0:T(8,128)(2,1)}, bf16[64,1024]{1,0:T(8,128)(2,1)S(1)}, u32[]{:S(2)}, u32[]{:S(2)}) collective-permute-start(bf16[64,1024]{1,0:T(8,128)(2,1)} %bitcast.7), channel_id=1, source_target_pairs={{0,16},{8,24},{16,0},{24,8},{1,17},{9,25},{17,1},{25,9},{2,18},{10... | collective-permute-start | bytes 393224 | tf_op jit(solution)/shard_map/ppermute | solution.py:385
  7.1 6.9 %collective-permute-start.3 = (bf16[64,1024]{1,0:T(8,128)(2,1)}, bf16[64,1024]{1,0:T(8,128)(2,1)S(1)}, u32[]{:S(2)}, u32[]{:S(2)}) collective-permute-start(bf16[64,1024]{1,0:T(8,128)(2,1)} %bitcast.8), channel_id=1, source_target_pairs={{0,24},{8,16},{16,8},{24,0},{1,25},{9,17},{17,9},{25,1},{2,26},{10... | collective-permute-start | bytes 393224 | tf_op jit(solution)/shard_map/ppermute | solution.py:385
  7.2 0.7 %copy-start.10 = (s32[128]{0:T(128)S(1)}, s32[128]{0:T(128)}, u32[]{:S(2)}) copy-start(s32[128]{0:T(128)} %end_ref.1) | copy-start | bytes 1540
  7.8 1.4 %copy-start = (bf16[128,4096]{1,0:T(8,128)(2,1)S(1)}, bf16[128,4096]{1,0:T(8,128)(2,1)}, u32[]{:S(2)}) copy-start(bf16[128,4096]{1,0:T(8,128)(2,1)} %grad_out_ref.1) | copy-start | bytes 3145732
  7.8 1.5 %copy-start.1 = (bf16[128,4096]{1,0:T(8,128)(2,1)S(1)}, bf16[128,4096]{1,0:T(8,128)(2,1)}, u32[]{:S(2)}) copy-start(bf16[128,4096]{1,0:T(8,128)(2,1)} %gate_ref.1) | copy-start | bytes 3145732
  7.8 1.9 %copy-start.2 = (bf16[128,4096]{1,0:T(8,128)(2,1)S(1)}, bf16[128,4096]{1,0:T(8,128)(2,1)}, u32[]{:S(2)}) copy-start(bf16[128,4096]{1,0:T(8,128)(2,1)} %conv_in_ref.1) | copy-start | bytes 3145732
  9.7 5.0 %copy-start.3 = (bf16[1024,64]{0,1:T(8,128)(2,1)S(1)}, bf16[1024,64]{0,1:T(8,128)(2,1)}, u32[]{:S(2)}) copy-start(bf16[1024,64]{0,1:T(8,128)(2,1)} %param.8) | copy-start | bytes 393220
  12.7 0.7 %copy-start.4 = (bf16[64,1024]{1,0:T(8,128)(2,1)}, bf16[64,1024]{1,0:T(8,128)(2,1)S(1)}, u32[]{:S(2)}) copy-start(bf16[64,1024]{1,0:T(8,128)(2,1)S(1)} %collective-permute-done.1.refs_1_) | copy-start | bytes 393220
  13.4 0.7 %copy-start.6 = (bf16[64,1024]{1,0:T(8,128)(2,1)}, bf16[64,1024]{1,0:T(8,128)(2,1)S(1)}, u32[]{:S(2)}) copy-start(bf16[64,1024]{1,0:T(8,128)(2,1)S(1)} %collective-permute-done.2.refs_2_) | copy-start | bytes 393220
  14.1 0.6 %copy-start.8 = (bf16[64,1024]{1,0:T(8,128)(2,1)}, bf16[64,1024]{1,0:T(8,128)(2,1)S(1)}, u32[]{:S(2)}) copy-start(bf16[64,1024]{1,0:T(8,128)(2,1)S(1)} %collective-permute-done.3.refs_3_) | copy-start | bytes 393220
  14.7 0.9 %copy-start.5 = (bf16[64,1024]{1,0:T(8,128)(2,1)S(1)}, bf16[64,1024]{1,0:T(8,128)(2,1)}, u32[]{:S(2)}) copy-start(bf16[64,1024]{1,0:T(8,128)(2,1)} %copy-done.4) | copy-start | bytes 393220
  15.6 0.9 %copy-start.7 = (bf16[64,1024]{1,0:T(8,128)(2,1)S(1)}, bf16[64,1024]{1,0:T(8,128)(2,1)}, u32[]{:S(2)}) copy-start(bf16[64,1024]{1,0:T(8,128)(2,1)} %copy-done.6) | copy-start | bytes 393220
  16.5 0.9 %copy-start.9 = (bf16[64,1024]{1,0:T(8,128)(2,1)S(1)}, bf16[64,1024]{1,0:T(8,128)(2,1)}, u32[]{:S(2)}) copy-start(bf16[64,1024]{1,0:T(8,128)(2,1)} %copy-done.8) | copy-start | bytes 393220
  22.8 1.7 %collective-permute-start.4 = (bf16[2,64,1024]{2,1,0:T(8,128)(2,1)}, bf16[2,64,1024]{2,1,0:T(8,128)(2,1)S(1)}, u32[]{:S(2)}, u32[]{:S(2)}) collective-permute-start(bf16[2,64,1024]{2,1,0:T(8,128)(2,1)} %get-tuple-element.39), channel_id=1, source_target_pairs={{0,8},{8,0},{16,24},{24,16},{1,9},{9,1},{17,25},{25,17},{2,10},{10... | collective-permute-start | bytes 786440 | tf_op jit(solution)/shard_map/ppermute | solution.py:385
  24.6 4.4 %collective-permute-start.5 = (bf16[32,1024]{1,0:T(8,128)(2,1)S(1)}, bf16[32,1024]{1,0:T(8,128)(2,1)S(1)}, u32[]{:S(2)}, u32[]{:S(2)}) collective-permute-start(bf16[32,1024]{1,0:T(8,128)(2,1)S(1)} %get-tuple-element.44), channel_id=1, source_target_pairs={{0,16},{8,24},{16,0},{24,8},{1,17},{9,25},{17,1},{25,9},{2,18},{10... | collective-permute-start | bytes 196616 | tf_op jit(solution)/shard_map/ppermute | solution.py:385
  26.4 7.7 %collective-permute-start.6 = (bf16[32,1024]{1,0:T(8,128)(2,1)S(1)}, bf16[32,1024]{1,0:T(8,128)(2,1)S(1)}, u32[]{:S(2)}, u32[]{:S(2)}) collective-permute-start(bf16[32,1024]{1,0:T(8,128)(2,1)S(1)} %get-tuple-element.47), channel_id=1, source_target_pairs={{0,16},{8,24},{16,0},{24,8},{1,17},{9,25},{17,1},{25,9},{2,18},{10... | collective-permute-start | bytes 196616 | tf_op jit(solution)/shard_map/ppermute | solution.py:385
  29.0 5.1 %collective-permute-start.7 = (bf16[32,1024]{1,0:T(8,128)(2,1)S(1)}, bf16[32,1024]{1,0:T(8,128)(2,1)S(1)}, u32[]{:S(2)}, u32[]{:S(2)}) collective-permute-start(bf16[32,1024]{1,0:T(8,128)(2,1)S(1)} %add_convert_fusion.3.order_ref), channel_id=1, source_target_pairs={{0,1},{1,0},{2,3},{3,2},{4,5},{5,4},{6,7},{7,6},{8,9},{9,8},{10,11... | collective-permute-start | bytes 196616 | tf_op jit(solution)/shard_map/ppermute | solution.py:385
  34.2 5.6 %collective-permute-start.8 = (bf16[32,1024]{1,0:T(8,128)(2,1)S(1)}, bf16[32,1024]{1,0:T(8,128)(2,1)S(1)}, u32[]{:S(2)}, u32[]{:S(2)}) collective-permute-start(bf16[32,1024]{1,0:T(8,128)(2,1)S(1)} %add_convert_fusion.2), channel_id=1, source_target_pairs={{0,2},{1,3},{2,0},{3,1},{4,6},{5,7},{6,4},{7,5},{8,10},{9,11},{10,... | collective-permute-start | bytes 196616 | tf_op jit(solution)/shard_map/ppermute | solution.py:385
  39.8 5.7 %collective-permute-start.9 = (bf16[32,1024]{1,0:T(8,128)(2,1)S(1)}, bf16[32,1024]{1,0:T(8,128)(2,1)S(1)}, u32[]{:S(2)}, u32[]{:S(2)}) collective-permute-start(bf16[32,1024]{1,0:T(8,128)(2,1)S(1)} %add_convert_fusion.1), channel_id=1, source_target_pairs={{0,4},{1,5},{2,6},{3,7},{4,0},{5,1},{6,2},{7,3},{8,12},{9,13},{10,... | collective-permute-start | bytes 196616 | tf_op jit(solution)/shard_map/ppermute | solution.py:385
  45.6 4.3 %collective-permute-start.10 = (bf16[32,1024]{1,0:T(8,128)(2,1)S(1)}, bf16[32,1024]{1,0:T(8,128)(2,1)S(1)}, u32[]{:S(2)}, u32[]{:S(2)}) collective-permute-start(bf16[32,1024]{1,0:T(8,128)(2,1)S(1)} %add_convert_fusion), channel_id=1, source_target_pairs={{0,1},{1,0},{2,3},{3,2},{4,5},{5,4},{6,7},{7,6},{8,9},{9,8},{10,11... | collective-permute-start | bytes 196616 | tf_op jit(solution)/shard_map/ppermute | solution.py:385

commit v6 on v3

--- a/solution.py
+++ b/solution.py
@@ -247,7 +247,7 @@
 
 
 def params():
-    return pltpu.CompilerParams(vmem_limit_bytes=14 * 1024 * 1024)
+    return pltpu.CompilerParams(vmem_limit_bytes=18 * 1024 * 1024)
 
 
 def cost(flops, moved):

time: 48.5 us -> 48.5 us (level)
  no operation moved by 1% of the time
where the time goes in v6:
time: 48.5 us; the launch traced here: 48.4 us
  waiting for transfers between devices  16.3 us (34%)
  starting transfers between devices  15.6 us (32%)
  Pallas kernels  11.4 us (24%)
  other arithmetic  3 us (6%)
  local copies, waits for them, and re-layouts  1.24 us (3%)
  between operations  0.76 us (2%)
    ppermute x9, starting transfers between devices, swap(): lax.ppermute(value, axis, [(source, source ^ bit) for source in range(lax...  14.3 us
    ppermute x9, waiting for transfers between devices, swap(): lax.ppermute(value, axis, [(source, source ^ bit) for source in range(lax...  13.7 us
    pallas_call x1, Pallas kernels, own_input(): pl.pallas_call(own_input_kernel, in_specs=[scalars(), *inside(4), *outsid...  3.12 us
    pallas_call x1, Pallas kernels, own_filter(): pl.pallas_call(own_filter_kernel, in_specs=inside(6), out_specs=inside(3)...  3.02 us
    ppermute x1, waiting for transfers between devices, body(): lax.ppermute(following, 'ctx', [(source, source - 1) for source in range(...  2.64 us
    pallas_call x1, Pallas kernels, halo_input(): pl.pallas_call(halo_input_kernel, in_specs=inside(8), out_specs=[pl.Block...  2.42 us
    convert_element_type x5, other arithmetic, narrow(): return value.astype(jnp.bfloat16)  2.19 us
    pallas_call x1, Pallas kernels, halo_filter(): pl.pallas_call(halo_filter_kernel, in_specs=[scalars(), *inside(6)], out_...  1.55 us
  transfers between devices with their start and end apart: 10, of which 8 were waited for; matrix products, arithmetic and copies ran while one was open for 0% of the time, Pallas kernels for 20%

profile of v6, /device:TPU:0, one launch (start us, length us, event | category | flops | bytes accessed | tf_op | source)
XLA Modules:
  0.0 48.4 jit_solution(5578277842929365726)
XLA Ops:
  0.6 2.1 %multiply_convert_fusion = bf16[64,4096]{1,0:T(8,128)(2,1)} fusion(bf16[128,4096]{1,0:T(8,128)(2,1)} %gate_ref.1, bf16[128,4096]{1,0:T(8,128)(2,1)} %grad_out_ref.1), kind=kLoop, calls=%fused_computation | loop fusion | flops 1048576 | bytes 1572864 | tf_op jit(solution)/shard_map/convert_element_type | solution.py:365
  2.7 1.3 %collective-permute-start = (bf16[64,4096]{1,0:T(8,128)(2,1)}, bf16[64,4096]{1,0:T(8,128)(2,1)S(1)}, u32[]{:S(2)}, u32[]{:S(2)}) collective-permute-start(bf16[64,4096]{1,0:T(8,128)(2,1)} %multiply_convert_fusion), channel_id=1, source_target_pairs={{1,0},{2,1},{3,2},{4,3},{5,4},{6,5},{7,6},{9,8},{10,9},{11,10},{12... | collective-permute-start | bytes 1572872 | tf_op jit(solution)/shard_map/ppermute | solution.py:381
  4.0 0.5 %collective-permute-start.1 = (bf16[64,1024]{1,0:T(8,128)(2,1)}, bf16[64,1024]{1,0:T(8,128)(2,1)S(1)}, u32[]{:S(2)}, u32[]{:S(2)}) collective-permute-start(bf16[64,1024]{1,0:T(8,128)(2,1)} %bitcast.11), channel_id=1, source_target_pairs={{0,8},{8,0},{16,24},{24,16},{1,9},{9,1},{17,25},{25,17},{2,10},{10... | collective-permute-start | bytes 393224 | tf_op jit(solution)/shard_map/ppermute | solution.py:361
  4.6 2.6 %collective-permute-start.2 = (bf16[64,1024]{1,0:T(8,128)(2,1)}, bf16[64,1024]{1,0:T(8,128)(2,1)S(1)}, u32[]{:S(2)}, u32[]{:S(2)}) collective-permute-start(bf16[64,1024]{1,0:T(8,128)(2,1)} %bitcast.12), channel_id=1, source_target_pairs={{0,16},{8,24},{16,0},{24,8},{1,17},{9,25},{17,1},{25,9},{2,18},{10... | collective-permute-start | bytes 393224 | tf_op jit(solution)/shard_map/ppermute | solution.py:361
  7.2 0.7 %copy-done.4 = s32[128]{0:T(128)S(1)} copy-done((s32[128]{0:T(128)S(1)}, s32[128]{0:T(128)}, u32[]{:S(2)}) %copy-start.4) | copy-done | bytes 536
  7.8 1.3 %basis.1 = (bf16[256,256]{1,0:T(8,128)(2,1)S(1)}, bf16[256,128]{1,0:T(8,128)(2,1)S(1)}, bf16[256,256]{1,0:T(8,128)(2,1)S(1)}, bf16[128,256]{1,0:T(8,128)(2,1)S(1...) custom-call(s32[128]{0:T(128)S(1)} %copy-done.4, ...), custom_call_target="tpu_custom_call" | custom-call | flops 1500000000 | bytes 1000000 | tf_op jit(solution)/shard_map/basis/pallas_call | solution.py:260
  9.7 3.0 %own_filter.1 = (f32[64,4096]{1,0:T(8,128)S(1)}, bf16[128,4096]{1,0:T(8,128)(2,1)S(1)}, f32[128,4096]{1,0:T(8,128)S(1)}) custom-call(bf16[256,256]{1,0:T(8,128)(2,1)S(1)} %get-tuple-element.25.rows_ref, bf16[128,256]{1,0:T(8,128)(2,1)S(1)} %get-tuple-element.26.filter_ref, bf16[128,128]{1,0:T(8,128)(2,1)S(1)} %get-tuple-element.27.last_ref, ...), custom_call_target="tpu_custom_call" | custom-call | flops 1342177280 | bytes 4194304 | tf_op jit(solution)/shard_map/own_filter/pallas_call | solution.py:285
  12.7 1.2 %collective-permute-done.3.refs_3_ = bf16[64,1024]{1,0:T(8,128)(2,1)S(1)} collective-permute-done((bf16[64,1024]{1,0:T(8,128)(2,1)}, bf16[64,1024]{1,0:T(8,128)(2,1)S(1)}, u32[]{:S(2)}, u32[]{:S(2)}) %collective-permute-start.3) | collective-permute-done | bytes 131104 | tf_op jit(solution)/shard_map/ppermute | solution.py:361
  14.0 3.1 %own_input.1 = (bf16[64,4096]{1,0:T(8,128)(2,1)S(1)}, f32[64,4096]{1,0:T(8,128)S(1)}, bf16[64,4096]{1,0:T(8,128)(2,1)S(1)}) custom-call(s32[1]{0:T(128)} %bitcast.1.place_ref, bf16[256,256]{1,0:T(8,128)(2,1)S(1)} %get-tuple-element.25.rows_ref, bf16[256,128]{1,0:T(8,128)(2,1)S(1)} %get-tuple-element.30.taps_ref, ...), custom_call_target="tpu_custom_call" | custom-call | flops 2013265920 | bytes 4718592 | tf_op jit(solution)/shard_map/own_input/pallas_call | solution.py:306
  17.1 2.6 %collective-permute-done.halo_ref = bf16[64,4096]{1,0:T(8,128)(2,1)S(1)} collective-permute-done((bf16[64,4096]{1,0:T(8,128)(2,1)}, bf16[64,4096]{1,0:T(8,128)(2,1)S(1)}, u32[]{:S(2)}, u32[]{:S(2)}) %collective-permute-start) | collective-permute-done | bytes 524320 | tf_op jit(solution)/shard_map/ppermute | solution.py:381
  19.7 1.5 %halo_filter.1 = (f32[2,64,1024]{2,1,0:T(8,128)S(1)}, bf16[2,64,1024]{2,1,0:T(8,128)(2,1)S(1)}) custom-call(s32[1]{0:T(128)} %bitcast.1.place_ref, bf16[128,128]{1,0:T(8,128)(2,1)S(1)} %get-tuple-element.21.rows_ref, bf16[128,128]{1,0:T(8,128)(2,1)S(1)} %get-tuple-element.24.filter_ref, f32[64,4096]{1,0:T(8,128)S(1)} %get-tuple-element.28.own_ref, ...), custom_call_target="tpu_custom_call" | custom-call | flops 335544320 | bytes 2621440 | tf_op jit(solution)/shard_map/halo_filter/pallas_call | solution.py:326
  21.4 1.5 %collective-permute-done.4 = bf16[2,64,1024]{2,1,0:T(8,128)(2,1)S(1)} collective-permute-done((bf16[2,64,1024]{2,1,0:T(8,128)(2,1)S(1)}, bf16[2,64,1024]{2,1,0:T(8,128)(2,1)S(1)}, u32[]{:S(2)}, u32[]{:S(2)}) %collective-permute-start.4) | collective-permute-done | bytes 262176 | tf_op jit(solution)/shard_map/ppermute | solution.py:361
  23.0 1.8 %collective-permute-start.5 = (bf16[1,64,1024]{2,1,0:T(8,128)(2,1)S(1)}, bf16[1,64,1024]{2,1,0:T(8,128)(2,1)S(1)}, u32[]{:S(2)}, u32[]{:S(2)}) collective-permute-start(bf16[1,64,1024]{2,1,0:T(8,128)(2,1)S(1)} %slice.46), channel_id=1, source_target_pairs={{0,16},{8,24},{16,0},{24,8},{1,17},{9,25},{17,1},{25,9},{2,18},{10... | collective-permute-start | bytes 393224 | tf_op jit(solution)/shard_map/ppermute | solution.py:361
  24.8 2.4 %halo_input.1 = (bf16[128,4096]{1,0:T(8,128)(2,1)}, f32[1,64,1024]{2,1,0:T(8,128)S(1)}) custom-call(bf16[128,128]{1,0:T(8,128)(2,1)S(1)} %get-tuple-element.21.rows_ref, bf16[128,128]{1,0:T(8,128)(2,1)S(1)} %get-tuple-element.22.taps_ref, bf16[128,128]{1,0:T(8,128)(2,1)S(1)} %get-tuple-element.23.input_ref, f32[1,64,1024]{2,1,0:T(8,128)S(1)} %slice.31.after_ref, ...), custom_call_target="tpu_custom_call" | custom-call | flops 469762048 | bytes 2621440 | tf_op jit(solution)/shard_map/halo_input/pallas_call | solution.py:345
  27.2 1.4 %collective-permute-done.5 = bf16[1,64,1024]{2,1,0:T(8,128)(2,1)S(1)} collective-permute-done((bf16[1,64,1024]{2,1,0:T(8,128)(2,1)S(1)}, bf16[1,64,1024]{2,1,0:T(8,128)(2,1)S(1)}, u32[]{:S(2)}, u32[]{:S(2)}) %collective-permute-start.5) | collective-permute-done | bytes 131104 | tf_op jit(solution)/shard_map/ppermute | solution.py:361
  28.6 2.7 %collective-permute-start.6 = (bf16[32,1024]{1,0:T(8,128)(2,1)S(1)}, bf16[32,1024]{1,0:T(8,128)(2,1)S(1)}, u32[]{:S(2)}, u32[]{:S(2)}) collective-permute-start(bf16[32,1024]{1,0:T(8,128)(2,1)S(1)} %fusion.1), channel_id=1, source_target_pairs={{0,1},{1,0},{2,3},{3,2},{4,5},{5,4},{6,7},{7,6},{8,9},{9,8},{10,11... | collective-permute-start | bytes 196616 | tf_op jit(solution)/shard_map/ppermute | solution.py:361
  31.3 2.2 %collective-permute-done.6 = bf16[32,1024]{1,0:T(8,128)(2,1)S(1)} collective-permute-done((bf16[32,1024]{1,0:T(8,128)(2,1)S(1)}, bf16[32,1024]{1,0:T(8,128)(2,1)S(1)}, u32[]{:S(2)}, u32[]{:S(2)}) %collective-permute-start.6) | collective-permute-done | bytes 65568 | tf_op jit(solution)/shard_map/ppermute | solution.py:361
  33.6 1.6 %collective-permute-start.7 = (bf16[32,1024]{1,0:T(8,128)(2,1)S(1)}, bf16[32,1024]{1,0:T(8,128)(2,1)S(1)}, u32[]{:S(2)}, u32[]{:S(2)}) collective-permute-start(bf16[32,1024]{1,0:T(8,128)(2,1)S(1)} %fusion), channel_id=1, source_target_pairs={{0,2},{1,3},{2,0},{3,1},{4,6},{5,7},{6,4},{7,5},{8,10},{9,11},{10,... | collective-permute-start | bytes 196616 | tf_op jit(solution)/shard_map/ppermute | solution.py:361
  35.2 2.7 %collective-permute-done.7 = bf16[32,1024]{1,0:T(8,128)(2,1)S(1)} collective-permute-done((bf16[32,1024]{1,0:T(8,128)(2,1)S(1)}, bf16[32,1024]{1,0:T(8,128)(2,1)S(1)}, u32[]{:S(2)}, u32[]{:S(2)}) %collective-permute-start.7) | collective-permute-done | bytes 65568 | tf_op jit(solution)/shard_map/ppermute | solution.py:361
  37.9 2.9 %collective-permute-start.8 = (bf16[32,1024]{1,0:T(8,128)(2,1)S(1)}, bf16[32,1024]{1,0:T(8,128)(2,1)S(1)}, u32[]{:S(2)}, u32[]{:S(2)}) collective-permute-start(bf16[32,1024]{1,0:T(8,128)(2,1)S(1)} %add_convert_fusion.1), channel_id=1, source_target_pairs={{0,4},{1,5},{2,6},{3,7},{4,0},{5,1},{6,2},{7,3},{8,12},{9,13},{10,... | collective-permute-start | bytes 196616 | tf_op jit(solution)/shard_map/ppermute | solution.py:361
  40.8 2.4 %collective-permute-done.8 = bf16[32,1024]{1,0:T(8,128)(2,1)S(1)} collective-permute-done((bf16[32,1024]{1,0:T(8,128)(2,1)S(1)}, bf16[32,1024]{1,0:T(8,128)(2,1)S(1)}, u32[]{:S(2)}, u32[]{:S(2)}) %collective-permute-start.8) | collective-permute-done | bytes 65568 | tf_op jit(solution)/shard_map/ppermute | solution.py:361
  43.2 2.2 %collective-permute-start.9 = (bf16[32,1024]{1,0:T(8,128)(2,1)S(1)}, bf16[32,1024]{1,0:T(8,128)(2,1)S(1)}, u32[]{:S(2)}, u32[]{:S(2)}) collective-permute-start(bf16[32,1024]{1,0:T(8,128)(2,1)S(1)} %add_convert_fusion), channel_id=1, source_target_pairs={{0,1},{1,0},{2,3},{3,2},{4,5},{5,4},{6,7},{7,6},{8,9},{9,8},{10,11... | collective-permute-start | bytes 196616 | tf_op jit(solution)/shard_map/ppermute | solution.py:361
  45.4 2.2 %collective-permute-done.9 = bf16[32,1024]{1,0:T(8,128)(2,1)S(1)} collective-permute-done((bf16[32,1024]{1,0:T(8,128)(2,1)S(1)}, bf16[32,1024]{1,0:T(8,128)(2,1)S(1)}, u32[]{:S(2)}, u32[]{:S(2)}) %collective-permute-start.9) | collective-permute-done | bytes 65568 | tf_op jit(solution)/shard_map/ppermute | solution.py:361
  47.6 0.7 %convert_bitcast_fusion = f32[1024,64]{0,1:T(8,128)} fusion(bf16[32,1024]{1,0:T(8,128)(2,1)S(1)} %get-tuple-element.41, bf16[32,1024]{1,0:T(8,128)(2,1)S(1)} %get-tuple-element.40), kind=kLoop, calls=%fused_computation.3 | loop fusion | flops 262144 | bytes 393216 | tf_op jit(solution)/shard_map/transpose | solution.py:412
  (22 shorter events, 0.9 us)
Async XLA Ops:
  2.7 17.0 %collective-permute-start = (bf16[64,4096]{1,0:T(8,128)(2,1)}, bf16[64,4096]{1,0:T(8,128)(2,1)S(1)}, u32[]{:S(2)}, u32[]{:S(2)}) collective-permute-start(bf16[64,4096]{1,0:T(8,128)(2,1)} %multiply_convert_fusion), channel_id=1, source_target_pairs={{1,0},{2,1},{3,2},{4,3},{5,4},{6,5},{7,6},{9,8},{10,9},{11,10},{12... | collective-permute-start | bytes 1572872 | tf_op jit(solution)/shard_map/ppermute | solution.py:381
  4.0 8.7 %collective-permute-start.1 = (bf16[64,1024]{1,0:T(8,128)(2,1)}, bf16[64,1024]{1,0:T(8,128)(2,1)S(1)}, u32[]{:S(2)}, u32[]{:S(2)}) collective-permute-start(bf16[64,1024]{1,0:T(8,128)(2,1)} %bitcast.11), channel_id=1, source_target_pairs={{0,8},{8,0},{16,24},{24,16},{1,9},{9,1},{17,25},{25,17},{2,10},{10... | collective-permute-start | bytes 393224 | tf_op jit(solution)/shard_map/ppermute | solution.py:361
  4.6 8.2 %collective-permute-start.2 = (bf16[64,1024]{1,0:T(8,128)(2,1)}, bf16[64,1024]{1,0:T(8,128)(2,1)S(1)}, u32[]{:S(2)}, u32[]{:S(2)}) collective-permute-start(bf16[64,1024]{1,0:T(8,128)(2,1)} %bitcast.12), channel_id=1, source_target_pairs={{0,16},{8,24},{16,0},{24,8},{1,17},{9,25},{17,1},{25,9},{2,18},{10... | collective-permute-start | bytes 393224 | tf_op jit(solution)/shard_map/ppermute | solution.py:361
  7.1 6.8 %collective-permute-start.3 = (bf16[64,1024]{1,0:T(8,128)(2,1)}, bf16[64,1024]{1,0:T(8,128)(2,1)S(1)}, u32[]{:S(2)}, u32[]{:S(2)}) collective-permute-start(bf16[64,1024]{1,0:T(8,128)(2,1)} %bitcast.13), channel_id=1, source_target_pairs={{0,24},{8,16},{16,8},{24,0},{1,25},{9,17},{17,9},{25,1},{2,26},{10... | collective-permute-start | bytes 393224 | tf_op jit(solution)/shard_map/ppermute | solution.py:361
  7.2 0.7 %copy-start.4 = (s32[128]{0:T(128)S(1)}, s32[128]{0:T(128)}, u32[]{:S(2)}) copy-start(s32[128]{0:T(128)} %end_ref.1) | copy-start | bytes 1540
  7.8 1.3 %copy-start = (bf16[128,4096]{1,0:T(8,128)(2,1)S(1)}, bf16[128,4096]{1,0:T(8,128)(2,1)}, u32[]{:S(2)}) copy-start(bf16[128,4096]{1,0:T(8,128)(2,1)} %grad_out_ref.1) | copy-start | bytes 3145732
  7.8 1.5 %copy-start.1 = (bf16[128,4096]{1,0:T(8,128)(2,1)S(1)}, bf16[128,4096]{1,0:T(8,128)(2,1)}, u32[]{:S(2)}) copy-start(bf16[128,4096]{1,0:T(8,128)(2,1)} %gate_ref.1) | copy-start | bytes 3145732
  7.8 1.9 %copy-start.2 = (bf16[128,4096]{1,0:T(8,128)(2,1)S(1)}, bf16[128,4096]{1,0:T(8,128)(2,1)}, u32[]{:S(2)}) copy-start(bf16[128,4096]{1,0:T(8,128)(2,1)} %conv_in_ref.1) | copy-start | bytes 3145732
  9.7 4.3 %copy-start.3 = (bf16[1024,64]{0,1:T(8,128)(2,1)S(1)}, bf16[1024,64]{0,1:T(8,128)(2,1)}, u32[]{:S(2)}) copy-start(bf16[1024,64]{0,1:T(8,128)(2,1)} %param.8) | copy-start | bytes 393220
  21.3 1.6 %collective-permute-start.4 = (bf16[2,64,1024]{2,1,0:T(8,128)(2,1)S(1)}, bf16[2,64,1024]{2,1,0:T(8,128)(2,1)S(1)}, u32[]{:S(2)}, u32[]{:S(2)}) collective-permute-start(bf16[2,64,1024]{2,1,0:T(8,128)(2,1)S(1)} %get-tuple-element.35), channel_id=1, source_target_pairs={{0,8},{8,0},{16,24},{24,16},{1,9},{9,1},{17,25},{25,17},{2,10},{10... | collective-permute-start | bytes 786440 | tf_op jit(solution)/shard_map/ppermute | solution.py:361
  23.0 5.6 %collective-permute-start.5 = (bf16[1,64,1024]{2,1,0:T(8,128)(2,1)S(1)}, bf16[1,64,1024]{2,1,0:T(8,128)(2,1)S(1)}, u32[]{:S(2)}, u32[]{:S(2)}) collective-permute-start(bf16[1,64,1024]{2,1,0:T(8,128)(2,1)S(1)} %slice.46), channel_id=1, source_target_pairs={{0,16},{8,24},{16,0},{24,8},{1,17},{9,25},{17,1},{25,9},{2,18},{10... | collective-permute-start | bytes 393224 | tf_op jit(solution)/shard_map/ppermute | solution.py:361
  28.6 4.9 %collective-permute-start.6 = (bf16[32,1024]{1,0:T(8,128)(2,1)S(1)}, bf16[32,1024]{1,0:T(8,128)(2,1)S(1)}, u32[]{:S(2)}, u32[]{:S(2)}) collective-permute-start(bf16[32,1024]{1,0:T(8,128)(2,1)S(1)} %fusion.1), channel_id=1, source_target_pairs={{0,1},{1,0},{2,3},{3,2},{4,5},{5,4},{6,7},{7,6},{8,9},{9,8},{10,11... | collective-permute-start | bytes 196616 | tf_op jit(solution)/shard_map/ppermute | solution.py:361
  33.6 4.3 %collective-permute-start.7 = (bf16[32,1024]{1,0:T(8,128)(2,1)S(1)}, bf16[32,1024]{1,0:T(8,128)(2,1)S(1)}, u32[]{:S(2)}, u32[]{:S(2)}) collective-permute-start(bf16[32,1024]{1,0:T(8,128)(2,1)S(1)} %fusion), channel_id=1, source_target_pairs={{0,2},{1,3},{2,0},{3,1},{4,6},{5,7},{6,4},{7,5},{8,10},{9,11},{10,... | collective-permute-start | bytes 196616 | tf_op jit(solution)/shard_map/ppermute | solution.py:361
  37.9 5.2 %collective-permute-start.8 = (bf16[32,1024]{1,0:T(8,128)(2,1)S(1)}, bf16[32,1024]{1,0:T(8,128)(2,1)S(1)}, u32[]{:S(2)}, u32[]{:S(2)}) collective-permute-start(bf16[32,1024]{1,0:T(8,128)(2,1)S(1)} %add_convert_fusion.1), channel_id=1, source_target_pairs={{0,4},{1,5},{2,6},{3,7},{4,0},{5,1},{6,2},{7,3},{8,12},{9,13},{10,... | collective-permute-start | bytes 196616 | tf_op jit(solution)/shard_map/ppermute | solution.py:361
  43.2 4.4 %collective-permute-start.9 = (bf16[32,1024]{1,0:T(8,128)(2,1)S(1)}, bf16[32,1024]{1,0:T(8,128)(2,1)S(1)}, u32[]{:S(2)}, u32[]{:S(2)}) collective-permute-start(bf16[32,1024]{1,0:T(8,128)(2,1)S(1)} %add_convert_fusion), channel_id=1, source_target_pairs={{0,1},{1,0},{2,3},{3,2},{4,5},{5,4},{6,7},{7,6},{8,9},{9,8},{10,11... | collective-permute-start | bytes 196616 | tf_op jit(solution)/shard_map/ppermute | solution.py:361
